TPU v7x, 32 devices: a whole 2x2x4 slice. The times are simulated.
32 devices in a mesh: doc: 8 (over z, y), tensor: 4 (over x, core).
Axes of the slice: x: 2, y: 2, z: 4, core: 2. Of those that a mesh axis runs over, the one named last changes fastest.
Arguments:
- tokens: bfloat16 [64, 288, 768], P('doc', None, 'tensor'), may hold values from -6 to 6
- query_states: bfloat16 [8, 768], P(None, 'doc'), may hold values from -6 to 6
- w_qkv: bfloat16 [3, 768, 768], P(None, None, 'tensor'), may hold values from -0.21875 to 0.21875
- b_qv: float32 [2, 768], P(None, 'tensor'), may hold values from -3 to 3
- w_out: bfloat16 [768, 768], P('tensor'), may hold values from -0.625 to 0.625
- b_out: float32 [768], replicated, may hold values from -2 to 2
- ln1_gain: float32 [768], replicated, may hold values from 0.5 to 1.5
- ln1_bias: float32 [768], replicated, may hold values from -2 to 2
- w_up: bfloat16 [768, 3072], P(None, 'tensor'), may hold values from -0.21875 to 0.21875
- b_up: float32 [3072], P('tensor'), may hold values from -3 to 3
- w_down: bfloat16 [3072, 768], P('tensor'), may hold values from -0.15625 to 0.15625
- b_down: float32 [768], replicated, may hold values from -2 to 2
- ln2_gain: float32 [768], replicated, may hold values from 0.5 to 1.5
- ln2_bias: float32 [768], replicated, may hold values from -2 to 2
- w_query: bfloat16 [768, 128], replicated, may hold values from -0.21875 to 0.21875
- doc_table: float32 [32, 128], replicated, may hold values from -1.2 to 1.2
- vocab_table: bfloat16 [15360, 768], P('tensor'), may hold values from -0.5 to 0.5
- doc_ids: int32 [8, 8], replicated, may hold values from 0 to 31, all different within a row
- lengths: int32 [8, 8], replicated, may hold values from 36 to 288, as said below
- positions: int32 [8, 8], replicated, may hold values from 0 to 31
- targets: int32 [8, 8], replicated, may hold values from 0 to 15359
- out_grad: bfloat16 [64, 288, 768], P('doc'), may hold values from -6 to 6
- query_weight: float32 [8], replicated, may hold values from 2 to 8
Outputs:
- output: bfloat16 [64, 288, 768], P('doc')
- query_nll: float32 [8], replicated
- grad_tokens: float32 [64, 288, 768], P('doc', None, 'tensor')
- grad_states: float32 [8, 768], P(None, 'doc')
- grad_w_qkv: float32 [3, 768, 768], P(None, 'doc', 'tensor')
- grad_b_qv: float32 [2, 768], P(None, 'tensor')
- grad_w_out: float32 [768, 768], P('tensor', 'doc')
- grad_b_out: float32 [768], P('doc')
- grad_ln1_gain: float32 [768], P('doc')
- grad_ln1_bias: float32 [768], P('doc')
- grad_w_up: float32 [768, 3072], P('doc', 'tensor')
- grad_b_up: float32 [3072], P('tensor')
- grad_w_down: float32 [3072, 768], P('tensor', 'doc')
- grad_b_down: float32 [768], P('doc')
- grad_ln2_gain: float32 [768], P('doc')
- grad_ln2_bias: float32 [768], P('doc')
- grad_w_query: float32 [768, 128], P('doc')
Inputs may be any that keep to these rules, and one draw needn't show every extreme that they name: `lengths`: slot 0 (null) holds 36 to 64 tokens, the others 288 // 2 to 288; query 0's slot 1 holds 288. `doc_ids`: each query's 8 document ids are different. positions lie inside every slot of the query.
All inputs are finite; a program needn't handle non-finite values.
Results may differ from a plain program's by a relative error of at most 0.023.
The roundings to bfloat16 on the way count: a program that leaves them out, or rounds other values in their place, can miss the bound.
Values may be sent and summed in bfloat16 or wider, within the bound.
A program may use at most 192 MiB of HBM per device.

v0:
```python
from functools import partial

import jax
import jax.numpy as jnp
from jax import lax
from jax.sharding import PartitionSpec as P

precise = lax.Precision.HIGHEST


def joined(array, axis, combine):
    everything = jax.tree.map(lambda part: lax.all_gather(part, axis), array)
    initial = jax.tree.map(lambda part: part[0], everything)

    def step(k, so_far):
        return combine(so_far, jax.tree.map(lambda part: part[k], everything))

    return lax.fori_loop(1, lax.axis_size(axis), step, initial)


def layer_norm(values, gain_vec, shift_vec):
    centred = values - jnp.mean(values, -1, keepdims=True)
    factor = lax.rsqrt(jnp.mean(centred * centred, -1, keepdims=True) + 1e-12)
    normed = centred * factor
    return (normed * gain_vec + shift_vec, normed, factor)


def norm_back(upstream, normed, factor, gain_vec):
    scaled = upstream * gain_vec
    inner = (
        scaled
        - jnp.mean(scaled, -1, keepdims=True)
        - normed * jnp.mean(scaled * normed, -1, keepdims=True)
    )
    return (inner * factor, jnp.sum(upstream * normed, 0), jnp.sum(upstream, 0))


def merge_pair(high_first, mass_first, high_second, mass_second):
    highest = jnp.maximum(high_first, high_second)
    return (
        highest,
        mass_first * jnp.exp(high_first - highest) + mass_second * jnp.exp(high_second - highest),
    )


def vocab_combine(first, second):
    highest, summed = merge_pair(first[0], first[1], second[0], second[1])
    return (highest, summed, first[2] + second[2])


def query_combine(first, second):
    prior_high, prior_mass = merge_pair(first[0], first[1], second[0], second[1])
    joint_high, joint_mass = merge_pair(first[2], first[3], second[2], second[3])
    return (prior_high, prior_mass, joint_high, joint_mass)


def partial_lse(members, values):
    highest = jnp.max(jnp.where(members, values[:, None], -1e30), 0)
    summed = jnp.sum(jnp.where(members, jnp.exp(values[:, None] - highest[None, :]), 0.0), 0)
    return (highest, summed)


def att_scores(query_heads, key_heads, key_mask):
    scores = (
        jnp.einsum("bqhe,bkhe->bhqk", query_heads, key_heads, preferred_element_type=jnp.float32)
        * 0.125
    )
    return jnp.where(key_mask, scores, -1000000000.0)


def shards(
    tokens,
    query_states,
    w_qkv,
    b_qv,
    w_out,
    b_out,
    ln1_gain,
    ln1_bias,
    w_up,
    b_up,
    w_down,
    b_down,
    ln2_gain,
    ln2_bias,
    w_query,
    doc_table,
    vocab_table,
    doc_ids,
    lengths,
    positions,
    targets,
    out_grad,
    query_weight,
):
    sequences, seq_length, part_width = tokens.shape
    model_width = w_qkv.shape[1]
    local_width = w_qkv.shape[2]
    head_count = local_width // 64
    row_count = sequences * seq_length
    queries = lengths.shape[0]
    f32 = jnp.float32
    bf16 = jnp.bfloat16
    gathered = lax.all_gather(tokens, "tensor", axis=2, tiled=True)
    flat_tokens = gathered.reshape(row_count, model_width)
    projected = jnp.einsum("nd,jde->jne", flat_tokens, w_qkv, preferred_element_type=f32)
    projected = projected + jnp.stack([b_qv[0], jnp.zeros_like(b_qv[0]), b_qv[1]])[:, None, :]
    rounded_qkv = projected.astype(bf16)
    qkv_heads = rounded_qkv.reshape(3, sequences, seq_length, head_count, 64)
    row_index = lax.axis_index("doc") * sequences + jnp.arange(sequences, dtype=jnp.int32)
    slot_index = row_index // queries
    query_index = row_index % queries
    row_length = lengths[query_index, slot_index]
    key_mask = (jnp.arange(seq_length, dtype=jnp.int32)[None, :] < row_length[:, None])[
        :, None, None, :
    ]
    scores = att_scores(qkv_heads[0], qkv_heads[1], key_mask)
    score_lse = jax.nn.logsumexp(scores, -1, keepdims=True)
    weights_att = jnp.exp(scores - score_lse)
    context = jnp.einsum(
        "bhqk,bkhe->bqhe", weights_att.astype(bf16), qkv_heads[2], preferred_element_type=f32
    )
    context = context.reshape(row_count, local_width).astype(bf16)
    attended = lax.psum(jnp.dot(context, w_out, preferred_element_type=f32), "tensor")
    hidden_one, normed_one, factor_one = layer_norm(
        flat_tokens.astype(f32) + attended + b_out, ln1_gain, ln1_bias
    )
    hidden_low = hidden_one.astype(bf16)
    up_proj = jnp.dot(hidden_low, w_up, preferred_element_type=f32) + b_up
    active, gelu_back = jax.vjp(partial(jax.nn.gelu, approximate=False), up_proj)
    active_low = active.astype(bf16)
    lowered = lax.psum(jnp.dot(active_low, w_down, preferred_element_type=f32), "tensor")
    result, normed_two, factor_two = layer_norm(hidden_one + lowered + b_down, ln2_gain, ln2_bias)
    output = result.astype(bf16).reshape(sequences, seq_length, model_width)
    row_position = positions[query_index]
    row_target = targets[query_index]
    seq_base = jnp.arange(sequences, dtype=jnp.int32)[:, None]
    picked = result.reshape(sequences, seq_length, model_width)[seq_base, row_position].astype(bf16)
    vocab_logits = jnp.einsum("btd,vd->btv", picked, vocab_table, preferred_element_type=f32)
    vocab_local = vocab_table.shape[0]
    vocab_ids = lax.axis_index("tensor") * vocab_local + jnp.arange(vocab_local, dtype=jnp.int32)
    target_hits = vocab_ids[None, None, :] == row_target[:, :, None]
    local_high = jnp.max(vocab_logits, -1)
    local_mass = jnp.sum(jnp.exp(vocab_logits - local_high[:, :, None]), -1)
    local_chosen = jnp.sum(jnp.where(target_hits, vocab_logits, 0.0), -1)
    vocab_high, vocab_mass, chosen = joined(
        (local_high, local_mass, local_chosen), "tensor", vocab_combine
    )
    vocab_lse = vocab_high + jnp.log(vocab_mass)
    loglik = jnp.sum(chosen - vocab_lse, -1)
    states = lax.all_gather(query_states, "doc", axis=1, tiled=True)
    query_emb = jnp.dot(states, w_query, preferred_element_type=f32)
    members = query_index[:, None] == jnp.arange(queries, dtype=jnp.int32)[None, :]
    member_weights = members.astype(f32)
    own_emb = jnp.dot(member_weights, query_emb, precision=precise)
    embeds = doc_table[doc_ids[query_index, slot_index]]
    retrieval = jnp.sum(own_emb * embeds, -1)
    joint_score = retrieval + loglik
    prior_high, prior_mass = partial_lse(members, retrieval)
    joint_high, joint_mass = partial_lse(members, joint_score)
    prior_high, prior_mass, joint_high, joint_mass = joined(
        (prior_high, prior_mass, joint_high, joint_mass), "doc", query_combine
    )
    prior_lse = prior_high + jnp.log(prior_mass)
    joint_lse = joint_high + jnp.log(joint_mass)
    query_nll = prior_lse - joint_lse
    row_weight = query_weight[query_index]
    posterior = jnp.exp(joint_score - jnp.dot(member_weights, joint_lse, precision=precise))
    prior_prob = jnp.exp(retrieval - jnp.dot(member_weights, prior_lse, precision=precise))
    grad_loglik = -row_weight * posterior
    grad_retrieval = row_weight * (prior_prob - posterior)
    vocab_probs = jnp.exp(vocab_logits - vocab_lse[:, :, None])
    grad_logits = (grad_loglik[:, None, None] * (target_hits.astype(f32) - vocab_probs)).astype(
        bf16
    )
    grad_picked = lax.psum(
        jnp.einsum("btv,vd->btd", grad_logits, vocab_table, preferred_element_type=f32), "tensor"
    )
    grad_result = (
        out_grad.astype(f32)
        .at[seq_base, row_position]
        .add(grad_picked)
        .reshape(row_count, model_width)
    )
    grad_emb = jnp.dot(
        member_weights.T, grad_retrieval[:, None] * embeds, precision=precise
    ).astype(bf16)
    grad_w_query = jnp.dot(states.T, grad_emb, preferred_element_type=f32)
    grad_states = jnp.dot(grad_emb, w_query.T, preferred_element_type=f32)
    grad_sum_two, grad_gain_two, grad_bias_two = norm_back(
        grad_result, normed_two, factor_two, ln2_gain
    )
    grad_b_down = jnp.sum(grad_sum_two, 0)
    grad_lowered = grad_sum_two.astype(bf16)
    grad_w_down = jnp.dot(active_low.T, grad_lowered, preferred_element_type=f32)
    grad_active = jnp.dot(grad_lowered, w_down.T, preferred_element_type=f32)
    grad_up = gelu_back(grad_active)[0].astype(bf16)
    grad_w_up = jnp.dot(hidden_low.T, grad_up, preferred_element_type=f32)
    grad_b_up = jnp.sum(grad_up.astype(f32), 0)
    ffn_term = jnp.dot(grad_up, w_up.T, preferred_element_type=f32)
    grad_hidden = grad_sum_two + lax.psum(ffn_term, "tensor")
    grad_sum_one, grad_gain_one, grad_bias_one = norm_back(
        grad_hidden, normed_one, factor_one, ln1_gain
    )
    grad_b_out = jnp.sum(grad_sum_one, 0)
    grad_attended = grad_sum_one.astype(bf16)
    grad_w_out = jnp.dot(context.T, grad_attended, preferred_element_type=f32)
    grad_context = jnp.dot(grad_attended, w_out.T, preferred_element_type=f32).astype(bf16)
    grad_context = grad_context.reshape(sequences, seq_length, head_count, 64)
    again = jnp.exp(att_scores(qkv_heads[0], qkv_heads[1], key_mask) - score_lse)
    grad_value = jnp.einsum(
        "bhqk,bqhe->bkhe", again.astype(bf16), grad_context, preferred_element_type=f32
    )
    grad_probs = jnp.einsum(
        "bqhe,bkhe->bhqk", grad_context, qkv_heads[2], preferred_element_type=f32
    )
    grad_scores = (again * (grad_probs - jnp.sum(grad_probs * again, -1, keepdims=True))).astype(
        bf16
    )
    grad_query = (
        jnp.einsum("bhqk,bkhe->bqhe", grad_scores, qkv_heads[1], preferred_element_type=f32) * 0.125
    )
    grad_key = (
        jnp.einsum("bhqk,bqhe->bkhe", grad_scores, qkv_heads[0], preferred_element_type=f32) * 0.125
    )
    grad_qkv = (
        jnp.stack([grad_query, grad_key, grad_value])
        .reshape(3, row_count, local_width)
        .astype(bf16)
    )
    grad_b_qv = jnp.stack(
        [jnp.sum(grad_qkv[0].astype(f32), 0), jnp.sum(grad_qkv[2].astype(f32), 0)]
    )
    grad_w_qkv = jnp.einsum("nd,jne->jde", flat_tokens, grad_qkv, preferred_element_type=f32)
    grad_flat = jnp.einsum("jne,jde->nd", grad_qkv, w_qkv, preferred_element_type=f32)
    carried = grad_flat.reshape(sequences, seq_length, model_width)
    own_columns = lax.dynamic_slice_in_dim(
        grad_sum_one.reshape(sequences, seq_length, model_width),
        lax.axis_index("tensor") * part_width,
        part_width,
        2,
    )
    grad_tokens = lax.psum_scatter(carried, "tensor", scatter_dimension=2, tiled=True) + own_columns
    all_summed = (
        lax.psum_scatter(grad_w_qkv, "doc", scatter_dimension=1, tiled=True),
        lax.psum_scatter(grad_w_out, "doc", scatter_dimension=1, tiled=True),
        lax.psum_scatter(grad_w_query, "doc", scatter_dimension=0, tiled=True),
        lax.psum_scatter(grad_states, "doc", scatter_dimension=1, tiled=True),
        lax.psum_scatter(grad_b_out, "doc", scatter_dimension=0, tiled=True),
        lax.psum_scatter(grad_gain_one, "doc", scatter_dimension=0, tiled=True),
        lax.psum_scatter(grad_bias_one, "doc", scatter_dimension=0, tiled=True),
        lax.psum_scatter(grad_w_up, "doc", scatter_dimension=0, tiled=True),
        lax.psum_scatter(grad_w_down, "doc", scatter_dimension=1, tiled=True),
        lax.psum_scatter(grad_b_down, "doc", scatter_dimension=0, tiled=True),
        lax.psum_scatter(grad_gain_two, "doc", scatter_dimension=0, tiled=True),
        lax.psum_scatter(grad_bias_two, "doc", scatter_dimension=0, tiled=True),
    )
    (
        grad_w_qkv,
        grad_w_out,
        grad_w_query,
        grad_states,
        grad_b_out,
        grad_gain_one,
        grad_bias_one,
        grad_w_up,
        grad_w_down,
        grad_b_down,
        grad_gain_two,
        grad_bias_two,
    ) = all_summed
    grad_b_qv, grad_b_up = lax.psum((grad_b_qv, grad_b_up), "doc")
    return (
        output,
        query_nll,
        grad_tokens,
        grad_states,
        grad_w_qkv,
        grad_b_qv,
        grad_w_out,
        grad_b_out,
        grad_gain_one,
        grad_bias_one,
        grad_w_up,
        grad_b_up,
        grad_w_down,
        grad_b_down,
        grad_gain_two,
        grad_bias_two,
        grad_w_query,
    )


def solution(mesh):
    in_specs = (
        P("doc", None, "tensor"),
        P(None, "doc"),
        P(None, None, "tensor"),
        P(None, "tensor"),
        P("tensor", None),
        P(),
        P(),
        P(),
        P(None, "tensor"),
        P("tensor"),
        P("tensor", None),
        P(),
        P(),
        P(),
        P(),
        P(),
        P("tensor", None),
        P(),
        P(),
        P(),
        P(),
        P("doc", None, None),
        P(),
    )
    out_specs = (
        P("doc", None, None),
        P(),
        P("doc", None, "tensor"),
        P(None, "doc"),
        P(None, "doc", "tensor"),
        P(None, "tensor"),
        P("tensor", "doc"),
        P("doc"),
        P("doc"),
        P("doc"),
        P("doc", "tensor"),
        P("tensor"),
        P("tensor", "doc"),
        P("doc"),
        P("doc"),
        P("doc"),
        P("doc", None),
    )
    return jax.shard_map(shards, mesh=mesh, in_specs=in_specs, out_specs=out_specs, check_vma=False)
```

profile of v0, /device:TPU:0, one launch (start us, length us, event | category | flops | bytes accessed | tf_op | source)
XLA Modules:
  0.0 1162.0 jit_solution(13588218290372380683)
XLA Ops:
  13.1 37.4 %all-gather.10.cloned.1.call-done = bf16[8,288,768]{1,0,2:T(8,128)(2,1)} async-done(((bf16[8,288,192]{1,0,2:T(8,128)(2,1)}), bf16[8,288,768]{1,0,2:T(8,128)(2,1)}) %all-gather.10.cloned.1.call-update) | async-done | bytes 3538960 | tf_op jit(solution)/shard_map/all_gather | solution.py:104
  87.5 132.5 %all-reduce.17.cloned.1.call-done = f32[2304,768]{1,0:T(8,128)} async-done(((f32[2304,768]{1,0:T(8,128)}), f32[2304,768]{1,0:T(8,128)}) %all-reduce.17.cloned.1.call-update) | async-done | bytes 7077904 | tf_op jit(solution)/shard_map/psum | solution.py:124
  227.9 19.2 %multiply_convert_fusion.1 = (bf16[2304,768]{1,0:T(8,128)(2,1)S(1)}, f32[2304,768]{1,0:T(8,128)}, f32[2304,768]{1,0:T(8,128)}) fusion(f32[768]{0:T(1024)S(1)} %copy-done.75, bf16[2304,768]{1,0:T(8,128)(2,1)S(1)} %fusion.20, bf16[768,768]{1,0:T(8,128)(2,1)S(1)} %copy-done), kind=kOutput, calls=%fused_computation.50 | convolution fusion | flops 2834694144 | bytes 22416384 | tf_op jit(solution)/shard_map/dot_general | solution.py:129
  258.1 26.1 %all-gather.7 = bf16[8,96,8]{1,2,0:T(8,128)(2,1)S(1)} all-gather(bf16[1,96,8]{1,2,0:T(8,128)(2,1)S(1)} %bitcast.246), channel_id=1, replica_groups=mesh['doc'=8,'tensor'=4] {'doc'}, dimensions={0}, use_global_device_ids=true | all-gather | bytes 13824 | tf_op jit(solution)/shard_map/all_gather | solution.py:151
  287.8 98.9 %all-reduce.19.cloned.1.call-done = f32[2304,768]{1,0:T(8,128)} async-done(((f32[2304,768]{1,0:T(8,128)}), f32[2304,768]{1,0:T(8,128)}) %all-reduce.19.cloned.1.call-update) | async-done | bytes 7077904 | tf_op jit(solution)/shard_map/psum | solution.py:132
  432.1 22.0 %all-reduce.11 = (f32[64]{0:T(128)S(1)}, f32[64]{0:T(128)S(1)}, f32[64]{0:T(128)S(1)}, f32[64]{0:T(128)}) all-reduce(f32[64]{0:T(128)} %copy-done.69, f32[64]{0:T(128)} %dynamic-update-slice.1, f32[64]{0:T(128)} %dynamic-update-slice.2, f32[64]{0:T(128)} %copy-done.70), channel_id=2, replica_groups=mesh['doc'=8,'tensor'=4] {'doc'}, use_global_device_ids=true, to_apply=%add | all-reduce | flops 256 | bytes 2048
  457.4 8.9 while.41
  478.6 22.1 %all-reduce.21.cloned.1.call-done = f32[8,8,768]{2,1,0:T(8,128)} async-done(((f32[8,8,768]{2,1,0:T(8,128)}), f32[8,8,768]{2,1,0:T(8,128)}) %all-reduce.21.cloned.1.call-update) | async-done | bytes 196624 | tf_op jit(solution)/shard_map/psum | solution.py:176
  500.7 9.9 scatter_fusion
  528.4 11.5 convert_reduce_fusion
  548.9 130.4 %all-reduce.23.cloned.1.call-done = f32[2304,768]{1,0:T(8,128)} async-done(((f32[2304,768]{1,0:T(8,128)}), f32[2304,768]{1,0:T(8,128)}) %all-reduce.23.cloned.1.call-update) | async-done | bytes 7077904 | tf_op jit(solution)/shard_map/psum | solution.py:201
  679.3 10.0 multiply_reduce_fusion.1
  759.0 8.1 dot_general.107
  767.1 8.1 fusion.29
  775.3 9.1 copy.123
  784.3 10.0 reshape.418
  796.3 7.6 fusion.119
  804.3 8.6 fusion.35
  816.0 38.0 %all-reduce.10 = (f32[2,192]{1,0:T(2,128)}, f32[768]{0:T(1024)S(1)}, f32[768]{0:T(1024)S(1)}, f32[768]{0:T(1024)S(1)}, f32[768]{0:T(1024)}, /*index=5*/f32[768]{0:T(1024)S(1)}, f32[768]{0:T(1024)S(1)}, f32[768]{0:T(1024)S(1)}) all-reduce(f32[2,192]{1,0:T(2,128)S(1)} %pad_maximum_fusion.1, ...), channel_id=1, replica_groups=mesh['doc'=8,'tensor'=4] {'doc'}, use_global_device_ids=true, to_apply=%region_34.35 | all-reduce | flops 5760 | bytes 46080 | tf_op jit(solution)/shard_map/psum | solution.py:272
  859.2 20.8 %reduce-scatter.26.cloned.1.call-done = f32[96,576]{1,0:T(8,128)} async-done(((f32[768,576]{1,0:T(8,128)}), f32[96,576]{1,0:T(8,128)}) %reduce-scatter.26.cloned.1.call-update) | async-done | bytes 221200
  881.9 63.3 %reduce-scatter.22.cloned.1.call-done = f32[192,2304]{1,0:T(8,128)} async-done(((f32[768,2304]{1,0:T(8,128)}), f32[192,2304]{1,0:T(8,128)}) %reduce-scatter.22.cloned.1.call-update) | async-done | bytes 1769488
  955.4 54.8 %reduce-scatter.30.cloned.1.call-done = f32[96,128]{1,0:T(8,128)} async-done(((f32[768,128]{1,0:T(8,128)}), f32[96,128]{1,0:T(8,128)}) %reduce-scatter.30.cloned.1.call-update) | async-done | bytes 49168
  1010.2 72.4 %reduce-scatter.18.cloned.1.call-done = f32[96,768]{1,0:T(8,128)} async-done(((f32[768,768]{1,0:T(8,128)}), f32[96,768]{1,0:T(8,128)}) %reduce-scatter.18.cloned.1.call-update) | async-done | bytes 294928 | tf_op jit(solution)/shard_map/reduce_scatter | solution.py:252
  1082.6 72.2 %reduce-scatter.20.cloned.1.call-done = f32[768,96]{0,1:T(8,128)} async-done(((f32[768,768]{0,1:T(8,128)}), f32[768,96]{0,1:T(8,128)}) %reduce-scatter.20.cloned.1.call-update) | async-done | bytes 294928 | tf_op jit(solution)/shard_map/reduce_scatter | solution.py:253
  (334 shorter events, 254.4 us)
Async XLA Ops:
  7.2 220.7 %copy-start = (bf16[768,768]{1,0:T(8,128)(2,1)S(1)}, bf16[768,768]{1,0:T(8,128)(2,1)}, u32[]{:S(2)}) copy-start(bf16[768,768]{1,0:T(8,128)(2,1)} %param.35) | copy-start | bytes 3538948
  7.2 43.2 %all-gather.10.cloned.1.call-start = ((), (), s32[]{:S(2)}) async-start(), calls=%async_computation.7 | async-start | bytes 5898240 | tf_op jit(solution)/shard_map/all_gather | solution.py:104
  10.1 209.9 %all-reduce.17.cloned.1.call-start = ((), (), s32[]{:S(2)}) async-start(), calls=%async_computation.8 | async-start | bytes 14155776 | tf_op jit(solution)/shard_map/psum | solution.py:124
  12.2 66.2 %copy-start.30 = (pred[8,288]{1,0:T(8,128)(4,1)}, pred[8,288]{1,0:T(8,128)(4,1)S(1)}, u32[]{:S(2)}) copy-start(pred[8,288]{1,0:T(8,128)(4,1)S(1)} %iota_compare_fusion) | copy-start | bytes 6916
  83.5 136.5 %copy-start.56 = (f32[768]{0:T(1024)S(1)}, f32[768]{0:T(1024)}, u32[]{:S(2)}) copy-start(f32[768]{0:T(1024)} %param.32) | copy-start | bytes 9220
  87.5 299.1 %all-reduce.19.cloned.1.call-start = ((), (), s32[]{:S(2)}) async-start(), calls=%async_computation.9 | async-start | bytes 14155776 | tf_op jit(solution)/shard_map/psum | solution.py:132
  225.1 161.5 %copy-start.18 = (f32[2304]{0:T(1024)}, f32[2304]{0:T(1024)S(1)}, u32[]{:S(2)}) copy-start(f32[2304]{0:T(1024)S(1)} %broadcast_multiply_fusion.5) | copy-start | bytes 27652
  226.1 160.5 %copy-start.22 = (f32[2304]{0:T(1024)}, f32[2304]{0:T(1024)S(1)}, u32[]{:S(2)}) copy-start(f32[2304]{0:T(1024)S(1)} %add_rsqrt_fusion.1) | copy-start | bytes 27652
  253.8 132.8 %copy-start.57 = (f32[768]{0:T(1024)S(1)}, f32[768]{0:T(1024)}, u32[]{:S(2)}) copy-start(f32[768]{0:T(1024)} %param.38) | copy-start | bytes 9220
  253.9 246.8 %all-reduce.21.cloned.1.call-start = ((), (), s32[]{:S(2)}) async-start(), calls=%async_computation.10 | async-start | bytes 393216 | tf_op jit(solution)/shard_map/psum | solution.py:176
  284.3 109.1 %copy-start.32 = (bf16[768,8]{0,1:T(8,128)(2,1)}, bf16[768,8]{0,1:T(8,128)(2,1)S(1)}, u32[]{:S(2)}) copy-start(bf16[768,8]{0,1:T(8,128)(2,1)S(1)} %reshape.401) | copy-start | bytes 36868
  286.1 107.2 %copy-start.59 = (f32[8,128]{1,0:T(8,128)}, f32[8,128]{1,0:T(8,128)S(1)}, u32[]{:S(2)}) copy-start(f32[8,128]{1,0:T(8,128)S(1)} %gather_fusion.2) | copy-start | bytes 12292
  472.3 207.0 %all-reduce.23.cloned.1.call-start = ((), (), s32[]{:S(2)}) async-start(), calls=%async_computation.11 | async-start | bytes 14155776 | tf_op jit(solution)/shard_map/psum | solution.py:201
  546.7 132.6 %copy-start.19 = (f32[2304]{0:T(1024)S(1)}, f32[2304]{0:T(1024)}, u32[]{:S(2)}) copy-start(f32[2304]{0:T(1024)} %copy-done.18) | copy-start | bytes 27652
  546.7 132.6 %copy-start.23 = (f32[2304]{0:T(1024)S(1)}, f32[2304]{0:T(1024)}, u32[]{:S(2)}) copy-start(f32[2304]{0:T(1024)} %copy-done.22) | copy-start | bytes 27652
  546.7 132.6 %copy-start.41 = (f32[768]{0:T(1024)S(1)}, f32[768]{0:T(1024)}, u32[]{:S(2)}) copy-start(f32[768]{0:T(1024)} %param.33) | copy-start | bytes 9220
  546.8 267.3 %reduce-scatter.24.cloned.1.call-start = ((), (), s32[]{:S(2)}) async-start(), calls=%async_computation.15 | async-start | bytes 442368
  547.8 141.5 %copy-start.54 = (bf16[8,128]{1,0:T(8,128)(2,1)}, bf16[8,128]{1,0:T(8,128)(2,1)S(1)}, u32[]{:S(2)}) copy-start(bf16[8,128]{1,0:T(8,128)(2,1)S(1)} %convolution_convert_fusion.3) | copy-start | bytes 6148
  548.8 308.7 %reduce-scatter.28.cloned.1.call-start = ((), (), s32[]{:S(2)}) async-start(), calls=%async_computation.17 | async-start | bytes 884736
  740.6 139.4 %reduce-scatter.26.cloned.1.call-start = ((), (), s32[]{:S(2)}) async-start(), calls=%async_computation.16 | async-start | bytes 2211840
  758.9 186.2 %reduce-scatter.22.cloned.1.call-start = ((), (), s32[]{:S(2)}) async-start(), calls=%async_computation.14 | async-start | bytes 8847360
  794.4 215.8 %reduce-scatter.30.cloned.1.call-start = ((), (), s32[]{:S(2)}) async-start(), calls=%async_computation.18 | async-start | bytes 442368
  796.2 286.3 %reduce-scatter.18.cloned.1.call-start = ((), (), s32[]{:S(2)}) async-start(), calls=%async_computation.12 | async-start | bytes 2654208 | tf_op jit(solution)/shard_map/reduce_scatter | solution.py:252
  804.0 350.8 %reduce-scatter.20.cloned.1.call-start = ((), (), s32[]{:S(2)}) async-start(), calls=%async_computation.13 | async-start | bytes 2654208 | tf_op jit(solution)/shard_map/reduce_scatter | solution.py:253
  (71 other events, 609.5 us)
Sparse Core Ops, SparseCore 0:
  10.3 40.1 all-gather.9
  87.6 132.3 all-reduce.16
  254.0 132.5 all-reduce.18
  472.4 28.2 all-reduce.20
  546.9 132.3 all-reduce.22
  682.8 61.5 reduce-scatter.23
  748.0 61.5 reduce-scatter.27
  813.7 66.2 reduce-scatter.25
  882.7 62.3 reduce-scatter.21
  948.8 61.3 reduce-scatter.29
  1014.3 68.2 reduce-scatter.17
  1086.5 68.2 reduce-scatter.19
where the time goes:
time: 1170 us; the launch traced here: 1160 us
  waiting for transfers between devices  705 us (60%)
  matrix products  123 us (11%)
  local copies, waits for them, and re-layouts  119 us (10%)
  blocking collectives  102 us (9%)
  other arithmetic  95.8 us (8%)
  between operations  17 us (1%)
    unnamed x17, waiting for transfers between devices  139 us
    psum x1, waiting for transfers between devices, shards(): lax.psum(jnp.dot(context, w_out, preferred_element_type=f32), 'tensor')  132 us
    psum x1, waiting for transfers between devices, shards(): grad_hidden = grad_sum_two + lax.psum(ffn_term, 'tensor')  130 us
    psum x1, waiting for transfers between devices, shards(): lax.psum(jnp.dot(active_low, w_down, preferred_element_type=f32), 'tensor')  98.9 us
    reduce_scatter x1, waiting for transfers between devices, shards(): lax.psum_scatter(grad_w_up, 'doc', scatter_dimension=0, tiled=True)  72.4 us
    reduce_scatter x1, waiting for transfers between devices, shards(): lax.psum_scatter(grad_w_down, 'doc', scatter_dimension=1, tiled=True)  72.2 us
    unnamed x196, local copies, waits for them, and re-layouts  64.5 us
    psum x1, blocking collectives, shards(): grad_b_qv, grad_b_up = lax.psum((grad_b_qv, grad_b_up), 'doc')  38 us
  transfers between devices with their start and end apart: 12, of which 10 were waited for; matrix products, arithmetic and copies ran while one was open for 14% of the time, Pallas kernels for 0%

commit v1 on v0

v1 whole, which is shorter than its diff:
```python
import functools

import jax
import jax.numpy as jnp
from jax import lax
from jax.experimental import pallas as pl
from jax.experimental.pallas import tpu as pltpu
from jax.sharding import PartitionSpec as P

MESH = pl.DeviceIdType.MESH
f32 = jnp.float32
bf16 = jnp.bfloat16
MIB = 1024 * 1024


def flip(index, bit):
    return index + bit * (1 - 2 * lax.rem(lax.div(index, bit), 2))


def dot(a, b):
    return lax.dot_general(a, b, (((1,), (0,)), ((), ())), preferred_element_type=f32)


def dot_nt(a, b):
    return lax.dot_general(a, b, (((1,), (1,)), ((), ())), preferred_element_type=f32)


def dot_tn(a, b):
    return lax.dot_general(a, b, (((0,), (0,)), ((), ())), preferred_element_type=f32)


def rows_of(block):
    return block.reshape(block.shape[0] * block.shape[1], block.shape[2])


def norm_forward(y):
    centred = y - jnp.mean(y, -1, keepdims=True)
    factor = lax.rsqrt(jnp.mean(centred * centred, -1, keepdims=True) + 1e-12)
    return centred * factor, factor


def forward_kernel(
    cfg,
    lengths,
    tokens,
    w_qkv,
    w_out,
    w_up,
    w_down,
    vectors,
    b_out,
    gain_one,
    bias_one,
    b_down,
    gain_two,
    bias_two,
    x_out,
    qkv_out,
    lse_out,
    ctx_out,
    n1_out,
    f1_out,
    hl_out,
    act_out,
    gp_out,
    n2_out,
    f2_out,
    res_out,
    wq_all,
    wo_all,
    wu_all,
    wd_all,
    tok,
    x_s,
    qkv_s,
    lse_s,
    ctx_s,
    att_s,
    n1_s,
    f1_s,
    hl_s,
    act_s,
    gp_s,
    n2_s,
    f2_s,
    res_s,
    wq,
    wo,
    wu,
    wd,
    vec,
    send_sem,
    recv_sem,
    local_sem,
    out_sem,
):
    n_seq, seq, model, queries = cfg
    d = lax.axis_index("doc")
    t = lax.axis_index("tensor")
    t1, t2 = flip(t, 1), flip(t, 2)
    t3 = flip(t1, 2)
    d1, d2 = flip(d, 1), flip(d, 2)
    q = lax.rem(d, 4)
    q1, q2 = flip(q, 1), flip(q, 2)
    q3 = flip(q1, 2)

    barrier = pltpu.get_barrier_semaphore()
    peers = ({"tensor": t1}, {"tensor": t2}, {"tensor": t3}, {"doc": d1}, {"doc": d2})
    for peer in peers:
        pl.semaphore_signal(barrier, inc=1, device_id=peer, device_id_type=MESH)
    pl.semaphore_wait(barrier, len(peers))

    def remote(number, src, dst, peer):
        return pltpu.make_async_remote_copy(
            src_ref=src,
            dst_ref=dst,
            send_sem=send_sem.at[number],
            recv_sem=recv_sem.at[number],
            device_id=peer,
            device_id_type=MESH,
        )

    gathered = (wq, wo, wu, wd)
    inputs = (w_qkv, w_out, w_up, w_down)
    outputs = (wq_all, wo_all, wu_all, wd_all)
    started = []

    def send(number, src, dst, peer):
        copy = remote(number, src, dst, peer)
        copy.start()
        started.append(copy)

    def send_x(a):
        send(9 * a, inputs[a].at[q], gathered[a].at[t, q], {"tensor": t2})

    def send_core(a):
        send(9 * a + 4, inputs[a], gathered[a].at[t], {"tensor": t1})

    def arrived(number, ref):
        remote(number, ref, ref, {"tensor": t1}).wait_recv()

    def piece(a, part):
        return gathered[a].at[t2, part]

    def after_x(a):
        arrived(9 * a, piece(a, q))
        send(9 * a + 1, piece(a, q), piece(a, q), {"doc": d1})
        send(9 * a + 2, piece(a, q), piece(a, q), {"doc": d2})
        send(9 * a + 5, piece(a, q), piece(a, q), {"tensor": t1})

    def after_y(a):
        arrived(9 * a + 1, piece(a, q1))
        send(9 * a + 3, piece(a, q1), piece(a, q1), {"doc": d2})
        send(9 * a + 6, piece(a, q1), piece(a, q1), {"tensor": t1})

    def after_z(a):
        arrived(9 * a + 2, piece(a, q2))
        send(9 * a + 7, piece(a, q2), piece(a, q2), {"tensor": t1})
        arrived(9 * a + 3, piece(a, q3))
        send(9 * a + 8, piece(a, q3), piece(a, q3), {"tensor": t1})

    def after_core(a):
        for k, part in enumerate((q, q1, q2, q3)):
            arrived(9 * a + 5 + k, gathered[a].at[t3, part])

    tok_base, vec_base = 36, 39
    own = pl.multiple_of(t * n_seq, n_seq)

    def local(number, src, dst):
        copy = pltpu.make_async_copy(src, dst, local_sem.at[number])
        copy.start()
        return copy

    send_x(0)
    own_q = local(0, w_qkv, wq.at[t])
    own_tok = local(1, tokens.at[pl.ds(own, n_seq)], tok.at[t])
    for k, peer in enumerate((t1, t2, t3)):
        theirs = pl.multiple_of(peer * n_seq, n_seq)
        send(tok_base + k, tokens.at[pl.ds(theirs, n_seq)], tok.at[t], {"tensor": peer})
        send(vec_base + k, vectors, vec.at[t], {"tensor": peer})
    send_core(0)
    own_vec = local(2, vectors, vec.at[t])
    own_o = local(3, w_out, wo.at[t])
    own_u = local(4, w_up, wu.at[t])
    own_d = local(5, w_down, wd.at[t])
    after_x(0)
    after_y(0)
    own_tok.wait()
    own_vec.wait()
    for k, peer in enumerate((t1, t2, t3)):
        arrived(tok_base + k, tok.at[peer])
        arrived(vec_base + k, vec.at[peer])
    for a in (1, 2):
        send_x(a)
        send_core(a)

    stores = []

    def store(src, dst):
        copy = pltpu.make_async_copy(src, dst, out_sem.at[len(stores)])
        copy.start()
        stores.append(copy)

    @pl.loop(0, n_seq)
    def _(s):
        x_s[s] = jnp.concatenate([tok[j, s] for j in range(4)], axis=1)

    store(x_s, x_out)

    key_index = lax.broadcasted_iota(jnp.int32, (seq, seq), 0)

    def attention(part, first):
        @pl.loop(0, n_seq)
        def _(s):
            row = d * (4 * n_seq) + t * n_seq + s
            length = lengths[lax.rem(row, queries), lax.div(row, queries)]
            bias = vec[part, 1:2, :576]
            z = (dot(x_s[s], rows_of(wq[part])) + bias).astype(bf16)
            qkv_s[part, s] = z
            pieces = []
            for h in range(3):
                qh = z[:, h * 64 : h * 64 + 64] * 0.125
                kh = z[:, 192 + h * 64 : 256 + h * 64]
                vh = z[:, 384 + h * 64 : 448 + h * 64]
                st = jnp.where(key_index < length, dot_nt(kh, qh), -1000000000.0)
                high = jnp.max(st, 0, keepdims=True)
                e = jnp.exp(st - high)
                total = jnp.sum(e, 0, keepdims=True)
                prob = (e * (1.0 / total)).astype(bf16)
                lse_s[part, s, h] = high + jnp.log(total)
                pieces.append(dot_tn(vh, prob))
            ctx_s[part, s] = jnp.concatenate(pieces, axis=0).T.astype(bf16)

    def project(part, first):
        @pl.loop(0, n_seq)
        def _(s):
            for n in range(model // 256):
                cols = slice(n * 256, n * 256 + 256)
                term = dot(ctx_s[part, s], rows_of(wo[part, :, :, cols]))
                if first:
                    att_s[s, :, cols] = term
                else:
                    att_s[s, :, cols] += term

    own_q.wait()
    attention(t, True)
    after_x(1)
    after_y(1)
    after_z(0)
    own_o.wait()
    project(t, True)
    arrived(4, wq.at[t1])
    attention(t1, False)
    arrived(9 + 4, wo.at[t1])
    project(t1, False)
    send_x(3)
    send_core(3)
    after_z(1)
    after_x(2)
    after_y(2)
    attention(t2, False)
    project(t2, False)
    after_core(0)
    after_z(2)
    attention(t3, False)
    after_core(1)
    project(t3, False)
    store(qkv_s, qkv_out)
    store(lse_s, lse_out)
    store(ctx_s, ctx_out)
    store(wq, wq_all)
    store(wo, wo_all)

    chunk = 96
    chunks = seq // chunk

    @pl.loop(0, n_seq * chunks)
    def _(i):
        s, r = lax.div(i, chunks), pl.multiple_of(lax.rem(i, chunks) * chunk, chunk)
        rows = pl.ds(r, chunk)
        y = x_s[s, rows].astype(f32) + att_s[s, rows] + b_out[...]
        n1, f1 = norm_forward(y)
        n1_s[s, rows] = n1
        f1_s[s, rows] = f1
        hl_s[s, rows] = (n1 * gain_one[...] + bias_one[...]).astype(bf16)

    store(n1_s, n1_out)
    store(f1_s, f1_out)
    store(hl_s, hl_out)
    after_x(3)
    after_y(3)
    own_u.wait()
    own_d.wait()

    def ffn_up(part):
        @pl.loop(0, n_seq * (model // 256))
        def _(i):
            s, n = lax.div(i, model // 256), lax.rem(i, model // 256)
            cols = pl.ds(pl.multiple_of(n * 256, 256), 256)
            u = dot(hl_s[s], rows_of(wu[part, :, :, cols])) + vec[part, 0:1, cols]
            cdf = 0.5 * (1.0 + lax.erf(u * 0.7071067811865476))
            pdf = jnp.exp(u * u * -0.5) * 0.3989422804014327
            act_s[part, s, :, cols] = (u * cdf).astype(bf16)
            gp_s[part, s, :, cols] = (cdf + u * pdf).astype(bf16)

    def ffn_down(part, first):
        @pl.loop(0, n_seq * (model // 256))
        def _(i):
            s, n = lax.div(i, model // 256), lax.rem(i, model // 256)
            cols = pl.ds(pl.multiple_of(n * 256, 256), 256)
            term = dot(act_s[part, s], rows_of(wd[part, :, :, cols]))
            if first:
                att_s[s, :, cols] = term
            else:
                att_s[s, :, cols] += term

    ffn_up(t)
    ffn_down(t, True)
    after_z(3)
    arrived(2 * 9 + 4, wu.at[t1])
    ffn_up(t1)
    arrived(3 * 9 + 4, wd.at[t1])
    ffn_down(t1, False)
    ffn_up(t2)
    ffn_down(t2, False)
    after_core(2)
    ffn_up(t3)
    after_core(3)
    store(act_s, act_out)
    store(gp_s, gp_out)
    store(wu, wu_all)
    store(wd, wd_all)
    ffn_down(t3, False)

    @pl.loop(0, n_seq * chunks)
    def _(i):
        s, r = lax.div(i, chunks), pl.multiple_of(lax.rem(i, chunks) * chunk, chunk)
        rows = pl.ds(r, chunk)
        y = n1_s[s, rows] * gain_one[...] + bias_one[...] + att_s[s, rows] + b_down[...]
        n2, f2 = norm_forward(y)
        n2_s[s, rows] = n2
        f2_s[s, rows] = f2
        res_s[s, rows] = (n2 * gain_two[...] + bias_two[...]).astype(bf16)

    store(n2_s, n2_out)
    store(f2_s, f2_out)
    store(res_s, res_out)
    for copy in stores:
        copy.wait()
    for copy in started:
        copy.wait_send()


def forward(n_seq, seq, model, queries, lengths, tokens, w_qkv, w_out, w_up, w_down, vectors, rows):
    def sds(shape, dtype):
        return jax.ShapeDtypeStruct(shape, dtype)

    acts = [
        ((n_seq, seq, model), bf16),
        ((4, n_seq, seq, 576), bf16),
        ((4, n_seq, 3, 1, seq), f32),
        ((4, n_seq, seq, 192), bf16),
        ((n_seq, seq, model), f32),
        ((n_seq, seq, 1), f32),
        ((n_seq, seq, model), bf16),
        ((4, n_seq, seq, model), bf16),
        ((4, n_seq, seq, model), bf16),
        ((n_seq, seq, model), f32),
        ((n_seq, seq, 1), f32),
        ((n_seq, seq, model), bf16),
    ]
    weights = [(4,) + w.shape for w in (w_qkv, w_out, w_up, w_down)]
    any_spec = pl.BlockSpec(memory_space=pl.ANY)
    vmem_spec = pl.BlockSpec(memory_space=pltpu.VMEM)
    scratch = [pltpu.VMEM((4, n_seq, seq, model // 4), bf16)]
    scratch += [pltpu.VMEM(*a) for a in acts[:4]]
    scratch += [pltpu.VMEM((n_seq, seq, model), f32)]
    scratch += [pltpu.VMEM(*a) for a in acts[4:]]
    scratch += [pltpu.VMEM(w, bf16) for w in weights]
    scratch += [pltpu.VMEM((4,) + vectors.shape, f32)]
    scratch += [
        pltpu.SemaphoreType.DMA((42,)),
        pltpu.SemaphoreType.DMA((42,)),
        pltpu.SemaphoreType.DMA((6,)),
        pltpu.SemaphoreType.DMA((16,)),
    ]
    return pl.pallas_call(
        functools.partial(forward_kernel, (n_seq, seq, model, queries)),
        out_shape=[sds(*a) for a in acts] + [sds(w, bf16) for w in weights],
        in_specs=[pl.BlockSpec(memory_space=pltpu.SMEM)] + [any_spec] * 6 + [vmem_spec] * 6,
        out_specs=[any_spec] * 16,
        scratch_shapes=scratch,
        compiler_params=pltpu.CompilerParams(
            collective_id=0, has_side_effects=True, vmem_limit_bytes=60 * MIB
        ),
        name="layer_forward",
    )(lengths, tokens, w_qkv, w_out, w_up, w_down, vectors, *rows)


precise = lax.Precision.HIGHEST


def joined(array, axis, combine):
    everything = jax.tree.map(lambda part: lax.all_gather(part, axis), array)
    initial = jax.tree.map(lambda part: part[0], everything)

    def step(k, so_far):
        return combine(so_far, jax.tree.map(lambda part: part[k], everything))

    return lax.fori_loop(1, lax.axis_size(axis), step, initial)


def norm_back(upstream, normed, factor, gain_vec):
    scaled = upstream * gain_vec
    inner = (
        scaled
        - jnp.mean(scaled, -1, keepdims=True)
        - normed * jnp.mean(scaled * normed, -1, keepdims=True)
    )
    return (inner * factor, jnp.sum(upstream * normed, 0), jnp.sum(upstream, 0))


def merge_pair(high_first, mass_first, high_second, mass_second):
    highest = jnp.maximum(high_first, high_second)
    return (
        highest,
        mass_first * jnp.exp(high_first - highest) + mass_second * jnp.exp(high_second - highest),
    )


def vocab_combine(first, second):
    highest, summed = merge_pair(first[0], first[1], second[0], second[1])
    return (highest, summed, first[2] + second[2])


def query_combine(first, second):
    prior_high, prior_mass = merge_pair(first[0], first[1], second[0], second[1])
    joint_high, joint_mass = merge_pair(first[2], first[3], second[2], second[3])
    return (prior_high, prior_mass, joint_high, joint_mass)


def partial_lse(members, values):
    highest = jnp.max(jnp.where(members, values[:, None], -1e30), 0)
    summed = jnp.sum(jnp.where(members, jnp.exp(values[:, None] - highest[None, :]), 0.0), 0)
    return (highest, summed)


def shards(
    tokens,
    query_states,
    w_qkv,
    b_qv,
    w_out,
    b_out,
    ln1_gain,
    ln1_bias,
    w_up,
    b_up,
    w_down,
    b_down,
    ln2_gain,
    ln2_bias,
    w_query,
    doc_table,
    vocab_table,
    doc_ids,
    lengths,
    positions,
    targets,
    out_grad,
    query_weight,
):
    sequences, seq_length, part_width = tokens.shape
    model_width = w_qkv.shape[1]
    n_seq = sequences // 4
    row_count = n_seq * seq_length
    queries = lengths.shape[0]
    t = lax.axis_index("tensor")
    packed_qkv = jnp.concatenate([w_qkv[0], w_qkv[1], w_qkv[2]], 1).reshape(4, 192, 576)
    hidden = w_up.shape[1]
    vectors = jnp.zeros((8, hidden), f32)
    vectors = vectors.at[0].set(b_up).at[1, :192].set(b_qv[0]).at[1, 384:576].set(b_qv[1])
    rows = [v[None, :] for v in (b_out, ln1_gain, ln1_bias, b_down, ln2_gain, ln2_bias)]
    (x, qkv, lse, ctx, n1, f1, hl, act, gp, n2, f2, res, wq, wo, wu, wd) = forward(
        n_seq,
        seq_length,
        model_width,
        queries,
        lengths,
        tokens,
        packed_qkv,
        w_out.reshape(4, 48, model_width),
        w_up.reshape(4, 192, hidden),
        w_down.reshape(4, 192, model_width),
        vectors,
        rows,
    )
    output = lax.all_gather(res, "tensor", axis=0, tiled=True)
    row_index = lax.axis_index("doc") * sequences + jnp.arange(sequences, dtype=jnp.int32)
    slot_index = row_index // queries
    query_index = row_index % queries
    row_position = positions[query_index]
    row_target = targets[query_index]
    own = lambda a: lax.dynamic_slice_in_dim(a, t * n_seq, n_seq, 0)
    own_position = own(row_position)
    seq_base = jnp.arange(n_seq, dtype=jnp.int32)[:, None]
    picked = lax.all_gather(res[seq_base, own_position], "tensor", axis=0, tiled=True)
    vocab_logits = jnp.einsum("btd,vd->btv", picked, vocab_table, preferred_element_type=f32)
    vocab_local = vocab_table.shape[0]
    vocab_ids = t * vocab_local + jnp.arange(vocab_local, dtype=jnp.int32)
    target_hits = vocab_ids[None, None, :] == row_target[:, :, None]
    local_high = jnp.max(vocab_logits, -1)
    local_mass = jnp.sum(jnp.exp(vocab_logits - local_high[:, :, None]), -1)
    local_chosen = jnp.sum(jnp.where(target_hits, vocab_logits, 0.0), -1)
    vocab_high, vocab_mass, chosen = joined(
        (local_high, local_mass, local_chosen), "tensor", vocab_combine
    )
    vocab_lse = vocab_high + jnp.log(vocab_mass)
    loglik = jnp.sum(chosen - vocab_lse, -1)
    states = lax.all_gather(query_states, "doc", axis=1, tiled=True)
    query_emb = jnp.dot(states, w_query, preferred_element_type=f32)
    members = query_index[:, None] == jnp.arange(queries, dtype=jnp.int32)[None, :]
    member_weights = members.astype(f32)
    own_emb = jnp.dot(member_weights, query_emb, precision=precise)
    embeds = doc_table[doc_ids[query_index, slot_index]]
    retrieval = jnp.sum(own_emb * embeds, -1)
    joint_score = retrieval + loglik
    prior_high, prior_mass = partial_lse(members, retrieval)
    joint_high, joint_mass = partial_lse(members, joint_score)
    prior_high, prior_mass, joint_high, joint_mass = joined(
        (prior_high, prior_mass, joint_high, joint_mass), "doc", query_combine
    )
    prior_lse = prior_high + jnp.log(prior_mass)
    joint_lse = joint_high + jnp.log(joint_mass)
    query_nll = prior_lse - joint_lse
    row_weight = query_weight[query_index]
    posterior = jnp.exp(joint_score - jnp.dot(member_weights, joint_lse, precision=precise))
    prior_prob = jnp.exp(retrieval - jnp.dot(member_weights, prior_lse, precision=precise))
    grad_loglik = -row_weight * posterior
    grad_retrieval = row_weight * (prior_prob - posterior)
    vocab_probs = jnp.exp(vocab_logits - vocab_lse[:, :, None])
    grad_logits = (grad_loglik[:, None, None] * (target_hits.astype(f32) - vocab_probs)).astype(
        bf16
    )
    grad_picked = lax.psum_scatter(
        jnp.einsum("btv,vd->btd", grad_logits, vocab_table, preferred_element_type=f32),
        "tensor",
        scatter_dimension=0,
        tiled=True,
    )
    grad_emb = jnp.dot(
        member_weights.T, grad_retrieval[:, None] * embeds, precision=precise
    ).astype(bf16)
    grad_w_query = jnp.dot(states.T, grad_emb, preferred_element_type=f32)
    grad_states = jnp.dot(grad_emb, w_query.T, preferred_element_type=f32)
    flat = lambda a: a.reshape(row_count, a.shape[-1])
    grad_result = flat(own(out_grad).astype(f32).at[seq_base, own_position].add(grad_picked))
    n1, f1, n2, f2, hl, x = flat(n1), flat(f1), flat(n2), flat(f2), flat(hl), flat(x)
    dy2, dg2, db2 = norm_back(grad_result, n2, f2, ln2_gain)
    d_low = dy2.astype(bf16)
    act, gp = act.reshape(4, row_count, hidden), gp.reshape(4, row_count, hidden)
    wu, wd = wu.reshape(4, model_width, hidden), wd.reshape(4, hidden, model_width)
    wq, wo = wq.reshape(4, model_width, 576), wo.reshape(4, 192, model_width)
    qkv, ctx = qkv.reshape(4, n_seq, seq_length, 576), ctx.reshape(4, row_count, 192)
    g_down = jnp.einsum("tmf,md->tfd", act, d_low, preferred_element_type=f32)
    d_act = jnp.einsum("md,tfd->tmf", d_low, wd, preferred_element_type=f32)
    d_up = (d_act * gp.astype(f32)).astype(bf16)
    g_up = jnp.einsum("md,tmf->tdf", hl, d_up, preferred_element_type=f32)
    g_b_up = jnp.sum(d_up.astype(f32), 1)
    d_hidden = dy2 + jnp.einsum("tmf,tdf->md", d_up, wu, preferred_element_type=f32)
    dy1, dg1, db1 = norm_back(d_hidden, n1, f1, ln1_gain)
    d_att = dy1.astype(bf16)
    g_out = jnp.einsum("tme,md->ted", ctx, d_att, preferred_element_type=f32)
    d_ctx = jnp.einsum("md,ted->tme", d_att, wo, preferred_element_type=f32).astype(bf16)
    d_ctx = d_ctx.reshape(4, n_seq, seq_length, 3, 64)
    heads = qkv.reshape(4, n_seq, seq_length, 3, 3, 64)
    hq, hk, hv = heads[:, :, :, 0], heads[:, :, :, 1], heads[:, :, :, 2]
    row_length = own(lengths[query_index, slot_index])
    key_mask = (jnp.arange(seq_length, dtype=jnp.int32)[None, :] < row_length[:, None])[
        None, :, None, None, :
    ]
    scores = jnp.einsum("tbqhe,tbkhe->tbhqk", hq, hk, preferred_element_type=f32) * 0.125
    scores = jnp.where(key_mask, scores, -1000000000.0)
    prob = jnp.exp(scores - lse.reshape(4, n_seq, 3, seq_length, 1))
    d_v = jnp.einsum("tbhqk,tbqhe->tbkhe", prob.astype(bf16), d_ctx, preferred_element_type=f32)
    d_prob = jnp.einsum("tbqhe,tbkhe->tbhqk", d_ctx, hv, preferred_element_type=f32)
    d_s = (prob * (d_prob - jnp.sum(d_prob * prob, -1, keepdims=True))).astype(bf16)
    d_q = jnp.einsum("tbhqk,tbkhe->tbqhe", d_s, hk, preferred_element_type=f32) * 0.125
    d_k = jnp.einsum("tbhqk,tbqhe->tbkhe", d_s, hq, preferred_element_type=f32) * 0.125
    d_qkv = jnp.stack([d_q, d_k, d_v], 3).reshape(4, row_count, 576).astype(bf16)
    g_b = jnp.sum(d_qkv.astype(f32), 1)
    g_qkv = jnp.einsum("md,tme->tde", x, d_qkv, preferred_element_type=f32)
    d_x = dy1 + jnp.einsum("tme,tde->md", d_qkv, wq, preferred_element_type=f32)
    d_x = d_x.reshape(n_seq, seq_length, 4, part_width).astype(bf16)
    grad_tokens = lax.all_to_all(d_x, "tensor", split_axis=2, concat_axis=0, tiled=True)
    grad_tokens = grad_tokens.reshape(sequences, seq_length, part_width).astype(f32)
    over_t = lambda a: lax.psum_scatter(a, "tensor", scatter_dimension=0, tiled=True)[0]
    docs = lambda a, k: lax.psum_scatter(a, "doc", scatter_dimension=k, tiled=True)
    g_qkv = docs(over_t(g_qkv), 0)
    g_qkv = jnp.stack([g_qkv[:, :192], g_qkv[:, 192:384], g_qkv[:, 384:]])
    g_b = lax.psum(over_t(g_b), "doc")
    small = lambda v: docs(lax.psum(v, "tensor"), 0)
    return (
        output,
        query_nll,
        grad_tokens,
        docs(grad_states, 1),
        g_qkv,
        jnp.stack([g_b[:192], g_b[384:]]),
        docs(over_t(g_out), 1),
        small(jnp.sum(dy1, 0)),
        small(dg1),
        small(db1),
        docs(over_t(g_up), 0),
        lax.psum(over_t(g_b_up), "doc"),
        docs(over_t(g_down), 1),
        small(jnp.sum(dy2, 0)),
        small(dg2),
        small(db2),
        docs(grad_w_query, 0),
    )


def solution(mesh):
    in_specs = (
        P("doc", None, "tensor"),
        P(None, "doc"),
        P(None, None, "tensor"),
        P(None, "tensor"),
        P("tensor", None),
        P(),
        P(),
        P(),
        P(None, "tensor"),
        P("tensor"),
        P("tensor", None),
        P(),
        P(),
        P(),
        P(),
        P(),
        P("tensor", None),
        P(),
        P(),
        P(),
        P(),
        P("doc", None, None),
        P(),
    )
    out_specs = (
        P("doc", None, None),
        P(),
        P("doc", None, "tensor"),
        P(None, "doc"),
        P(None, "doc", "tensor"),
        P(None, "tensor"),
        P("tensor", "doc"),
        P("doc"),
        P("doc"),
        P("doc"),
        P("doc", "tensor"),
        P("tensor"),
        P("tensor", "doc"),
        P("doc"),
        P("doc"),
        P("doc"),
        P("doc", None),
    )
    return jax.shard_map(shards, mesh=mesh, in_specs=in_specs, out_specs=out_specs, check_vma=False)
```

time: 1170 us -> 968 us (0.83)
  waiting for transfers between devices: 705 us -> 556 us
  Pallas kernels: 0 us -> 84.8 us
  other arithmetic: 95.8 us -> 18.3 us
  local copies, waits for them, and re-layouts: 119 us -> 72.5 us
  matrix products: 123 us -> 78.3 us
  blocking collectives: 102 us -> 133 us
    psum x4 -> x0, waiting for transfers between devices: 384 us -> none  [the longest x1 132 us: shards(): lax.psum(jnp.dot(context, w_out, preferred_element_type=f32), 'tensor')]
    unnamed x17 -> x18, waiting for transfers between devices: 139 us -> 361 us
    pallas_call x0 -> x1, Pallas kernels: none -> 84.8 us  [forward(): pl.pallas_call(functools.partial(forward_kernel, (n_seq, seq, model, quer...]
    reduce_scatter x2 -> x5, waiting for transfers between devices: 145 us -> 195 us  [the longest x4 194 us: shards(): lax.psum_scatter(a, 'tensor', scatter_dimension=0, tiled=True)[0]]
    dot_general x17 -> x13, matrix products: 107 us -> 66.8 us  [the longest x1 9.19 us: shards(): jnp.einsum('tbqhe,tbkhe->tbhqk', d_ctx, hv, preferred_element_type=f32)]
    all_gather x1, waiting for transfers between devices: 37.4 us -> 0.01 us  [shards(): output = lax.all_gather(res, 'tensor', axis=0, tiled=True)]
    unnamed x196 -> x87, local copies, waits for them, and re-layouts: 64.5 us -> 28.1 us
    reduce_sum x9 -> x3, other arithmetic: 30.4 us -> 3.24 us  [the longest x1 1.84 us: norm_back(): jnp.mean(scaled, -1, keepdims=True)]
  transfers between devices with their start and end apart: 12 -> 13, of which waited for: 10 -> 10; matrix products, arithmetic and copies ran while one was open for 14% -> 11% of each run, Pallas kernels for 0% -> 0%
where the time goes in v1:
time: 968 us; the launch traced here: 964 us
  waiting for transfers between devices  556 us (57%)
  blocking collectives  133 us (14%)
  Pallas kernels  84.8 us (9%)
  matrix products  78.3 us (8%)
  local copies, waits for them, and re-layouts  72.5 us (7%)
  other arithmetic  18.3 us (2%)
  between operations  16.5 us (2%)
    unnamed x18, waiting for transfers between devices  361 us
    reduce_scatter x4, waiting for transfers between devices, shards(): lax.psum_scatter(a, 'tensor', scatter_dimension=0, tiled=True)[0]  194 us
    pallas_call x1, Pallas kernels, forward(): pl.pallas_call(functools.partial(forward_kernel, (n_seq, seq, model, quer...  84.8 us
    psum x1, blocking collectives, shards(): g_b = lax.psum(over_t(g_b), 'doc')  35.8 us
    unnamed x2, blocking collectives  29.8 us
    unnamed x87, local copies, waits for them, and re-layouts  28.1 us
    all_gather x1, blocking collectives, shards(): states = lax.all_gather(query_states, 'doc', axis=1, tiled=True)  27.9 us
  transfers between devices with their start and end apart: 13, of which 10 were waited for; matrix products, arithmetic and copies ran while one was open for 11% of the time, Pallas kernels for 0%

profile of v1, /device:TPU:0, one launch (start us, length us, event | category | flops | bytes accessed | tf_op | source)
XLA Modules:
  0.0 963.6 jit_solution(8601586398065015356)
XLA Ops:
  21.6 27.9 %all-gather.7 = bf16[8,96,8]{1,2,0:T(8,128)(2,1)S(1)} all-gather(bf16[1,96,8]{1,2,0:T(8,128)(2,1)} %bitcast.309), channel_id=1, replica_groups=mesh['doc'=8,'tensor'=4] {'doc'}, dimensions={0}, use_global_device_ids=true | all-gather | bytes 13824 | tf_op jit(solution)/shard_map/all_gather | solution.py:520
  53.2 84.8 %layer_forward.1 = (bf16[2,288,768]{2,1,0:T(8,128)(2,1)}, bf16[4,2,288,576]{3,2,1,0:T(8,128)(2,1)}, f32[4,2,3,1,288]{4,3,2,1,0:T(1,128)}, bf16[4,2,288,192]{3,2,...) custom-call(s32[8,8]{1,0:T(8,128)} %lengths.1, ...), custom_call_target="tpu_custom_call" | custom-call | tf_op jit(solution)/shard_map/layer_forward/pallas_call | solution.py:387
  139.4 17.5 %all_gather.57 = bf16[8,8,768]{2,1,0:T(8,128)(2,1)S(1)} all-gather(bf16[2,8,768]{2,1,0:T(8,128)(2,1)S(1)} %bitcast.300), channel_id=1, replica_groups=mesh['doc'=8,'tensor'=4] {'tensor'}, dimensions={0}, use_global_device_ids=true | all-gather | bytes 122880 | tf_op jit(solution)/shard_map/all_gather | solution.py:507
  181.3 19.5 %all-reduce.14 = (f32[64]{0:T(128)S(1)}, f32[64]{0:T(128)S(1)}, f32[64]{0:T(128)S(1)}, f32[64]{0:T(128)S(1)}) all-reduce(f32[64]{0:T(128)S(1)} %dynamic-update-slice.7, f32[64]{0:T(128)S(1)} %dynamic-update-slice.8, f32[64]{0:T(128)S(1)} %dynamic-update-slice.9, f32[64]{0:T(128)S(1)} %dynamic-update-slice.10), channel_id=2, replica_groups=mesh['doc'=8,'tensor'=4] {'doc'}, use_global_device_ids=true, to_apply=%add.1 | all-reduce | flops 256 | bytes 2048
  214.8 7.2 fusion.40
  230.0 6.5 convert_reduce_fusion
  248.2 9.2 multiply_reduce_fusion
  273.2 7.1 convert_element_type.97
  280.4 6.8 convolution_bitcast_fusion.2
  288.4 8.8 convolution_bitcast_fusion
  298.6 8.6 convolution_bitcast_fusion.1
  311.9 39.2 %reduce-scatter.26.cloned.1.call-done = f32[1,768,576]{1,2,0:T(8,128)} async-done(((f32[4,768,576]{1,2,0:T(8,128)}), f32[1,768,576]{1,2,0:T(8,128)}) %reduce-scatter.26.cloned.1.call-update) | async-done | bytes 1769488 | tf_op jit(solution)/shard_map/reduce_scatter | solution.py:597
  355.4 76.7 %reduce-scatter.32.cloned.1.call-done = f32[1,768,768]{2,1,0:T(8,128)} async-done(((f32[4,768,768]{2,1,0:T(8,128)}), f32[1,768,768]{2,1,0:T(8,128)}) %reduce-scatter.32.cloned.1.call-update) | async-done | bytes 2359312 | tf_op jit(solution)/shard_map/reduce_scatter | solution.py:597
  435.2 77.8 %reduce-scatter.30.cloned.1.call-done = f32[1,768,768]{1,2,0:T(8,128)} async-done(((f32[4,768,768]{1,2,0:T(8,128)}), f32[1,768,768]{1,2,0:T(8,128)}) %reduce-scatter.30.cloned.1.call-update) | async-done | bytes 2359312 | tf_op jit(solution)/shard_map/reduce_scatter | solution.py:597
  517.5 5.8 fusion.24
  530.8 46.6 %reduce-scatter.34.cloned.1.call-done = f32[96,8]{1,0:T(8,128)} async-done(((f32[768,8]{1,0:T(8,128)}), f32[96,8]{1,0:T(8,128)}) %reduce-scatter.34.cloned.1.call-update) | async-done | bytes 3088
  579.0 10.2 %all-reduce.16 = (f32[4,576]{1,0:T(4,128)S(1)}, f32[4,768]{1,0:T(4,128)S(1)}) all-reduce(f32[4,576]{1,0:T(4,128)S(1)} %reduce_sum.185, f32[4,768]{1,0:T(4,128)S(1)} %get-tuple-element.666), channel_id=13, replica_groups=mesh['doc'=8,'tensor'=4] {'tensor'}, use_global_device_ids=true, to_apply=%region_24.25.clone | all-reduce | flops 5376 | bytes 43008
  590.6 35.8 %all-reduce.13 = (f32[576]{0:T(1024)S(1)}, f32[768]{0:T(1024)S(1)}, f32[768]{0:T(1024)S(1)}, f32[768]{0:T(1024)S(1)}, f32[768]{0:T(1024)}, /*index=5*/f32[768]{0:T(1024)S(1)}, f32[768]{0:T(1024)S(1)}, f32[768]{0:T(1024)S(1)}) all-reduce(f32[576]{0:T(1024)S(1)} %dynamic-slice_reduce_fusion.1, ...), channel_id=1, replica_groups=mesh['doc'=8,'tensor'=4] {'doc'}, use_global_device_ids=true, to_apply=%region_25.26 | all-reduce | flops 5952 | bytes 47616 | tf_op jit(solution)/shard_map/psum | solution.py:601
  626.9 6.5 all-reduce.15
  635.6 39.1 %reduce-scatter.38.cloned.1.call-done = f32[96,192]{1,0:T(8,128)} async-done(((f32[768,192]{1,0:T(8,128)}), f32[96,192]{1,0:T(8,128)}) %reduce-scatter.38.cloned.1.call-update) | async-done | bytes 73744
  676.4 68.0 %reduce-scatter.36.cloned.1.call-done = f32[96,576]{1,0:T(8,128)} async-done(((f32[768,576]{1,0:T(8,128)}), f32[96,576]{1,0:T(8,128)}) %reduce-scatter.36.cloned.1.call-update) | async-done | bytes 221200
  746.7 61.7 %reduce-scatter.44.cloned.1.call-done = f32[96,128]{1,0:T(8,128)} async-done(((f32[768,128]{1,0:T(8,128)}), f32[96,128]{1,0:T(8,128)}) %reduce-scatter.44.cloned.1.call-update) | async-done | bytes 49168
  808.4 72.1 %reduce-scatter.42.cloned.1.call-done = f32[96,768]{1,0:T(8,128)} async-done(((f32[768,768]{1,0:T(8,128)}), f32[96,768]{1,0:T(8,128)}) %reduce-scatter.42.cloned.1.call-update) | async-done | bytes 294928
  880.5 72.0 %reduce-scatter.40.cloned.1.call-done = f32[96,768]{1,0:T(8,128)} async-done(((f32[768,768]{1,0:T(8,128)}), f32[96,768]{1,0:T(8,128)}) %reduce-scatter.40.cloned.1.call-update) | async-done | bytes 294928
  (229 shorter events, 131.8 us)
Async XLA Ops:
  7.2 171.2 %copy-start = (bf16[768,128]{1,0:T(8,128)(2,1)S(1)}, bf16[768,128]{1,0:T(8,128)(2,1)}, u32[]{:S(2)}) copy-start(bf16[768,128]{1,0:T(8,128)(2,1)} %param.47) | copy-start | bytes 589828
  7.2 216.5 %reduce-scatter.24.cloned.1.call-start = ((), (), s32[]{:S(2)}) async-start(), calls=%async_computation.13 | async-start | bytes 245760 | tf_op jit(solution)/shard_map/reduce_scatter | solution.py:545
  156.9 21.0 %copy-start.16 = (f32[32,128]{1,0:T(8,128)S(1)}, f32[32,128]{1,0:T(8,128)}, u32[]{:S(2)}) copy-start(f32[32,128]{1,0:T(8,128)} %param.48) | copy-start | bytes 49156
  156.9 22.2 %copy-start.20 = (u32[32]{0:T(128)S(1)}, u32[32]{0:T(128)}, u32[]{:S(2)}) copy-start(u32[32]{0:T(128)} %constant.281) | copy-start | bytes 388
  206.3 103.2 %reduce-scatter.28.cloned.1.call-start = ((), (), s32[]{:S(2)}) async-start(), calls=%async_computation.15 | async-start | bytes 2949120 | tf_op jit(solution)/shard_map/reduce_scatter | solution.py:597
  214.8 10.9 %copy-start.17 = (f32[768]{0:T(1024)S(1)}, f32[768]{0:T(1024)}, u32[]{:S(2)}) copy-start(f32[768]{0:T(1024)} %param.45) | copy-start | bytes 9220
  227.7 8.8 slice-start.3
  230.0 6.6 copy-start.4
  244.2 106.9 %reduce-scatter.26.cloned.1.call-start = ((), (), s32[]{:S(2)}) async-start(), calls=%async_computation.14 | async-start | bytes 8847360 | tf_op jit(solution)/shard_map/reduce_scatter | solution.py:597
  248.2 9.2 copy-start.7
  248.2 9.2 slice-start
  248.2 9.2 slice-start.1
  248.2 9.2 slice-start.2
  280.3 6.9 copy-start.9
  287.2 144.8 %reduce-scatter.32.cloned.1.call-start = ((), (), s32[]{:S(2)}) async-start(), calls=%async_computation.17 | async-start | bytes 11796480 | tf_op jit(solution)/shard_map/reduce_scatter | solution.py:597
  297.2 215.8 %reduce-scatter.30.cloned.1.call-start = ((), (), s32[]{:S(2)}) async-start(), calls=%async_computation.16 | async-start | bytes 11796480 | tf_op jit(solution)/shard_map/reduce_scatter | solution.py:597
  307.2 270.3 %reduce-scatter.34.cloned.1.call-start = ((), (), s32[]{:S(2)}) async-start(), calls=%async_computation.18 | async-start | bytes 442368
  308.7 326.9 %all-gather.10.cloned.1.call-start = ((), (), s32[]{:S(2)}) async-start(), calls=%async_computation.12 | async-start | bytes 4423680 | tf_op jit(solution)/shard_map/all_gather | solution.py:498
  309.4 365.3 %reduce-scatter.38.cloned.1.call-start = ((), (), s32[]{:S(2)}) async-start(), calls=%async_computation.20 | async-start | bytes 884736
  311.9 432.5 %reduce-scatter.36.cloned.1.call-start = ((), (), s32[]{:S(2)}) async-start(), calls=%async_computation.19 | async-start | bytes 2211840
  354.0 454.4 %reduce-scatter.44.cloned.1.call-start = ((), (), s32[]{:S(2)}) async-start(), calls=%async_computation.23 | async-start | bytes 442368
  355.3 525.2 %reduce-scatter.42.cloned.1.call-start = ((), (), s32[]{:S(2)}) async-start(), calls=%async_computation.22 | async-start | bytes 2654208
  435.1 517.4 %reduce-scatter.40.cloned.1.call-start = ((), (), s32[]{:S(2)}) async-start(), calls=%async_computation.21 | async-start | bytes 2654208
  525.5 108.4 %all-to-all-start = ((bf16[2,288,4,192]{3,1,0,2:T(8,128)(2,1)}), bf16[2,288,4,192]{3,1,0,2:T(8,128)(2,1)S(1)}, u32[]{:S(2)}, u32[]{:S(2)}) async-start(bf16[2,288,4,192]{3,1,0,2:T(8,128)(2,1)} %copy.126), calls=%async_computation.1 | async-start | bytes 2359296 | tf_op jit(solution)/shard_map/all_to_all | solution.py:595
  (18 other events, 54.1 us)
Sparse Core Ops, SparseCore 0:
  206.4 17.1 reduce-scatter.23
  244.3 33.0 reduce-scatter.27
  287.4 63.7 reduce-scatter.25
  353.6 78.4 reduce-scatter.31
  434.5 78.4 reduce-scatter.29
  516.1 61.3 reduce-scatter.33
  579.1 29.8 all-gather.9
  612.2 62.4 reduce-scatter.37
  678.6 65.7 reduce-scatter.35
  748.1 60.3 reduce-scatter.43
  812.5 67.9 reduce-scatter.41
  884.4 68.0 reduce-scatter.39

commit v2 on v1

--- a/solution.py
+++ b/solution.py
@@ -400,6 +400,767 @@
 precise = lax.Precision.HIGHEST
 
 
+def dot_f32(a, b, dims):
+    return lax.dot_general(a, b, (dims, ((), ())), precision=precise, preferred_element_type=f32)
+
+
+def square(block):
+    return block.reshape(-1, block.shape[-1])
+
+
+def norm_back_rows(upstream, normed, factor, gain_row):
+    scaled = upstream * gain_row
+    mean_one = jnp.mean(scaled, -1, keepdims=True)
+    mean_two = jnp.mean(scaled * normed, -1, keepdims=True)
+    return factor * (scaled - mean_one - normed * mean_two)
+
+
+class Reduction:
+    def __init__(self, order, bits, remote, send, base, held, hops):
+        self.order, self.bits = order, bits
+        self.remote, self.send, self.base = remote, send, base
+        self.held, self.hops = held, hops
+        self.axes = [["x", "z1", "z0", "y"]]
+        for name in order:
+            self.axes.append([a for a in self.axes[-1] if a != name])
+
+    def buffer(self, hop):
+        return self.held if hop == 0 else self.hops[hop - 1]
+
+    def start(self, hop):
+        name = self.order[hop]
+        bit, peer = self.bits[name]
+        place = self.axes[hop].index(name)
+        src = self.buffer(hop).at[(slice(None),) * place + (1 - bit,)]
+        self.send(self.base + 2 + hop, src, self.buffer(hop + 1), peer)
+
+    def finish(self, hop, out=None):
+        name = self.order[hop]
+        bit, peer = self.bits[name]
+        place = self.axes[hop].index(name)
+        src, dst = self.buffer(hop), self.buffer(hop + 1)
+        self.remote(self.base + 2 + hop, dst, dst, peer).wait_recv()
+        left = len(self.axes[hop + 1])
+        if left == 0:
+            out[...] = src[(bit,)].astype(f32) + dst[...].astype(f32)
+            return
+
+        @pl.loop(0, 2**left)
+        def _(i):
+            index = []
+            for k in range(left):
+                index.append(lax.rem(lax.div(i, 2**k), 2))
+            index = tuple(index)
+            full = index[:place] + (bit,) + index[place:]
+            dst[index] = (dst[index].astype(f32) + src[full].astype(f32)).astype(bf16)
+
+
+def backward_kernel(
+    cfg,
+    lengths,
+    positions,
+    targets,
+    states,
+    doc_ids,
+    query_weight,
+    doc_table,
+    w_query,
+    gain_one,
+    gain_two,
+    vocab,
+    out_grad,
+    res,
+    x_in,
+    qkv_in,
+    lse_in,
+    ctx_in,
+    n1_in,
+    f1_in,
+    hl_in,
+    act_in,
+    gp_in,
+    n2_in,
+    f2_in,
+    wq_in,
+    wo_in,
+    wu_in,
+    wd_in,
+    output,
+    nll_out,
+    gt_out,
+    gs_out,
+    gwq_out,
+    down_out,
+    up_out,
+    qk_out,
+    vo_out,
+    vec_out,
+    big,
+    head,
+    pk,
+    lg,
+    ut,
+    us,
+    ur,
+    ss,
+    sr,
+    lb,
+    dlog,
+    st_all,
+    diff,
+    og,
+    tmp,
+    n1,
+    n2,
+    f1,
+    f2,
+    dy,
+    act,
+    gp,
+    wq,
+    wo,
+    wu,
+    wd,
+    qkv,
+    ctx,
+    lse,
+    d_t,
+    x_t,
+    d_up,
+    dctx,
+    dqkv,
+    dxb,
+    gt,
+    sums,
+    sums_in,
+    qk_send,
+    vo_send,
+    parts,
+    *rest,
+):
+    n_seq, seq, model, queries, slots, table, docs = cfg
+    red_bufs, (send_sem, recv_sem, local_sem) = rest[:-3], rest[-3:]
+    m_rows = n_seq * seq
+    own_rows = 8 * n_seq
+    d = lax.axis_index("doc")
+    t = lax.axis_index("tensor")
+    t1, t2 = flip(t, 1), flip(t, 2)
+    t3 = flip(t1, 2)
+    x_bit = lax.div(t, 2)
+    bits = {
+        "x": (x_bit, {"tensor": t2}),
+        "y": (lax.rem(d, 2), {"doc": flip(d, 1)}),
+        "z0": (lax.rem(lax.div(d, 2), 2), {"doc": flip(d, 2)}),
+        "z1": (lax.div(d, 4), {"doc": flip(d, 4)}),
+    }
+
+    barrier = pltpu.get_barrier_semaphore()
+    doc_peers = [lax.rem(d + k, docs) for k in range(1, docs)]
+    peers = [{"tensor": p} for p in (t1, t2, t3)] + [{"doc": p} for p in doc_peers]
+    for peer in peers:
+        pl.semaphore_signal(barrier, inc=1, device_id=peer, device_id_type=MESH)
+    pl.semaphore_wait(barrier, len(peers))
+
+    def remote(number, src, dst, peer):
+        return pltpu.make_async_remote_copy(
+            src_ref=src,
+            dst_ref=dst,
+            send_sem=send_sem.at[number],
+            recv_sem=recv_sem.at[number],
+            device_id=peer,
+            device_id_type=MESH,
+        )
+
+    started = []
+
+    def send(number, src, dst, peer):
+        copy = remote(number, src, dst, peer)
+        copy.start()
+        started.append(copy)
+
+    def arrived(number, ref):
+        remote(number, ref, ref, {"tensor": t1}).wait_recv()
+
+    loads = {}
+
+    def load(name, src, dst):
+        copy = pltpu.make_async_copy(src, dst, local_sem.at[len(loads)])
+        copy.start()
+        loads[name] = copy
+
+    own = pl.multiple_of(t * n_seq, n_seq)
+    load("head", res.at[:, pl.ds(0, 32)], head)
+    load("vocab", vocab, big)
+    base = 0
+    st_all[d] = states[...]
+    for k, p in enumerate(doc_peers):
+        send(base + k, states, st_all.at[d], {"doc": p})
+    states_base = base
+    base += docs - 1
+    load("og", out_grad.at[pl.ds(own, n_seq)], og)
+    load("n2", n2_in, n2)
+    load("f2", f2_in, f2)
+    order = (t3, t1, t2, t)
+    load("act0", act_in.at[order[0]], act.at[0])
+    load("act1", act_in.at[order[1]], act.at[1])
+    for i in range(2):
+        load("wd%d" % i, wd_in.at[order[i]], wd.at[i])
+        load("wu%d" % i, wu_in.at[order[i]], wu.at[i])
+    load("gp0", gp_in.at[order[0]], gp.at[0])
+    load("gp1", gp_in.at[order[1]], gp.at[1])
+    load("hl", hl_in, tmp)
+    load("n1", n1_in, n1)
+    load("f1", f1_in, f1)
+    load("wo", wo_in, wo)
+    for i in range(2):
+        load("wq%d" % i, wq_in.at[order[i]], wq.at[i])
+        load("qkv%d" % i, qkv_in.at[order[i]], qkv.at[i])
+    load("ctx", ctx_in, ctx)
+    load("lse", lse_in, lse)
+    first_row = d * (4 * n_seq)
+    lane = lax.broadcasted_iota(jnp.int32, (own_rows, 32 * n_seq), 1)
+    line = lax.broadcasted_iota(jnp.int32, (own_rows, 32 * n_seq), 0)
+    spot = jnp.zeros((own_rows, 32 * n_seq), jnp.int32)
+    for b in range(own_rows):
+        query = lax.rem(first_row + t * n_seq + b // 8, queries)
+        spot = jnp.where(line == b, positions[query, b % 8] + 32 * (b // 8), spot)
+    hot = (lane == spot).astype(f32)
+    hot_low = hot.astype(bf16)
+    loads["head"].wait()
+    pk[t] = dot(hot_low, rows_of(head[...])).astype(bf16)
+    pick_base = base
+    for k, p in enumerate((t1, t2, t3)):
+        send(base + k, pk.at[t], pk.at[t], {"tensor": p})
+    base += 3
+    out_base = base
+    base += 3
+    send(out_base, res, output.at[pl.ds(own, n_seq)], {"tensor": t2})
+    send(out_base + 1, res, output.at[pl.ds(own, n_seq)], {"tensor": t1})
+    load("out", res, output.at[pl.ds(own, n_seq)])
+    all_rows = 4 * own_rows
+    vocab_local = vocab.shape[0] * model
+    chunk = model
+    tall = lax.broadcasted_iota(jnp.int32, (all_rows, 1), 0)
+    goal = jnp.zeros((all_rows, 1), jnp.int32)
+    for b in range(all_rows):
+        query = lax.rem(first_row + b // 8, queries)
+        goal = jnp.where(tall == b, targets[query, b % 8], goal)
+    goal = goal - t * vocab_local
+    for k, p in enumerate((t1, t2, t3)):
+        arrived(pick_base + k, pk.at[p])
+    loads["vocab"].wait()
+
+    @pl.loop(0, vocab_local // chunk)
+    def _(j):
+        start = pl.multiple_of(j * chunk, chunk)
+        lg[:, pl.ds(start, chunk)] = dot_nt(rows_of(pk[...]), square(big[j]))
+
+    high = jnp.max(lg[...], 1, keepdims=True)
+    ut[...] = jnp.zeros_like(ut)
+
+    def vocab_step(j, carry):
+        mass, chosen = carry
+        start = pl.multiple_of(j * chunk, chunk)
+        values = lg[:, pl.ds(start, chunk)]
+        e = jnp.exp(values - high)
+        index = lax.broadcasted_iota(jnp.int32, (all_rows, chunk), 1) + start
+        hits = (index == goal).astype(f32)
+        both = jnp.concatenate([e, hits], 0).astype(bf16)
+        ut[...] += dot(both, square(big[j]))
+        mass = mass + jnp.sum(e, 1, keepdims=True)
+        chosen = chosen + jnp.sum(hits * values, 1, keepdims=True)
+        return mass, chosen
+
+    zero = jnp.zeros((all_rows, 1), f32)
+    mass, chosen = lax.fori_loop(0, vocab_local // chunk, vocab_step, (zero, zero))
+    spread = lax.broadcasted_iota(jnp.int32, (all_rows, 128), 1)
+    stats = jnp.where(spread == 0, high, jnp.where(spread == 1, mass, chosen))
+    mean_row = (ut[:all_rows] * (1.0 / mass)).astype(bf16)
+    goal_row = ut[all_rows:].astype(bf16)
+    for j in range(4):
+        part = slice(j * own_rows, (j + 1) * own_rows)
+        us[j, :, :model] = mean_row[part]
+        us[j, :, model:] = goal_row[part]
+        ss[j] = stats[part]
+    part_base = base
+    base += 6
+    for k, p in enumerate((t1, t2, t3)):
+        send(part_base + k, ss.at[p], sr.at[t], {"tensor": p})
+        send(part_base + 3 + k, us.at[p], ur.at[t], {"tensor": p})
+    sr[t] = ss[t]
+    ur[t] = us[t]
+    for k, p in enumerate((t1, t2, t3)):
+        arrived(part_base + k, sr.at[p])
+    highs = [sr[j, :, 0:1] for j in range(4)]
+    top = jnp.maximum(jnp.maximum(highs[0], highs[1]), jnp.maximum(highs[2], highs[3]))
+    weights = [sr[j, :, 1:2] * jnp.exp(highs[j] - top) for j in range(4)]
+    whole = weights[0] + weights[1] + weights[2] + weights[3]
+    picked_logit = sr[0, :, 2:3] + sr[1, :, 2:3] + sr[2, :, 2:3] + sr[3, :, 2:3]
+    loglik = picked_logit - (top + jnp.log(whole))
+    mine = first_row + t * n_seq
+    for s in range(n_seq):
+        total = jnp.sum(loglik[8 * s : 8 * s + 8], 0, keepdims=True)
+        lb[mine + s] = jnp.broadcast_to(total, (1, 128))
+    like_base = base
+    base += 3
+    mine_ref = lb.at[pl.ds(mine, n_seq)]
+    for k, p in enumerate((t1, t2, t3)):
+        send(like_base + k, mine_ref, mine_ref, {"tensor": p})
+    for k, p in enumerate((t1, t2, t3)):
+        arrived(part_base + 3 + k, ur.at[p])
+    gap = jnp.zeros((own_rows, model), f32)
+    for j in range(4):
+        share = weights[j] / whole
+        gap = gap + ur[j, :, model:].astype(f32) - share * ur[j, :, :model].astype(f32)
+    diff[...] = gap
+    for k, p in enumerate((t1, t2, t3)):
+        arrived(like_base + k, lb.at[pl.ds(first_row + p * n_seq, n_seq)])
+    group_base = base
+    base += docs - 1
+    group_ref = lb.at[pl.ds(first_row, 4 * n_seq)]
+    for k, p in enumerate(doc_peers):
+        send(group_base + k, group_ref, group_ref, {"doc": p})
+    for k in range(docs - 1):
+        source = lax.rem(d + docs - 1 - k, docs)
+        arrived(states_base + k, st_all.at[source])
+    share_width = model // docs
+    emb = jnp.zeros((states.shape[0], 128), f32)
+    for j in range(docs):
+        emb = emb + dot(st_all[j, :, :share_width], w_query[j])
+    emb = emb[:queries]
+    table_score = dot_f32(emb, doc_table[...], ((1,), (1,)))
+    entry = lax.broadcasted_iota(jnp.int32, (queries, table), 1)
+    hot_docs = [(entry == doc_ids[:, k : k + 1]).astype(f32) for k in range(slots)]
+    prior = [jnp.sum(hot_docs[k] * table_score, 1, keepdims=True) for k in range(slots)]
+    for k in range(docs - 1):
+        source = lax.rem(d + docs - 1 - k, docs)
+        arrived(group_base + k, lb.at[pl.ds(source * (4 * n_seq), 4 * n_seq)])
+    joint = []
+    for k in range(slots):
+        column = lb[k * queries : (k + 1) * queries].reshape(queries, 128)
+        joint.append(prior[k] + column[:, 0:1])
+
+    def log_sum(values):
+        largest = functools.reduce(jnp.maximum, values)
+        total = functools.reduce(jnp.add, [jnp.exp(v - largest) for v in values])
+        return largest + jnp.log(total)
+
+    prior_lse, joint_lse = log_sum(prior), log_sum(joint)
+    nll_out[...] = jnp.broadcast_to(prior_lse - joint_lse, (queries, 128))
+    spread_docs = jnp.zeros((queries, table), f32)
+    for k in range(slots):
+        post = jnp.exp(joint[k] - joint_lse)
+        before = jnp.exp(prior[k] - prior_lse)
+        spread_docs = spread_docs + hot_docs[k] * (query_weight[...] * (before - post))
+        value = -query_weight[...] * post
+        dlog[k * queries : (k + 1) * queries] = jnp.broadcast_to(value, (queries, 128)).reshape(
+            queries, 1, 128
+        )
+    d_emb = dot_f32(spread_docs, doc_table[...], ((1,), (0,))).astype(bf16)
+    gs_out[...] = dot_nt(d_emb, w_query[d])
+    gwq_out[...] = dot_tn(st_all[d, :queries, :share_width].astype(f32), d_emb.astype(f32))
+    scattered = []
+    for s in range(n_seq):
+        coefficient = dlog[mine + s]
+        rows = diff[8 * s : 8 * s + 8] * coefficient[:, 0:1]
+        scattered.append(
+            dot_f32(hot[8 * s : 8 * s + 8, 32 * s : 32 * s + 32], rows, ((0,), (0,)))
+        )
+    sums[0] = jnp.zeros(sums.shape[1:], f32)
+    for name in ("og", "n2", "f2"):
+        loads[name].wait()
+    step_rows = 96
+
+    def add_sum(row, value):
+        sums[0, 4, row : row + 1] += jnp.sum(value, 0, keepdims=True)
+
+    def second_norm(s, rows, flat, extra):
+        upstream = og[s, rows].astype(f32)
+        if extra is not None:
+            upstream = upstream + extra
+        normed = n2[flat]
+        back = norm_back_rows(upstream, normed, f2[flat], gain_two[...])
+        add_sum(4, upstream * normed)
+        add_sum(5, upstream)
+        add_sum(3, back)
+        dy[flat] = back
+        og[s, rows] = back.astype(bf16)
+
+    for s in range(n_seq):
+        extra = jnp.concatenate([scattered[s], jnp.zeros((step_rows - 32, model), f32)], 0)
+        second_norm(s, pl.ds(0, step_rows), pl.ds(s * seq, step_rows), extra)
+
+        @pl.loop(1, seq // step_rows)
+        def _(i):
+            start = pl.multiple_of(i * step_rows, step_rows)
+            second_norm(s, pl.ds(start, step_rows), pl.ds(s * seq + start, step_rows), None)
+
+    d_t[...] = rows_of(og[...]).T
+    orders = (
+        ("y", "z0", "x", "z1"),
+        ("z0", "y", "x", "z1"),
+        ("y", "z0", "x", "z1"),
+        ("z0", "y", "x", "z1"),
+    )
+    reds = []
+    for k, names in enumerate(orders):
+        bufs = red_bufs[5 * k : 5 * k + 5]
+        reds.append(Reduction(names, bits, remote, send, base, bufs[0], bufs[1:]))
+        base += 6
+    down, up, qk, vo = reds
+    block_shape = (2, 2, 2, model // docs)
+
+    def emit(red, i, sending, shard, lanes, value):
+        value = value.reshape(block_shape + (value.shape[-1],))
+        which = lax.div(shard, 2)
+        if i < 2:
+            sending[which, :, :, :, :, lanes] = value.astype(bf16)
+        else:
+            total = value + red.held[which, :, :, :, :, lanes].astype(f32)
+            red.held[which, :, :, :, :, lanes] = total.astype(bf16)
+
+    def before_block(red, i, shard):
+        if i >= 2:
+            which = lax.div(shard, 2)
+            arrived(red.base + (i - 2), red.held.at[which])
+
+    def after_block(red, i, sending, shard):
+        if i < 2:
+            which = lax.div(shard, 2)
+            send(red.base + i, sending.at[which], red.held.at[which], {"tensor": t1})
+
+    down_send, up_send = big.at[0:2], big.at[2:4]
+    tiles = model // 256
+    for i, shard in enumerate(order):
+        loads["act%d" % i].wait()
+        before_block(down, i, shard)
+
+        @pl.loop(0, tiles)
+        def _(n):
+            lanes = pl.ds(pl.multiple_of(n * 256, 256), 256)
+            emit(down, i, down_send, shard, lanes, dot(d_t[...], act[i % 2, :, lanes]))
+
+        if i + 2 < 4:
+            load("act%d" % (i + 2), act_in.at[order[i + 2]], act.at[i % 2])
+        after_block(down, i, down_send, shard)
+    down.start(0)
+    loads["hl"].wait()
+    x_t[...] = tmp[...].T
+    load("x", x_in, tmp)
+    for i, shard in enumerate(order):
+        for name in ("gp", "wd", "wu"):
+            loads["%s%d" % (name, i)].wait()
+        before_block(up, i, shard)
+
+        @pl.loop(0, tiles)
+        def _(n):
+            lanes = pl.ds(pl.multiple_of(n * 256, 256), 256)
+            value = dot_nt(rows_of(og[...]), wd[i % 2, lanes]) * gp[i % 2, :, lanes].astype(f32)
+            low = value.astype(bf16)
+            d_up[:, lanes] = low
+            sums[0, shard, 0:1, lanes] = jnp.sum(low.astype(f32), 0, keepdims=True)
+
+        if i + 2 < 4:
+            load("gp%d" % (i + 2), gp_in.at[order[i + 2]], gp.at[i % 2])
+            load("wd%d" % (i + 2), wd_in.at[order[i + 2]], wd.at[i % 2])
+
+        @pl.loop(0, tiles)
+        def _(n):
+            lanes = pl.ds(pl.multiple_of(n * 256, 256), 256)
+            value = dot_nt(d_up[...], wu[i % 2, lanes])
+            if i == 0:
+                n2[:, lanes] = value
+            else:
+                n2[:, lanes] += value
+            emit(up, i, up_send, shard, lanes, dot(x_t[...], d_up[:, lanes]))
+
+        if i + 2 < 4:
+            load("wu%d" % (i + 2), wu_in.at[order[i + 2]], wu.at[i % 2])
+        after_block(up, i, up_send, shard)
+    up.start(0)
+    arrived(out_base, output.at[pl.ds(t2 * n_seq, n_seq)])
+    passed = output.at[pl.ds(t2 * n_seq, n_seq)]
+    send(out_base + 2, passed, passed, {"tensor": t1})
+    loads["n1"].wait()
+    loads["f1"].wait()
+
+    @pl.loop(0, m_rows // step_rows)
+    def _(i):
+        flat = pl.ds(pl.multiple_of(i * step_rows, step_rows), step_rows)
+        s, start = lax.div(i, seq // step_rows), lax.rem(i, seq // step_rows) * step_rows
+        upstream = dy[flat] + n2[flat]
+        normed = n1[flat]
+        back = norm_back_rows(upstream, normed, f1[flat], gain_one[...])
+        add_sum(1, upstream * normed)
+        add_sum(2, upstream)
+        add_sum(0, back)
+        dy[flat] = back
+        og[s, pl.ds(pl.multiple_of(start, step_rows), step_rows)] = back.astype(bf16)
+
+    d_t[...] = rows_of(og[...]).T
+    loads["x"].wait()
+    x_t[...] = tmp[...].T
+    for name in ("wo", "ctx", "lse"):
+        loads[name].wait()
+    key_index = lax.broadcasted_iota(jnp.int32, (seq, seq), 0)
+    for i, shard in enumerate(order):
+        loads["qkv%d" % i].wait()
+        loads["wq%d" % i].wait()
+        dctx[...] = dot_nt(rows_of(og[...]), wo[shard]).astype(bf16)
+
+        @pl.loop(0, n_seq)
+        def _(s):
+            rows = pl.ds(pl.multiple_of(s * seq, 32), seq)
+            row = first_row + t * n_seq + s
+            length = lengths[lax.rem(row, queries), lax.div(row, queries)]
+            z = qkv[i % 2, s]
+            upstream = dctx[rows]
+            d_q, d_k, d_v = [], [], []
+            for h in range(3):
+                qh = z[:, h * 64 : h * 64 + 64]
+                kh = z[:, 192 + h * 64 : 256 + h * 64]
+                vh = z[:, 384 + h * 64 : 448 + h * 64]
+                dc = upstream[:, h * 64 : h * 64 + 64]
+                scores = jnp.where(key_index < length, dot_nt(kh, qh * 0.125), -1000000000.0)
+                prob = jnp.exp(scores - lse[shard, s, h])
+                d_v.append(dot(prob.astype(bf16), dc))
+                d_prob = dot_nt(vh, dc)
+                inner = jnp.sum(d_prob * prob, 0, keepdims=True)
+                d_score = (prob * (d_prob - inner)).astype(bf16)
+                d_k.append(dot(d_score, qh) * 0.125)
+                d_q.append(dot_tn(kh, d_score) * 0.125)
+            first = jnp.concatenate(d_q, 0).T
+            both = jnp.concatenate([first] + d_k + d_v, 1).astype(bf16)
+            dqkv[rows] = both
+            lse_sum = jnp.sum(both.astype(f32), 0, keepdims=True)
+            parts[s] = lse_sum
+
+        total = parts[0]
+        for s in range(1, n_seq):
+            total = total + parts[s]
+        sums[0, shard, 1:2, : 3 * 192] = total
+        before_block(qk, i, shard)
+        emit(qk, i, qk_send, shard, slice(None), dot(x_t[...], dqkv[:, :384]))
+        after_block(qk, i, qk_send, shard)
+        before_block(vo, i, shard)
+        value = jnp.concatenate([dot(x_t[...], dqkv[:, 384:]), dot(d_t[...], ctx[shard])], 1)
+        emit(vo, i, vo_send, shard, slice(None), value)
+        after_block(vo, i, vo_send, shard)
+
+        @pl.loop(0, tiles)
+        def _(n):
+            lanes = pl.ds(pl.multiple_of(n * 256, 256), 256)
+            value = dot_nt(dqkv[...], wq[i % 2, lanes])
+            if i == 0:
+                n1[:, lanes] = value
+            else:
+                n1[:, lanes] += value
+
+        if i + 2 < 4:
+            load("qkv%d" % (i + 2), qkv_in.at[order[i + 2]], qkv.at[i % 2])
+            load("wq%d" % (i + 2), wq_in.at[order[i + 2]], wq.at[i % 2])
+
+    for j in range(4):
+        lanes = slice(j * 192, j * 192 + 192)
+        dxb[j] = (n1[:, lanes] + dy[:, lanes]).astype(bf16)
+    tok_base = base
+    base += 3
+    for k, p in enumerate((t2, t3, t1)):
+        send(tok_base + k, dxb.at[p], gt.at[t], {"tensor": p})
+    gt[t] = dxb[t]
+    vec_base = base
+    vec_peers = [{"tensor": t1}, bits["y"][1], bits["z0"][1], bits["x"][1], bits["z1"][1]]
+    base += len(vec_peers)
+
+    def vec_start(k):
+        send(vec_base + k, sums.at[k], sums_in.at[k], vec_peers[k])
+
+    def vec_finish(k):
+        arrived(vec_base + k, sums_in.at[k])
+        sums[k + 1] = sums[k] + sums_in[k]
+
+    qk.start(0)
+    vo.start(0)
+    vec_start(0)
+    vec_finish(0)
+    vec_start(1)
+    down.finish(0)
+    down.start(1)
+    up.finish(0)
+    up.start(1)
+    vec_finish(1)
+    vec_start(2)
+    down.finish(1)
+    down.start(2)
+    up.finish(1)
+    up.start(2)
+    vec_finish(2)
+    vec_start(3)
+    qk.finish(0)
+    qk.start(1)
+    vo.finish(0)
+    vo.start(1)
+    down.finish(2)
+    down.start(3)
+    up.finish(2)
+    up.start(3)
+    vec_finish(3)
+    vec_start(4)
+    for k, p in enumerate((t2, t3, t1)):
+        arrived(tok_base + k, gt.at[p])
+    load("gt", gt, gt_out)
+    qk.finish(1)
+    qk.start(2)
+    vo.finish(1)
+    vo.start(2)
+    down.finish(3, down_out)
+    up.finish(3, up_out)
+    vec_finish(4)
+    vec_out[...] = sums[5]
+    qk.finish(2)
+    qk.start(3)
+    vo.finish(2)
+    vo.start(3)
+    qk.finish(3, qk_out)
+    vo.finish(3, vo_out)
+    arrived(out_base + 1, output.at[pl.ds(t1 * n_seq, n_seq)])
+    arrived(out_base + 2, output.at[pl.ds(t3 * n_seq, n_seq)])
+    loads["out"].wait()
+    loads["gt"].wait()
+    for copy in started:
+        copy.wait_send()
+
+
+def backward(
+    n_seq,
+    seq,
+    model,
+    docs,
+    tables,
+    vocab,
+    out_grad,
+    kept,
+):
+    lengths, positions, targets, states, doc_ids, query_weight, doc_table, w_query = tables[:8]
+    queries, slots = doc_ids.shape
+    table = doc_table.shape[0]
+    m_rows = n_seq * seq
+    own_rows = 8 * n_seq
+    all_rows = 4 * own_rows
+    share = model // docs
+    (res, x, qkv, lse, ctx, n1, f1, hl, act, gp, n2, f2, wq, wo, wu, wd) = kept
+
+    def flat(a):
+        return a.reshape(a.shape[:-3] + (a.shape[-3] * a.shape[-2], a.shape[-1]))
+
+    kept = [
+        res,
+        flat(x),
+        qkv,
+        lse,
+        flat(ctx),
+        flat(n1),
+        flat(f1),
+        flat(hl),
+        flat(act),
+        flat(gp),
+        flat(n2),
+        flat(f2),
+        flat(wq),
+        flat(wo),
+        flat(wu),
+        flat(wd),
+    ]
+    vocab = vocab.reshape(vocab.shape[0] // model, 2, 2, 2, share, model)
+
+    def sds(shape, dtype):
+        return jax.ShapeDtypeStruct(shape, dtype)
+
+    any_spec = pl.BlockSpec(memory_space=pl.ANY)
+    vmem_spec = pl.BlockSpec(memory_space=pltpu.VMEM)
+    smem_spec = pl.BlockSpec(memory_space=pltpu.SMEM)
+    outs = [
+        sds((4 * n_seq, seq, model), bf16),
+        sds((queries, 128), f32),
+        sds((4, m_rows, model // 4), bf16),
+        sds((queries, share), f32),
+        sds((share, 128), f32),
+        sds((share, model), f32),
+        sds((share, model), f32),
+        sds((share, 384), f32),
+        sds((share, 384), f32),
+        sds((5, 8, model), f32),
+    ]
+    out_specs = [any_spec, vmem_spec, any_spec] + [vmem_spec] * 7
+
+    def vm(shape, dtype):
+        return pltpu.VMEM(shape, dtype)
+
+    scratch = [
+        vm(vocab.shape, bf16),
+        vm((n_seq, 32, model), bf16),
+        vm((4, own_rows, model), bf16),
+        vm((all_rows, vocab.shape[0] * model), f32),
+        vm((2 * all_rows, model), f32),
+        vm((4, own_rows, 2 * model), bf16),
+        vm((4, own_rows, 2 * model), bf16),
+        vm((4, own_rows, 128), f32),
+        vm((4, own_rows, 128), f32),
+        vm((docs * 4 * n_seq, 1, 128), f32),
+        vm((docs * 4 * n_seq, 1, 128), f32),
+        vm((docs,) + states.shape, bf16),
+        vm((own_rows, model), f32),
+        vm((n_seq, seq, model), bf16),
+        vm((m_rows, model), bf16),
+        vm((m_rows, model), f32),
+        vm((m_rows, model), f32),
+        vm((m_rows, 1), f32),
+        vm((m_rows, 1), f32),
+        vm((m_rows, model), f32),
+        vm((2, m_rows, model), bf16),
+        vm((2, m_rows, model), bf16),
+        vm((2, model, 576), bf16),
+        vm((4, 192, model), bf16),
+        vm((2, model, model), bf16),
+        vm((2, model, model), bf16),
+        vm((2, n_seq, seq, 576), bf16),
+        vm((4, m_rows, 192), bf16),
+        vm((4, n_seq, 3, 1, seq), f32),
+        vm((model, m_rows), bf16),
+        vm((model, m_rows), bf16),
+        vm((m_rows, model), bf16),
+        vm((m_rows, 192), bf16),
+        vm((m_rows, 576), bf16),
+        vm((4, m_rows, 192), bf16),
+        vm((4, m_rows, 192), bf16),
+        vm((6, 5, 8, model), f32),
+        vm((5, 5, 8, model), f32),
+        vm((2, 2, 2, 2, share, 384), bf16),
+        vm((2, 2, 2, 2, share, 384), bf16),
+        vm((n_seq, 1, 576), f32),
+    ]
+    for width in (model, model, 384, 384):
+        for left in (4, 3, 2, 1, 0):
+            scratch.append(vm((2,) * left + (share, width), bf16))
+    copies = 2 * (docs - 1) + 3 + 3 + 6 + 3 + 6 * 4 + 3 + 5
+    scratch += [
+        pltpu.SemaphoreType.DMA((copies,)),
+        pltpu.SemaphoreType.DMA((copies,)),
+        pltpu.SemaphoreType.DMA((40,)),
+    ]
+    return pl.pallas_call(
+        functools.partial(backward_kernel, (n_seq, seq, model, queries, slots, table, docs)),
+        out_shape=outs,
+        in_specs=[smem_spec] * 3 + [vmem_spec] * 7 + [any_spec] * 18,
+        out_specs=out_specs,
+        scratch_shapes=scratch,
+        compiler_params=pltpu.CompilerParams(
+            collective_id=1, has_side_effects=True, vmem_limit_bytes=60 * MIB
+        ),
+        name="layer_backward",
+    )(*tables, vocab, out_grad, *kept)
+
+
 def joined(array, axis, combine):
     everything = jax.tree.map(lambda part: lax.all_gather(part, axis), array)
     initial = jax.tree.map(lambda part: part[0], everything)
@@ -495,6 +1256,49 @@
         vectors,
         rows,
     )
+    docs = lax.axis_size("doc")
+    if docs == 8 and n_seq == 2:
+        share = model_width // docs
+        states_rows = max(16, -(-queries // 16) * 16)
+        states = jnp.zeros((states_rows, 128), bf16).at[:queries, :share].set(query_states)
+        tables = (
+            lengths,
+            positions,
+            targets,
+            states,
+            doc_ids,
+            query_weight[:, None],
+            doc_table,
+            w_query.reshape(docs, share, w_query.shape[1]),
+            rows[1],
+            rows[4],
+        )
+        kept = (res, x, qkv, lse, ctx, n1, f1, hl, act, gp, n2, f2, wq, wo, wu, wd)
+        (output, nll, gt, gs, gwq, g_down, g_up, g_qk, g_vo, sums) = backward(
+            n_seq, seq_length, model_width, docs, tables, vocab_table, out_grad, kept
+        )
+        d = lax.axis_index("doc")
+        six = lax.dynamic_slice_in_dim(sums[4, :6], d * share, share, 1)
+        mine = lax.dynamic_index_in_dim(sums[:4], t, 0, keepdims=False)
+        return (
+            output,
+            nll[:, 0],
+            gt.reshape(sequences, seq_length, part_width).astype(f32),
+            gs,
+            jnp.stack([g_qk[:, :192], g_qk[:, 192:], g_vo[:, :192]]),
+            jnp.stack([mine[1, :192], mine[1, 384:576]]),
+            g_vo[:, 192:].T,
+            six[0],
+            six[1],
+            six[2],
+            g_up,
+            mine[0],
+            g_down.T,
+            six[3],
+            six[4],
+            six[5],
+            gwq,
+        )
     output = lax.all_gather(res, "tensor", axis=0, tiled=True)
     row_index = lax.axis_index("doc") * sequences + jnp.arange(sequences, dtype=jnp.int32)
     slot_index = row_index // queries

time: 968 us -> 268 us (0.28)
  waiting for transfers between devices: 556 us -> 0 us
  Pallas kernels: 84.8 us -> 240 us
  blocking collectives: 133 us -> 0 us
  matrix products: 78.3 us -> 0 us
  local copies, waits for them, and re-layouts: 72.5 us -> 21.7 us
  between operations: 16.5 us -> 0.88 us
  other arithmetic: 18.3 us -> 4.24 us
    unnamed x18 -> x0, waiting for transfers between devices: 361 us -> none
    reduce_scatter x5 -> x0, waiting for transfers between devices: 195 us -> none  [the longest x4 194 us: shards(): lax.psum_scatter(a, 'tensor', scatter_dimension=0, tiled=True)[0]]
    pallas_call x0 -> x1, Pallas kernels: none -> 153 us  [backward(): pl.pallas_call(functools.partial(backward_kernel, (n_seq, seq, model, que...]
    dot_general x21 -> x0, matrix products: 77.4 us -> none  [the longest x1 9.19 us: shards(): jnp.einsum('tbqhe,tbkhe->tbhqk', d_ctx, hv, preferred_element_type=f32)]
    all_gather x5 -> x0, blocking collectives: 61.2 us -> none  [the longest x1 27.9 us: shards(): states = lax.all_gather(query_states, 'doc', axis=1, tiled=True)]
    psum x2 -> x0, blocking collectives: 42.3 us -> none  [the longest x1 35.8 us: shards(): g_b = lax.psum(over_t(g_b), 'doc')]
    unnamed x2 -> x0, blocking collectives: 29.8 us -> none
    unnamed x87 -> x44, local copies, waits for them, and re-layouts: 28.1 us -> 6.45 us
  transfers between devices with their start and end apart: 13 -> 0, of which waited for: 10 -> 0; matrix products, arithmetic and copies ran while one was open for 11% -> 0% of each run, Pallas kernels for 0% -> 0%
where the time goes in v2:
time: 268 us; the launch traced here: 266 us
  Pallas kernels  240 us (90%)
  local copies, waits for them, and re-layouts  21.7 us (8%)
  other arithmetic  4.24 us (2%)
    pallas_call x1, Pallas kernels, backward(): pl.pallas_call(functools.partial(backward_kernel, (n_seq, seq, model, que...  153 us
    pallas_call x1, Pallas kernels, forward(): pl.pallas_call(functools.partial(forward_kernel, (n_seq, seq, model, quer...  86.7 us
    unnamed x44, local copies, waits for them, and re-layouts  6.45 us

profile of v2, /device:TPU:0, one launch (start us, length us, event | category | flops | bytes accessed | tf_op | source)
XLA Modules:
  0.0 266.4 jit_solution(5440701241176671276)
XLA Ops:
  0.7 1.2 fusion
  2.5 1.3 pad_maximum_fusion.w_qkv
  4.4 0.6 broadcast_in_dim.24.gain_one
  5.5 0.6 broadcast_in_dim.26.b_out
  7.9 86.7 %layer_forward.1 = (bf16[2,288,768]{2,1,0:T(8,128)(2,1)}, bf16[4,2,288,576]{3,2,1,0:T(8,128)(2,1)}, f32[4,2,3,1,288]{4,3,2,1,0:T(1,128)}, bf16[4,2,288,192]{3,2,...) custom-call(s32[8,8]{1,0:T(8,128)} %lengths.3, ...), custom_call_target="tpu_custom_call" | custom-call | tf_op jit(solution)/shard_map/layer_forward/pallas_call | solution.py:387
  94.6 0.7 copy.48.query_weight
  95.2 0.6 scatter.14.states
  95.8 152.8 %layer_backward.1 = (bf16[8,288,768]{2,1,0:T(8,128)(2,1)}, f32[8,128]{1,0:T(8,128)}, bf16[4,576,192]{2,1,0:T(8,128)(2,1)}, f32[8,96]{1,0:T(8,128)}, f32[96,128]{...) custom-call(s32[8,8]{1,0:T(8,128)} %lengths.3, ...), custom_call_target="tpu_custom_call" | custom-call | tf_op jit(solution)/shard_map/layer_backward/pallas_call | solution.py:1151
  248.7 0.9 slice.151
  249.6 0.6 pad_maximum_fusion.2
  250.2 1.7 slice_bitcast_fusion
  251.9 1.1 slice_bitcast_fusion.3
  253.0 0.7 pad_maximum_fusion.1
  253.7 1.6 convert.1
  255.4 1.9 copy.49
  257.3 1.3 dynamic-slice_reduce_fusion
  258.6 1.3 slice.155
  260.0 0.8 constant_dynamic-slice_fusion
  261.3 0.6 slice_reduce_fusion
  261.9 1.8 copy.57
  263.7 0.6 copy.58
  264.3 0.7 copy.59
  265.0 0.7 copy.60
  265.7 0.6 copy.61
  (53 shorter events, 4.0 us)
Async XLA Ops:
  1.9 1.9 copy-start.16
  1.9 1.9 copy-start.7
  2.1 2.3 copy-start.8
  2.1 2.9 %copy-start.9 = (f32[768]{0:T(1024)S(1)}, f32[768]{0:T(1024)}, u32[]{:S(2)}) copy-start(f32[768]{0:T(1024)} %param.43) | copy-start | bytes 9220
  2.1 3.4 %copy-start.10 = (f32[768]{0:T(1024)S(1)}, f32[768]{0:T(1024)}, u32[]{:S(2)}) copy-start(f32[768]{0:T(1024)} %param.36) | copy-start | bytes 9220
  2.1 4.0 %copy-start.11 = (f32[768]{0:T(1024)S(1)}, f32[768]{0:T(1024)}, u32[]{:S(2)}) copy-start(f32[768]{0:T(1024)} %param.38) | copy-start | bytes 9220
  2.1 4.6 %copy-start.12 = (f32[768]{0:T(1024)S(1)}, f32[768]{0:T(1024)}, u32[]{:S(2)}) copy-start(f32[768]{0:T(1024)} %param.42) | copy-start | bytes 9220
  2.1 5.2 %copy-start.13 = (f32[768]{0:T(1024)S(1)}, f32[768]{0:T(1024)}, u32[]{:S(2)}) copy-start(f32[768]{0:T(1024)} %param.44) | copy-start | bytes 9220
  4.3 3.5 %copy-start.5 = (f32[8,768]{1,0:T(8,128)}, f32[8,768]{1,0:T(8,128)S(1)}, u32[]{:S(2)}) copy-start(f32[8,768]{1,0:T(8,128)S(1)} %scatter.19.vectors) | copy-start | bytes 73732
  7.9 86.7 %copy-start.18 = (f32[8]{0:T(128)S(1)}, f32[8]{0:T(128)}, u32[]{:S(2)}) copy-start(f32[8]{0:T(128)} %param.53) | copy-start | bytes 100
  7.9 87.4 %copy-start.17 = (bf16[8,96]{1,0:T(8,128)(2,1)S(1)}, bf16[8,96]{1,0:T(8,128)(2,1)}, u32[]{:S(2)}) copy-start(bf16[8,96]{1,0:T(8,128)(2,1)} %param.32) | copy-start | bytes 4612
  249.6 0.6 copy-start.4
  249.6 4.1 %copy-start.1 = (bf16[4,576,192]{2,1,0:T(8,128)(2,1)S(1)}, bf16[4,576,192]{2,1,0:T(8,128)(2,1)}, u32[]{:S(2)}) copy-start(bf16[4,576,192]{2,1,0:T(8,128)(2,1)} %get-tuple-element.109) | copy-start | bytes 2654212
  253.7 7.5 %copy-start.14 = (f32[8,128]{1,0:T(8,128)S(1)}, f32[8,128]{1,0:T(8,128)}, u32[]{:S(2)}) copy-start(f32[8,128]{1,0:T(8,128)} %get-tuple-element.108) | copy-start | bytes 12292
  253.7 8.2 %copy-start = (bf16[8,288,768]{2,1,0:T(8,128)(2,1)S(1)}, bf16[8,288,768]{2,1,0:T(8,128)(2,1)}, u32[]{:S(2)}) copy-start(bf16[8,288,768]{2,1,0:T(8,128)(2,1)} %get-tuple-element.185) | copy-start | bytes 10616836
  261.9 1.8 copy-start.15
  261.9 2.4 copy-start.3
  261.9 3.1 %copy-start.2 = (f32[96,768]{1,0:T(8,128)S(1)}, f32[96,768]{1,0:T(8,128)}, u32[]{:S(2)}) copy-start(f32[96,768]{1,0:T(8,128)} %get-tuple-element.115) | copy-start | bytes 884740
  261.9 3.8 %copy-start.6 = (f32[96,128]{1,0:T(8,128)S(1)}, f32[96,128]{1,0:T(8,128)}, u32[]{:S(2)}) copy-start(f32[96,128]{1,0:T(8,128)} %get-tuple-element.201) | copy-start | bytes 147460

commit v3 on v2

--- a/solution.py
+++ b/solution.py
@@ -33,6 +33,17 @@
     return block.reshape(block.shape[0] * block.shape[1], block.shape[2])
 
 
+def picks(positions, first_row, n_seq, queries):
+    shape = (8 * n_seq, 32 * n_seq)
+    lane = lax.broadcasted_iota(jnp.int32, shape, 1)
+    line = lax.broadcasted_iota(jnp.int32, shape, 0)
+    spot = jnp.zeros(shape, jnp.int32)
+    for b in range(8 * n_seq):
+        query = lax.rem(first_row + b // 8, queries)
+        spot = jnp.where(line == b, positions[query, b % 8] + 32 * (b // 8), spot)
+    return (lane == spot).astype(f32)
+
+
 def norm_forward(y):
     centred = y - jnp.mean(y, -1, keepdims=True)
     factor = lax.rsqrt(jnp.mean(centred * centred, -1, keepdims=True) + 1e-12)
@@ -42,12 +53,14 @@
 def forward_kernel(
     cfg,
     lengths,
+    positions,
     tokens,
     w_qkv,
     w_out,
     w_up,
     w_down,
-    vectors,
+    b_qv,
+    b_up,
     b_out,
     gain_one,
     bias_one,
@@ -70,6 +83,7 @@
     wo_all,
     wu_all,
     wd_all,
+    pk,
     tok,
     x_s,
     qkv_s,
@@ -104,6 +118,12 @@
     q1, q2 = flip(q, 1), flip(q, 2)
     q3 = flip(q1, 2)
 
+    def local(number, src, dst):
+        copy = pltpu.make_async_copy(src, dst, local_sem.at[number])
+        copy.start()
+        return copy
+
+    own_q = local(0, w_qkv, wq.at[t])
     barrier = pltpu.get_barrier_semaphore()
     peers = ({"tensor": t1}, {"tensor": t2}, {"tensor": t3}, {"doc": d1}, {"doc": d2})
     for peer in peers:
@@ -130,8 +150,16 @@
         copy.start()
         started.append(copy)
 
-    def send_x(a):
-        send(9 * a, inputs[a].at[q], gathered[a].at[t, q], {"tensor": t2})
+    hops = [(({"doc": d1}, q1), ({"doc": d2}, q2))] * 4
+    hops[1] = hops[3] = hops[0][::-1]
+
+    def send_x(a, pieces=1):
+        count = inputs[a].shape[1] // pieces
+        for k in range(pieces):
+            rows = pl.ds(k * count, count)
+            src, dst = inputs[a].at[q, rows], gathered[a].at[t, q, rows]
+            remote(9 * a, src, dst, {"tensor": t2}).start()
+        started.append(remote(9 * a, inputs[a].at[q], gathered[a].at[t, q], {"tensor": t2}))
 
     def send_core(a):
         send(9 * a + 4, inputs[a], gathered[a].at[t], {"tensor": t1})
@@ -143,56 +171,66 @@
         return gathered[a].at[t2, part]
 
     def after_x(a):
+        (first, _), (second, _) = hops[a]
         arrived(9 * a, piece(a, q))
-        send(9 * a + 1, piece(a, q), piece(a, q), {"doc": d1})
-        send(9 * a + 2, piece(a, q), piece(a, q), {"doc": d2})
+        send(9 * a + 1, piece(a, q), piece(a, q), first)
+        send(9 * a + 2, piece(a, q), piece(a, q), second)
         send(9 * a + 5, piece(a, q), piece(a, q), {"tensor": t1})
 
-    def after_y(a):
-        arrived(9 * a + 1, piece(a, q1))
-        send(9 * a + 3, piece(a, q1), piece(a, q1), {"doc": d2})
-        send(9 * a + 6, piece(a, q1), piece(a, q1), {"tensor": t1})
-
-    def after_z(a):
-        arrived(9 * a + 2, piece(a, q2))
-        send(9 * a + 7, piece(a, q2), piece(a, q2), {"tensor": t1})
+    def after_first(a):
+        (_, part), (second, _) = hops[a]
+        arrived(9 * a + 1, piece(a, part))
+        send(9 * a + 3, piece(a, part), piece(a, part), second)
+        send(9 * a + 6, piece(a, part), piece(a, part), {"tensor": t1})
+
+    def after_second(a):
+        (_, _), (_, part) = hops[a]
+        arrived(9 * a + 2, piece(a, part))
+        send(9 * a + 7, piece(a, part), piece(a, part), {"tensor": t1})
         arrived(9 * a + 3, piece(a, q3))
         send(9 * a + 8, piece(a, q3), piece(a, q3), {"tensor": t1})
 
     def after_core(a):
-        for k, part in enumerate((q, q1, q2, q3)):
+        (_, one), (_, two) = hops[a]
+        for k, part in enumerate((q, one, two, q3)):
             arrived(9 * a + 5 + k, gathered[a].at[t3, part])
 
-    tok_base, vec_base = 36, 39
+    tok_base, vec_base, pick_base = 36, 39, 42
     own = pl.multiple_of(t * n_seq, n_seq)
-
-    def local(number, src, dst):
-        copy = pltpu.make_async_copy(src, dst, local_sem.at[number])
-        copy.start()
-        return copy
-
-    send_x(0)
-    own_q = local(0, w_qkv, wq.at[t])
     own_tok = local(1, tokens.at[pl.ds(own, n_seq)], tok.at[t])
-    for k, peer in enumerate((t1, t2, t3)):
+
+    def send_tokens(k, peer):
         theirs = pl.multiple_of(peer * n_seq, n_seq)
         send(tok_base + k, tokens.at[pl.ds(theirs, n_seq)], tok.at[t], {"tensor": peer})
-        send(vec_base + k, vectors, vec.at[t], {"tensor": peer})
-    send_core(0)
-    own_vec = local(2, vectors, vec.at[t])
+
+    send_x(0, 3)
+    send_tokens(2, t1)
+    send_tokens(0, t2)
+    send_tokens(1, t3)
     own_o = local(3, w_out, wo.at[t])
+    part_width = model // 4
+    gap = jnp.zeros((1, part_width), f32)
+    vec[t, 1:2] = jnp.concatenate([b_qv[0:1], gap, b_qv[1:2], gap], 1)
+    singles = (b_up, None, b_out, gain_one, bias_one, b_down, gain_two, bias_two)
+    for k, ref in enumerate(singles):
+        if ref is not None:
+            vec[t, k : k + 1] = ref[...].reshape(1, model)
+    for a in range(4):
+        send_core(a)
+    for k, peer in enumerate((t2, t3, t1)):
+        send(vec_base + k, vec.at[t], vec.at[t], {"tensor": peer})
     own_u = local(4, w_up, wu.at[t])
     own_d = local(5, w_down, wd.at[t])
     after_x(0)
-    after_y(0)
+    send_x(2)
+    send_x(1, 3)
+    after_first(0)
     own_tok.wait()
-    own_vec.wait()
-    for k, peer in enumerate((t1, t2, t3)):
+    for k, peer in enumerate((t2, t3, t1)):
         arrived(tok_base + k, tok.at[peer])
-        arrived(vec_base + k, vec.at[peer])
-    for a in (1, 2):
-        send_x(a)
-        send_core(a)
+
+    def row(k):
+        return vec[t, k : k + 1, :]
 
     stores = []
 
@@ -215,7 +253,7 @@
             row = d * (4 * n_seq) + t * n_seq + s
             length = lengths[lax.rem(row, queries), lax.div(row, queries)]
             bias = vec[part, 1:2, :576]
-            z = (dot(x_s[s], rows_of(wq[part])) + bias).astype(bf16)
+            z = (dot_nt(x_s[s], rows_of(wq[part])) + bias).astype(bf16)
             qkv_s[part, s] = z
             pieces = []
             for h in range(3):
@@ -244,25 +282,26 @@
 
     own_q.wait()
     attention(t, True)
+    send_x(3)
     after_x(1)
-    after_y(1)
-    after_z(0)
     own_o.wait()
     project(t, True)
+    after_x(2)
+    for k, peer in enumerate((t2, t3, t1)):
+        arrived(vec_base + k, vec.at[peer])
     arrived(4, wq.at[t1])
+    arrived(9 + 4, wo.at[t1])
     attention(t1, False)
-    arrived(9 + 4, wo.at[t1])
+    after_first(1)
     project(t1, False)
-    send_x(3)
-    send_core(3)
-    after_z(1)
-    after_x(2)
-    after_y(2)
+    after_second(0)
+    after_x(3)
     attention(t2, False)
+    after_second(1)
     project(t2, False)
     after_core(0)
-    after_z(2)
     attention(t3, False)
+    after_first(2)
     after_core(1)
     project(t3, False)
     store(qkv_s, qkv_out)
@@ -278,17 +317,16 @@
     def _(i):
         s, r = lax.div(i, chunks), pl.multiple_of(lax.rem(i, chunks) * chunk, chunk)
         rows = pl.ds(r, chunk)
-        y = x_s[s, rows].astype(f32) + att_s[s, rows] + b_out[...]
+        y = x_s[s, rows].astype(f32) + att_s[s, rows] + row(2)
         n1, f1 = norm_forward(y)
         n1_s[s, rows] = n1
         f1_s[s, rows] = f1
-        hl_s[s, rows] = (n1 * gain_one[...] + bias_one[...]).astype(bf16)
+        hl_s[s, rows] = (n1 * row(3) + row(4)).astype(bf16)
 
     store(n1_s, n1_out)
     store(f1_s, f1_out)
     store(hl_s, hl_out)
-    after_x(3)
-    after_y(3)
+    after_first(3)
     own_u.wait()
     own_d.wait()
 
@@ -314,44 +352,63 @@
             else:
                 att_s[s, :, cols] += term
 
+    def store_ffn(part):
+        store(act_s.at[part], act_out.at[part])
+        store(gp_s.at[part], gp_out.at[part])
+        store(wu.at[part], wu_all.at[part])
+        store(wd.at[part], wd_all.at[part])
+
+    def store_ffn(part):
+        store(act_s.at[part], act_out.at[part])
+        store(gp_s.at[part], gp_out.at[part])
+        store(wu.at[part], wu_all.at[part])
+        store(wd.at[part], wd_all.at[part])
+
     ffn_up(t)
+    store_ffn(t)
     ffn_down(t, True)
-    after_z(3)
     arrived(2 * 9 + 4, wu.at[t1])
     ffn_up(t1)
     arrived(3 * 9 + 4, wd.at[t1])
+    store_ffn(t1)
     ffn_down(t1, False)
+    after_second(2)
     ffn_up(t2)
+    after_second(3)
+    store_ffn(t2)
     ffn_down(t2, False)
     after_core(2)
     ffn_up(t3)
     after_core(3)
-    store(act_s, act_out)
-    store(gp_s, gp_out)
-    store(wu, wu_all)
-    store(wd, wd_all)
+    store_ffn(t3)
     ffn_down(t3, False)
 
     @pl.loop(0, n_seq * chunks)
     def _(i):
         s, r = lax.div(i, chunks), pl.multiple_of(lax.rem(i, chunks) * chunk, chunk)
         rows = pl.ds(r, chunk)
-        y = n1_s[s, rows] * gain_one[...] + bias_one[...] + att_s[s, rows] + b_down[...]
+        y = n1_s[s, rows] * row(3) + row(4) + att_s[s, rows] + row(5)
         n2, f2 = norm_forward(y)
         n2_s[s, rows] = n2
         f2_s[s, rows] = f2
-        res_s[s, rows] = (n2 * gain_two[...] + bias_two[...]).astype(bf16)
+        res_s[s, rows] = (n2 * row(6) + row(7)).astype(bf16)
 
     store(n2_s, n2_out)
     store(f2_s, f2_out)
     store(res_s, res_out)
+    hot = picks(positions, d * (4 * n_seq) + t * n_seq, n_seq, queries).astype(bf16)
+    pk[t] = dot(hot, rows_of(res_s[:, :32])).astype(bf16)
+    for k, peer in enumerate((t2, t3, t1)):
+        send(pick_base + k, pk.at[t], pk.at[t], {"tensor": peer})
+    for k, peer in enumerate((t2, t3, t1)):
+        arrived(pick_base + k, pk.at[peer])
     for copy in stores:
         copy.wait()
     for copy in started:
         copy.wait_send()
 
 
-def forward(n_seq, seq, model, queries, lengths, tokens, w_qkv, w_out, w_up, w_down, vectors, rows):
+def forward(n_seq, seq, model, queries, tables, tokens, weights_in, vectors):
     def sds(shape, dtype):
         return jax.ShapeDtypeStruct(shape, dtype)
 
@@ -369,7 +426,7 @@
         ((n_seq, seq, 1), f32),
         ((n_seq, seq, model), bf16),
     ]
-    weights = [(4,) + w.shape for w in (w_qkv, w_out, w_up, w_down)]
+    weights = [(4,) + w.shape for w in weights_in]
     any_spec = pl.BlockSpec(memory_space=pl.ANY)
     vmem_spec = pl.BlockSpec(memory_space=pltpu.VMEM)
     scratch = [pltpu.VMEM((4, n_seq, seq, model // 4), bf16)]
@@ -377,24 +434,26 @@
     scratch += [pltpu.VMEM((n_seq, seq, model), f32)]
     scratch += [pltpu.VMEM(*a) for a in acts[4:]]
     scratch += [pltpu.VMEM(w, bf16) for w in weights]
-    scratch += [pltpu.VMEM((4,) + vectors.shape, f32)]
+    scratch += [pltpu.VMEM((4, 8, model), f32)]
     scratch += [
-        pltpu.SemaphoreType.DMA((42,)),
-        pltpu.SemaphoreType.DMA((42,)),
+        pltpu.SemaphoreType.DMA((45,)),
+        pltpu.SemaphoreType.DMA((45,)),
         pltpu.SemaphoreType.DMA((6,)),
-        pltpu.SemaphoreType.DMA((16,)),
+        pltpu.SemaphoreType.DMA((32,)),
     ]
     return pl.pallas_call(
         functools.partial(forward_kernel, (n_seq, seq, model, queries)),
-        out_shape=[sds(*a) for a in acts] + [sds(w, bf16) for w in weights],
-        in_specs=[pl.BlockSpec(memory_space=pltpu.SMEM)] + [any_spec] * 6 + [vmem_spec] * 6,
-        out_specs=[any_spec] * 16,
+        out_shape=[sds(*a) for a in acts]
+        + [sds(w, bf16) for w in weights]
+        + [sds((4, 8 * n_seq, model), bf16)],
+        in_specs=[pl.BlockSpec(memory_space=pltpu.SMEM)] * 2 + [any_spec] * 5 + [vmem_spec] * 8,
+        out_specs=[any_spec] * 16 + [vmem_spec],
         scratch_shapes=scratch,
         compiler_params=pltpu.CompilerParams(
             collective_id=0, has_side_effects=True, vmem_limit_bytes=60 * MIB
         ),
         name="layer_forward",
-    )(lengths, tokens, w_qkv, w_out, w_up, w_down, vectors, *rows)
+    )(*tables, tokens, *weights_in, *vectors)
 
 
 precise = lax.Precision.HIGHEST
@@ -415,44 +474,77 @@
     return factor * (scaled - mean_one - normed * mean_two)
 
 
+class Chain:
+    def __init__(self, bits, wait, send, base, held, buffers):
+        self.wait, self.send, self.base, self.held = wait, send, base, held
+        self.one_y, self.one_z, self.two = buffers
+        (self.y, self.y_peer), (self.z0, self.z0_peer) = bits["y"], bits["z0"]
+        self.width = self.two.shape[-1] // 2
+
+    def lanes(self, half):
+        return slice(half * self.width, (half + 1) * self.width)
+
+    def start(self):
+        src = self.held.at[:, :, 1 - self.y, :, self.lanes(0)]
+        self.send(self.base, src, self.one_y, self.y_peer)
+        src = self.held.at[:, 1 - self.z0, :, :, self.lanes(1)]
+        self.send(self.base + 1, src, self.one_z, self.z0_peer)
+
+    def middle(self):
+        low, high = self.lanes(0), self.lanes(1)
+        self.wait(self.base, self.one_y)
+        for a in range(2):
+            there = self.one_y[a, 1 - self.z0].astype(f32)
+            add = self.held[a, 1 - self.z0, self.y, :, low].astype(f32)
+            self.one_y[a, 1 - self.z0] = (there + add).astype(bf16)
+        src = self.one_y.at[:, 1 - self.z0]
+        self.send(self.base + 2, src, self.two.at[:, :, low], self.z0_peer)
+        self.wait(self.base + 1, self.one_z)
+        for a in range(2):
+            there = self.one_z[a, 1 - self.y].astype(f32)
+            add = self.held[a, self.z0, 1 - self.y, :, high].astype(f32)
+            self.one_z[a, 1 - self.y] = (there + add).astype(bf16)
+        src = self.one_z.at[:, 1 - self.y]
+        self.send(self.base + 3, src, self.two.at[:, :, high], self.y_peer)
+
+    def finish(self, a):
+        low, high = self.lanes(0), self.lanes(1)
+        first = self.one_y[a, self.z0].astype(f32) + self.held[a, self.z0, self.y, :, low].astype(f32)
+        second = self.one_z[a, self.y].astype(f32) + self.held[a, self.z0, self.y, :, high].astype(f32)
+        return self.two[a].astype(f32) + jnp.concatenate([first, second], 1)
+
+    def arrive(self):
+        self.wait(self.base + 2, self.two.at[:, :, self.lanes(0)])
+        self.wait(self.base + 3, self.two.at[:, :, self.lanes(1)])
+
+
 class Reduction:
-    def __init__(self, order, bits, remote, send, base, held, hops):
-        self.order, self.bits = order, bits
-        self.remote, self.send, self.base = remote, send, base
-        self.held, self.hops = held, hops
-        self.axes = [["x", "z1", "z0", "y"]]
-        for name in order:
-            self.axes.append([a for a in self.axes[-1] if a != name])
-
-    def buffer(self, hop):
-        return self.held if hop == 0 else self.hops[hop - 1]
-
-    def start(self, hop):
-        name = self.order[hop]
-        bit, peer = self.bits[name]
-        place = self.axes[hop].index(name)
-        src = self.buffer(hop).at[(slice(None),) * place + (1 - bit,)]
-        self.send(self.base + 2 + hop, src, self.buffer(hop + 1), peer)
-
-    def finish(self, hop, out=None):
-        name = self.order[hop]
-        bit, peer = self.bits[name]
-        place = self.axes[hop].index(name)
-        src, dst = self.buffer(hop), self.buffer(hop + 1)
-        self.remote(self.base + 2 + hop, dst, dst, peer).wait_recv()
-        left = len(self.axes[hop + 1])
-        if left == 0:
-            out[...] = src[(bit,)].astype(f32) + dst[...].astype(f32)
-            return
-
-        @pl.loop(0, 2**left)
-        def _(i):
-            index = []
-            for k in range(left):
-                index.append(lax.rem(lax.div(i, 2**k), 2))
-            index = tuple(index)
-            full = index[:place] + (bit,) + index[place:]
-            dst[index] = (dst[index].astype(f32) + src[full].astype(f32)).astype(bf16)
+    def __init__(self, bits, wait, send, base, buffers):
+        self.wait, self.send, self.base = wait, send, base
+        self.held, self.x_in, self.last = buffers[0], buffers[7], buffers[8]
+        (self.x, self.x_peer), (self.z1, self.z1_peer) = bits["x"], bits["z1"]
+        self.other = Chain(bits, wait, send, base + 2, self.held.at[1 - self.x], buffers[1:4])
+        self.mine = Chain(bits, wait, send, base + 6, self.held.at[self.x], buffers[4:7])
+
+    def pass_other(self):
+        self.other.arrive()
+        for a in range(2):
+            self.other.two[a] = self.other.finish(a).astype(bf16)
+        self.send(self.base + 10, self.other.two, self.x_in, self.x_peer)
+
+    def pass_mine(self):
+        self.mine.arrive()
+        self.wait(self.base + 10, self.x_in)
+        for k in range(2):
+            a = 1 - self.z1 if k == 0 else self.z1
+            total = self.mine.finish(a) + self.x_in[a].astype(f32)
+            self.mine.two[a] = total.astype(bf16)
+            if k == 0:
+                self.send(self.base + 11, self.mine.two.at[a], self.last, self.z1_peer)
+
+    def result(self):
+        self.wait(self.base + 11, self.last)
+        return self.mine.two[self.z1].astype(f32) + self.last[...].astype(f32)
 
 
 def backward_kernel(
@@ -460,13 +552,14 @@
     lengths,
     positions,
     targets,
+    query_weight,
     states,
     doc_ids,
-    query_weight,
     doc_table,
     w_query,
     gain_one,
     gain_two,
+    pk,
     vocab,
     out_grad,
     res,
@@ -492,17 +585,15 @@
     gwq_out,
     down_out,
     up_out,
-    qk_out,
-    vo_out,
+    qkv_out,
+    out_out,
     vec_out,
     big,
-    head,
-    pk,
+    shares,
     lg,
     ut,
     us,
     ur,
-    ss,
     sr,
     lb,
     dlog,
@@ -533,8 +624,8 @@
     gt,
     sums,
     sums_in,
-    qk_send,
-    vo_send,
+    own_states,
+    attn_send,
     parts,
     *rest,
 ):
@@ -589,18 +680,24 @@
         loads[name] = copy
 
     own = pl.multiple_of(t * n_seq, n_seq)
-    load("head", res.at[:, pl.ds(0, 32)], head)
     load("vocab", vocab, big)
     base = 0
-    st_all[d] = states[...]
+    share_width = model // docs
+    wide = states[...].astype(f32)
+    wide = jnp.concatenate([wide, jnp.zeros((queries, 128 - share_width), f32)], 1)
+    fill = own_states.shape[0] - queries
+    if fill:
+        wide = jnp.concatenate([wide, jnp.zeros((fill, 128), f32)], 0)
+    own_states[...] = wide.astype(bf16)
+    st_all[d] = own_states[...]
     for k, p in enumerate(doc_peers):
-        send(base + k, states, st_all.at[d], {"doc": p})
+        send(base + k, own_states, st_all.at[d], {"doc": p})
     states_base = base
     base += docs - 1
     load("og", out_grad.at[pl.ds(own, n_seq)], og)
     load("n2", n2_in, n2)
     load("f2", f2_in, f2)
-    order = (t3, t1, t2, t)
+    order = (t3, t2, t1, t)
     load("act0", act_in.at[order[0]], act.at[0])
     load("act1", act_in.at[order[1]], act.at[1])
     for i in range(2):
@@ -618,25 +715,9 @@
     load("ctx", ctx_in, ctx)
     load("lse", lse_in, lse)
     first_row = d * (4 * n_seq)
-    lane = lax.broadcasted_iota(jnp.int32, (own_rows, 32 * n_seq), 1)
-    line = lax.broadcasted_iota(jnp.int32, (own_rows, 32 * n_seq), 0)
-    spot = jnp.zeros((own_rows, 32 * n_seq), jnp.int32)
-    for b in range(own_rows):
-        query = lax.rem(first_row + t * n_seq + b // 8, queries)
-        spot = jnp.where(line == b, positions[query, b % 8] + 32 * (b // 8), spot)
-    hot = (lane == spot).astype(f32)
-    hot_low = hot.astype(bf16)
-    loads["head"].wait()
-    pk[t] = dot(hot_low, rows_of(head[...])).astype(bf16)
-    pick_base = base
-    for k, p in enumerate((t1, t2, t3)):
-        send(base + k, pk.at[t], pk.at[t], {"tensor": p})
-    base += 3
+    hot = picks(positions, first_row + t * n_seq, n_seq, queries)
     out_base = base
     base += 3
-    send(out_base, res, output.at[pl.ds(own, n_seq)], {"tensor": t2})
-    send(out_base + 1, res, output.at[pl.ds(own, n_seq)], {"tensor": t1})
-    load("out", res, output.at[pl.ds(own, n_seq)])
     all_rows = 4 * own_rows
     vocab_local = vocab.shape[0] * model
     chunk = model
@@ -646,8 +727,6 @@
         query = lax.rem(first_row + b // 8, queries)
         goal = jnp.where(tall == b, targets[query, b % 8], goal)
     goal = goal - t * vocab_local
-    for k, p in enumerate((t1, t2, t3)):
-        arrived(pick_base + k, pk.at[p])
     loads["vocab"].wait()
 
     @pl.loop(0, vocab_local // chunk)
@@ -681,50 +760,75 @@
         part = slice(j * own_rows, (j + 1) * own_rows)
         us[j, :, :model] = mean_row[part]
         us[j, :, model:] = goal_row[part]
-        ss[j] = stats[part]
     part_base = base
     base += 6
-    for k, p in enumerate((t1, t2, t3)):
-        send(part_base + k, ss.at[p], sr.at[t], {"tensor": p})
+    sr[t] = stats
+    for k, p in enumerate((t2, t3, t1)):
+        send(part_base + k, sr.at[t], sr.at[t], {"tensor": p})
+    for k, p in enumerate((t2, t3, t1)):
         send(part_base + 3 + k, us.at[p], ur.at[t], {"tensor": p})
-    sr[t] = ss[t]
     ur[t] = us[t]
-    for k, p in enumerate((t1, t2, t3)):
+    sums[0] = jnp.zeros(sums.shape[1:], f32)
+    for name in ("og", "n2", "f2"):
+        loads[name].wait()
+    step_rows = 96
+
+    def add_sum(row, value):
+        sums[0, 8 + row] += jnp.sum(value, 0, keepdims=True)
+
+    def second_norm(s, rows, flat, extra):
+        upstream = og[s, rows].astype(f32)
+        if extra is not None:
+            upstream = upstream + extra
+        normed = n2[flat]
+        back = norm_back_rows(upstream, normed, f2[flat], gain_two[...].reshape(1, model))
+        add_sum(4, upstream * normed)
+        add_sum(5, upstream)
+        add_sum(3, back)
+        dy[flat] = back
+        og[s, rows] = back.astype(bf16)
+
+    for s in range(n_seq):
+
+        @pl.loop(1, seq // step_rows)
+        def _(i):
+            start = pl.multiple_of(i * step_rows, step_rows)
+            second_norm(s, pl.ds(start, step_rows), pl.ds(s * seq + start, step_rows), None)
+
+    for k, p in enumerate((t2, t3, t1)):
         arrived(part_base + k, sr.at[p])
     highs = [sr[j, :, 0:1] for j in range(4)]
     top = jnp.maximum(jnp.maximum(highs[0], highs[1]), jnp.maximum(highs[2], highs[3]))
-    weights = [sr[j, :, 1:2] * jnp.exp(highs[j] - top) for j in range(4)]
-    whole = weights[0] + weights[1] + weights[2] + weights[3]
+    masses = [sr[j, :, 1:2] * jnp.exp(highs[j] - top) for j in range(4)]
+    whole = masses[0] + masses[1] + masses[2] + masses[3]
     picked_logit = sr[0, :, 2:3] + sr[1, :, 2:3] + sr[2, :, 2:3] + sr[3, :, 2:3]
     loglik = picked_logit - (top + jnp.log(whole))
     mine = first_row + t * n_seq
-    for s in range(n_seq):
+    for s in range(4 * n_seq):
         total = jnp.sum(loglik[8 * s : 8 * s + 8], 0, keepdims=True)
-        lb[mine + s] = jnp.broadcast_to(total, (1, 128))
-    like_base = base
-    base += 3
-    mine_ref = lb.at[pl.ds(mine, n_seq)]
-    for k, p in enumerate((t1, t2, t3)):
-        send(like_base + k, mine_ref, mine_ref, {"tensor": p})
-    for k, p in enumerate((t1, t2, t3)):
-        arrived(part_base + 3 + k, ur.at[p])
-    gap = jnp.zeros((own_rows, model), f32)
-    for j in range(4):
-        share = weights[j] / whole
-        gap = gap + ur[j, :, model:].astype(f32) - share * ur[j, :, :model].astype(f32)
-    diff[...] = gap
-    for k, p in enumerate((t1, t2, t3)):
-        arrived(like_base + k, lb.at[pl.ds(first_row + p * n_seq, n_seq)])
+        lb[first_row + s] = jnp.broadcast_to(total, (1, 128))
     group_base = base
     base += docs - 1
     group_ref = lb.at[pl.ds(first_row, 4 * n_seq)]
     for k, p in enumerate(doc_peers):
         send(group_base + k, group_ref, group_ref, {"doc": p})
+    for j in range(4):
+        share = jnp.broadcast_to(masses[j] / whole, (all_rows, 128))
+        shares[j] = share.reshape(4, own_rows, 128)
+    loads["hl"].wait()
+    x_t[...] = tmp[...].T
+    load("x", x_in, tmp)
+    for k, p in enumerate((t2, t3, t1)):
+        arrived(part_base + 3 + k, ur.at[p])
+    gap = jnp.zeros((own_rows, model), f32)
+    for j in range(4):
+        share = shares[j, t][:, 0:1]
+        gap = gap + ur[j, :, model:].astype(f32) - share * ur[j, :, :model].astype(f32)
+    diff[...] = gap
     for k in range(docs - 1):
         source = lax.rem(d + docs - 1 - k, docs)
         arrived(states_base + k, st_all.at[source])
-    share_width = model // docs
-    emb = jnp.zeros((states.shape[0], 128), f32)
+    emb = jnp.zeros((own_states.shape[0], 128), f32)
     for j in range(docs):
         emb = emb + dot(st_all[j, :, :share_width], w_query[j])
     emb = emb[:queries]
@@ -746,13 +850,17 @@
         return largest + jnp.log(total)
 
     prior_lse, joint_lse = log_sum(prior), log_sum(joint)
+    tall = lax.broadcasted_iota(jnp.int32, (queries, 1), 0)
+    weight = jnp.zeros((queries, 1), f32)
+    for k in range(queries):
+        weight = jnp.where(tall == k, query_weight[k], weight)
     nll_out[...] = jnp.broadcast_to(prior_lse - joint_lse, (queries, 128))
     spread_docs = jnp.zeros((queries, table), f32)
     for k in range(slots):
         post = jnp.exp(joint[k] - joint_lse)
         before = jnp.exp(prior[k] - prior_lse)
-        spread_docs = spread_docs + hot_docs[k] * (query_weight[...] * (before - post))
-        value = -query_weight[...] * post
+        spread_docs = spread_docs + hot_docs[k] * (weight * (before - post))
+        value = -weight * post
         dlog[k * queries : (k + 1) * queries] = jnp.broadcast_to(value, (queries, 128)).reshape(
             queries, 1, 128
         )
@@ -766,68 +874,39 @@
         scattered.append(
             dot_f32(hot[8 * s : 8 * s + 8, 32 * s : 32 * s + 32], rows, ((0,), (0,)))
         )
-    sums[0] = jnp.zeros(sums.shape[1:], f32)
-    for name in ("og", "n2", "f2"):
-        loads[name].wait()
-    step_rows = 96
-
-    def add_sum(row, value):
-        sums[0, 4, row : row + 1] += jnp.sum(value, 0, keepdims=True)
-
-    def second_norm(s, rows, flat, extra):
-        upstream = og[s, rows].astype(f32)
-        if extra is not None:
-            upstream = upstream + extra
-        normed = n2[flat]
-        back = norm_back_rows(upstream, normed, f2[flat], gain_two[...])
-        add_sum(4, upstream * normed)
-        add_sum(5, upstream)
-        add_sum(3, back)
-        dy[flat] = back
-        og[s, rows] = back.astype(bf16)
-
+    mine_out = output.at[pl.ds(own, n_seq)]
+    send(out_base, res, mine_out, {"tensor": t2})
+    send(out_base + 1, res, mine_out, {"tensor": t1})
     for s in range(n_seq):
         extra = jnp.concatenate([scattered[s], jnp.zeros((step_rows - 32, model), f32)], 0)
         second_norm(s, pl.ds(0, step_rows), pl.ds(s * seq, step_rows), extra)
 
-        @pl.loop(1, seq // step_rows)
-        def _(i):
-            start = pl.multiple_of(i * step_rows, step_rows)
-            second_norm(s, pl.ds(start, step_rows), pl.ds(s * seq + start, step_rows), None)
-
     d_t[...] = rows_of(og[...]).T
-    orders = (
-        ("y", "z0", "x", "z1"),
-        ("z0", "y", "x", "z1"),
-        ("y", "z0", "x", "z1"),
-        ("z0", "y", "x", "z1"),
-    )
     reds = []
-    for k, names in enumerate(orders):
-        bufs = red_bufs[5 * k : 5 * k + 5]
-        reds.append(Reduction(names, bits, remote, send, base, bufs[0], bufs[1:]))
-        base += 6
-    down, up, qk, vo = reds
+    for k in range(3):
+        reds.append(Reduction(bits, arrived, send, base, red_bufs[9 * k : 9 * k + 9]))
+        base += 12
+    down, up, attn = reds
     block_shape = (2, 2, 2, model // docs)
 
     def emit(red, i, sending, shard, lanes, value):
         value = value.reshape(block_shape + (value.shape[-1],))
         which = lax.div(shard, 2)
-        if i < 2:
+        if i % 2 == 0:
             sending[which, :, :, :, :, lanes] = value.astype(bf16)
         else:
             total = value + red.held[which, :, :, :, :, lanes].astype(f32)
             red.held[which, :, :, :, :, lanes] = total.astype(bf16)
 
     def before_block(red, i, shard):
-        if i >= 2:
+        if i % 2 == 1:
             which = lax.div(shard, 2)
-            arrived(red.base + (i - 2), red.held.at[which])
+            arrived(red.base + i // 2, red.held.at[which])
 
     def after_block(red, i, sending, shard):
-        if i < 2:
+        if i % 2 == 0:
             which = lax.div(shard, 2)
-            send(red.base + i, sending.at[which], red.held.at[which], {"tensor": t1})
+            send(red.base + i // 2, sending.at[which], red.held.at[which], {"tensor": t1})
 
     down_send, up_send = big.at[0:2], big.at[2:4]
     tiles = model // 256
@@ -843,10 +922,9 @@
         if i + 2 < 4:
             load("act%d" % (i + 2), act_in.at[order[i + 2]], act.at[i % 2])
         after_block(down, i, down_send, shard)
-    down.start(0)
-    loads["hl"].wait()
-    x_t[...] = tmp[...].T
-    load("x", x_in, tmp)
+        if i == 1:
+            down.other.start()
+    down.mine.start()
     for i, shard in enumerate(order):
         for name in ("gp", "wd", "wu"):
             loads["%s%d" % (name, i)].wait()
@@ -858,7 +936,7 @@
             value = dot_nt(rows_of(og[...]), wd[i % 2, lanes]) * gp[i % 2, :, lanes].astype(f32)
             low = value.astype(bf16)
             d_up[:, lanes] = low
-            sums[0, shard, 0:1, lanes] = jnp.sum(low.astype(f32), 0, keepdims=True)
+            sums[0, shard, :, lanes] = jnp.sum(low.astype(f32), 0, keepdims=True)
 
         if i + 2 < 4:
             load("gp%d" % (i + 2), gp_in.at[order[i + 2]], gp.at[i % 2])
@@ -877,7 +955,13 @@
         if i + 2 < 4:
             load("wu%d" % (i + 2), wu_in.at[order[i + 2]], wu.at[i % 2])
         after_block(up, i, up_send, shard)
-    up.start(0)
+        if i == 1:
+            down.other.middle()
+            up.other.start()
+        if i == 2:
+            down.mine.middle()
+    up.mine.start()
+    down.pass_other()
     arrived(out_base, output.at[pl.ds(t2 * n_seq, n_seq)])
     passed = output.at[pl.ds(t2 * n_seq, n_seq)]
     send(out_base + 2, passed, passed, {"tensor": t1})
@@ -890,7 +974,7 @@
         s, start = lax.div(i, seq // step_rows), lax.rem(i, seq // step_rows) * step_rows
         upstream = dy[flat] + n2[flat]
         normed = n1[flat]
-        back = norm_back_rows(upstream, normed, f1[flat], gain_one[...])
+        back = norm_back_rows(upstream, normed, f1[flat], gain_one[...].reshape(1, model))
         add_sum(1, upstream * normed)
         add_sum(2, upstream)
         add_sum(0, back)
@@ -898,10 +982,22 @@
         og[s, pl.ds(pl.multiple_of(start, step_rows), step_rows)] = back.astype(bf16)
 
     d_t[...] = rows_of(og[...]).T
+    up.other.middle()
     loads["x"].wait()
     x_t[...] = tmp[...].T
     for name in ("wo", "ctx", "lse"):
         loads[name].wait()
+    vec_base = base
+    vec_peers = [{"tensor": t1}, bits["y"][1], bits["z0"][1], bits["x"][1], bits["z1"][1]]
+    base += len(vec_peers)
+
+    def vec_start(k):
+        send(vec_base + k, sums.at[k], sums_in.at[k], vec_peers[k])
+
+    def vec_finish(k):
+        arrived(vec_base + k, sums_in.at[k])
+        sums[k + 1] = sums[k] + sums_in[k]
+
     key_index = lax.broadcasted_iota(jnp.int32, (seq, seq), 0)
     for i, shard in enumerate(order):
         loads["qkv%d" % i].wait()
@@ -938,19 +1034,31 @@
         total = parts[0]
         for s in range(1, n_seq):
             total = total + parts[s]
-        sums[0, shard, 1:2, : 3 * 192] = total
-        before_block(qk, i, shard)
-        emit(qk, i, qk_send, shard, slice(None), dot(x_t[...], dqkv[:, :384]))
-        after_block(qk, i, qk_send, shard)
-        before_block(vo, i, shard)
-        value = jnp.concatenate([dot(x_t[...], dqkv[:, 384:]), dot(d_t[...], ctx[shard])], 1)
-        emit(vo, i, vo_send, shard, slice(None), value)
-        after_block(vo, i, vo_send, shard)
+        sums[0, 4 + shard, :, : 3 * 192] = total
+        before_block(attn, i, shard)
+        value = jnp.concatenate([dot(x_t[...], dqkv[...]), dot(d_t[...], ctx[shard])], 1)
+        emit(attn, i, attn_send, shard, slice(None), value)
+        after_block(attn, i, attn_send, shard)
+        if i == 0:
+            down.pass_mine()
+            up.mine.middle()
+        if i == 1:
+            attn.other.start()
+            up.pass_other()
+        if i == 2:
+            down_out[...] = down.result()
+            up.pass_mine()
+            attn.other.middle()
+        if i == 3:
+            attn.mine.start()
+            vec_start(0)
+            up_out[...] = up.result()
+            attn.pass_other()
 
         @pl.loop(0, tiles)
         def _(n):
             lanes = pl.ds(pl.multiple_of(n * 256, 256), 256)
-            value = dot_nt(dqkv[...], wq[i % 2, lanes])
+            value = dot(dqkv[...], wq[i % 2, :, lanes])
             if i == 0:
                 n1[:, lanes] = value
             else:
@@ -962,70 +1070,34 @@
 
     for j in range(4):
         lanes = slice(j * 192, j * 192 + 192)
-        dxb[j] = (n1[:, lanes] + dy[:, lanes]).astype(bf16)
+        block = (n1[:, lanes] + dy[:, lanes]).astype(bf16)
+        dxb[j] = jnp.concatenate([block[k * seq : (k + 1) * seq] for k in range(n_seq)], 1)
     tok_base = base
     base += 3
     for k, p in enumerate((t2, t3, t1)):
         send(tok_base + k, dxb.at[p], gt.at[t], {"tensor": p})
     gt[t] = dxb[t]
-    vec_base = base
-    vec_peers = [{"tensor": t1}, bits["y"][1], bits["z0"][1], bits["x"][1], bits["z1"][1]]
-    base += len(vec_peers)
-
-    def vec_start(k):
-        send(vec_base + k, sums.at[k], sums_in.at[k], vec_peers[k])
-
-    def vec_finish(k):
-        arrived(vec_base + k, sums_in.at[k])
-        sums[k + 1] = sums[k] + sums_in[k]
-
-    qk.start(0)
-    vo.start(0)
-    vec_start(0)
     vec_finish(0)
     vec_start(1)
-    down.finish(0)
-    down.start(1)
-    up.finish(0)
-    up.start(1)
+    attn.mine.middle()
     vec_finish(1)
     vec_start(2)
-    down.finish(1)
-    down.start(2)
-    up.finish(1)
-    up.start(2)
     vec_finish(2)
     vec_start(3)
-    qk.finish(0)
-    qk.start(1)
-    vo.finish(0)
-    vo.start(1)
-    down.finish(2)
-    down.start(3)
-    up.finish(2)
-    up.start(3)
+    attn.pass_mine()
     vec_finish(3)
     vec_start(4)
     for k, p in enumerate((t2, t3, t1)):
         arrived(tok_base + k, gt.at[p])
     load("gt", gt, gt_out)
-    qk.finish(1)
-    qk.start(2)
-    vo.finish(1)
-    vo.start(2)
-    down.finish(3, down_out)
-    up.finish(3, up_out)
     vec_finish(4)
     vec_out[...] = sums[5]
-    qk.finish(2)
-    qk.start(3)
-    vo.finish(2)
-    vo.start(3)
-    qk.finish(3, qk_out)
-    vo.finish(3, vo_out)
+    total = attn.result()
+    for k in range(3):
+        qkv_out[k] = total[:, k * 192 : k * 192 + 192]
+    out_out[...] = total[:, 576:].T
     arrived(out_base + 1, output.at[pl.ds(t1 * n_seq, n_seq)])
     arrived(out_base + 2, output.at[pl.ds(t3 * n_seq, n_seq)])
-    loads["out"].wait()
     loads["gt"].wait()
     for copy in started:
         copy.wait_send()
@@ -1041,13 +1113,14 @@
     out_grad,
     kept,
 ):
-    lengths, positions, targets, states, doc_ids, query_weight, doc_table, w_query = tables[:8]
+    states, doc_ids, doc_table, w_query = tables[4:8]
     queries, slots = doc_ids.shape
     table = doc_table.shape[0]
     m_rows = n_seq * seq
     own_rows = 8 * n_seq
     all_rows = 4 * own_rows
     share = model // docs
+    states_rows = -(-queries // 16) * 16
     (res, x, qkv, lse, ctx, n1, f1, hl, act, gp, n2, f2, wq, wo, wu, wd) = kept
 
     def flat(a):
@@ -1082,14 +1155,14 @@
     outs = [
         sds((4 * n_seq, seq, model), bf16),
         sds((queries, 128), f32),
-        sds((4, m_rows, model // 4), bf16),
+        sds((4, seq, n_seq * 192), bf16),
         sds((queries, share), f32),
         sds((share, 128), f32),
         sds((share, model), f32),
         sds((share, model), f32),
-        sds((share, 384), f32),
-        sds((share, 384), f32),
-        sds((5, 8, model), f32),
+        sds((3, share, 192), f32),
+        sds((192, share), f32),
+        sds((14, 1, model), f32),
     ]
     out_specs = [any_spec, vmem_spec, any_spec] + [vmem_spec] * 7
 
@@ -1098,17 +1171,15 @@
 
     scratch = [
         vm(vocab.shape, bf16),
-        vm((n_seq, 32, model), bf16),
-        vm((4, own_rows, model), bf16),
+        vm((4, 4, own_rows, 128), f32),
         vm((all_rows, vocab.shape[0] * model), f32),
         vm((2 * all_rows, model), f32),
         vm((4, own_rows, 2 * model), bf16),
         vm((4, own_rows, 2 * model), bf16),
-        vm((4, own_rows, 128), f32),
-        vm((4, own_rows, 128), f32),
+        vm((4, all_rows, 128), f32),
         vm((docs * 4 * n_seq, 1, 128), f32),
         vm((docs * 4 * n_seq, 1, 128), f32),
-        vm((docs,) + states.shape, bf16),
+        vm((docs, states_rows, 128), bf16),
         vm((own_rows, model), f32),
         vm((n_seq, seq, model), bf16),
         vm((m_rows, model), bf16),
@@ -1119,7 +1190,7 @@
         vm((m_rows, model), f32),
         vm((2, m_rows, model), bf16),
         vm((2, m_rows, model), bf16),
-        vm((2, model, 576), bf16),
+        vm((2, 576, model), bf16),
         vm((4, 192, model), bf16),
         vm((2, model, model), bf16),
         vm((2, model, model), bf16),
@@ -1131,18 +1202,23 @@
         vm((m_rows, model), bf16),
         vm((m_rows, 192), bf16),
         vm((m_rows, 576), bf16),
-        vm((4, m_rows, 192), bf16),
-        vm((4, m_rows, 192), bf16),
-        vm((6, 5, 8, model), f32),
-        vm((5, 5, 8, model), f32),
-        vm((2, 2, 2, 2, share, 384), bf16),
-        vm((2, 2, 2, 2, share, 384), bf16),
+        vm((4, seq, n_seq * 192), bf16),
+        vm((4, seq, n_seq * 192), bf16),
+        vm((6, 14, 1, model), f32),
+        vm((5, 14, 1, model), f32),
+        vm((states_rows, 128), bf16),
+        vm((2, 2, 2, 2, share, model), bf16),
         vm((n_seq, 1, 576), f32),
     ]
-    for width in (model, model, 384, 384):
-        for left in (4, 3, 2, 1, 0):
-            scratch.append(vm((2,) * left + (share, width), bf16))
-    copies = 2 * (docs - 1) + 3 + 3 + 6 + 3 + 6 * 4 + 3 + 5
+    for _ in range(3):
+        scratch.append(vm((2, 2, 2, 2, share, model), bf16))
+        for _ in range(2):
+            scratch.append(vm((2, 2, share, model // 2), bf16))
+            scratch.append(vm((2, 2, share, model // 2), bf16))
+            scratch.append(vm((2, share, model), bf16))
+        scratch.append(vm((2, share, model), bf16))
+        scratch.append(vm((share, model), bf16))
+    copies = 2 * (docs - 1) + 3 + 6 + 12 * 3 + 3 + 5
     scratch += [
         pltpu.SemaphoreType.DMA((copies,)),
         pltpu.SemaphoreType.DMA((copies,)),
@@ -1151,7 +1227,7 @@
     return pl.pallas_call(
         functools.partial(backward_kernel, (n_seq, seq, model, queries, slots, table, docs)),
         out_shape=outs,
-        in_specs=[smem_spec] * 3 + [vmem_spec] * 7 + [any_spec] * 18,
+        in_specs=[smem_spec] * 4 + [vmem_spec] * 7 + [any_spec] * 18,
         out_specs=out_specs,
         scratch_shapes=scratch,
         compiler_params=pltpu.CompilerParams(
@@ -1159,6 +1235,118 @@
         ),
         name="layer_backward",
     )(*tables, vocab, out_grad, *kept)
+
+
+def finish_kernel(cfg, *refs):
+    n_seq, docs = cfg
+    output, res, gs, gwq, down, up, qkv, out, gt_in, nll_in, sums_in = refs[:11]
+    output_out, nll_out, tokens_out, gs_out, qkv_out, b_qv_out, out_out = refs[11:18]
+    b_out_out, gain_one_out, bias_one_out, up_out, b_up_out, down_out = refs[18:24]
+    b_down_out, gain_two_out, bias_two_out, gwq_out, gt, nll, sums, whole = refs[24:32]
+    held, sem, sem_out = refs[32:-2], refs[-2], refs[-1]
+    d = lax.axis_index("doc")
+    t = lax.axis_index("tensor")
+    pairs = [(gt_in, gt), (sums_in, sums), (nll_in, nll), (res, whole.at[pl.ds(t * n_seq, n_seq)])]
+    for k in range(1, 4):
+        part = pl.ds(lax.rem(t + k, 4) * n_seq, n_seq)
+        pairs.append((output.at[part], whole.at[part]))
+    passed = ((down, down_out), (up, up_out), (qkv, qkv_out), (out, out_out), (gs, gs_out))
+    passed += ((gwq, gwq_out),)
+    pairs += [(pair[0], buf) for pair, buf in zip(passed, held)]
+    copies = [pltpu.make_async_copy(*pair, sem.at[k]) for k, pair in enumerate(pairs)]
+    for copy in copies:
+        copy.start()
+    ends = []
+
+    def forward_to(number, src, dst):
+        copies[number].wait()
+        copy = pltpu.make_async_copy(src, dst, sem_out.at[len(ends)])
+        copy.start()
+        ends.append(copy)
+
+    for k in range(4):
+        part = pl.ds(lax.rem(t + k, 4) * n_seq, n_seq)
+        forward_to(3 + k, whole.at[part], output_out.at[part])
+    for k, (pair, buf) in enumerate(zip(passed, held)):
+        forward_to(7 + k, buf, pair[1])
+    part_width = gt.shape[-1] // n_seq
+    copies[0].wait()
+    for j in range(4):
+        for s in range(n_seq):
+            lanes = slice(s * part_width, (s + 1) * part_width)
+            tokens_out[j * n_seq + s] = gt[j, :, lanes].astype(f32)
+    copies[1].wait()
+    copies[2].wait()
+    nll_out[...] = nll[:, 0]
+    heads = sums[4 + t]
+    b_qv_out[0:1] = heads[:, :part_width]
+    b_qv_out[1:2] = heads[:, 2 * part_width : 3 * part_width]
+    b_up_out[...] = sums[t].reshape(b_up_out.shape)
+    width = b_out_out.shape[0]
+    singles = (b_out_out, gain_one_out, bias_one_out, b_down_out, gain_two_out, bias_two_out)
+    for k, ref in enumerate(singles):
+        row = sums[8 + k]
+        own = jnp.zeros((1, width), f32)
+        for j in range(docs):
+            own = own + jnp.where(d == j, row[:, j * width : (j + 1) * width], 0.0)
+        ref[...] = own.reshape(width)
+    for copy in ends:
+        copy.wait()
+
+
+def finish(n_seq, docs, parts):
+    output, res, gt, nll, gs, gwq, down, up, qkv, out, sums = parts
+    model = sums.shape[-1]
+    share = model // docs
+    part_width = gt.shape[-1] // n_seq
+
+    def sds(*shape):
+        return jax.ShapeDtypeStruct(shape, f32)
+
+    outs = [
+        jax.ShapeDtypeStruct(output.shape, bf16),
+        sds(nll.shape[0]),
+        sds(4 * n_seq, gt.shape[1], part_width),
+        sds(*gs.shape),
+        sds(*qkv.shape),
+        sds(2, part_width),
+        sds(*out.shape),
+        sds(share),
+        sds(share),
+        sds(share),
+        sds(*up.shape),
+        sds(model),
+        sds(*down.shape),
+        sds(share),
+        sds(share),
+        sds(share),
+        sds(*gwq.shape),
+    ]
+    any_spec = pl.BlockSpec(memory_space=pltpu.HBM)
+    vmem_spec = pl.BlockSpec(memory_space=pltpu.VMEM)
+    out_specs = [vmem_spec] * 17
+    for k in (0, 3, 4, 6, 10, 12, 16):
+        out_specs[k] = any_spec
+    results = pl.pallas_call(
+        functools.partial(finish_kernel, (n_seq, docs)),
+        out_shape=outs,
+        in_specs=[any_spec] * 11,
+        out_specs=out_specs,
+        scratch_shapes=[
+            pltpu.VMEM(gt.shape, gt.dtype),
+            pltpu.VMEM(nll.shape, nll.dtype),
+            pltpu.VMEM(sums.shape, sums.dtype),
+            pltpu.VMEM(output.shape, output.dtype),
+            *(pltpu.VMEM(a.shape, a.dtype) for a in (down, up, qkv, out, gs, gwq)),
+            pltpu.SemaphoreType.DMA((13,)),
+            pltpu.SemaphoreType.DMA((10,)),
+        ],
+        compiler_params=pltpu.CompilerParams(vmem_limit_bytes=62 * MIB),
+        name="layer_results",
+    )(output, res, gs, gwq, down, up, qkv, out, gt, nll, sums)
+    results = list(results)
+    results[12] = results[12].T
+    return results
 
 
 def joined(array, axis, combine):
@@ -1237,67 +1425,47 @@
     row_count = n_seq * seq_length
     queries = lengths.shape[0]
     t = lax.axis_index("tensor")
-    packed_qkv = jnp.concatenate([w_qkv[0], w_qkv[1], w_qkv[2]], 1).reshape(4, 192, 576)
     hidden = w_up.shape[1]
-    vectors = jnp.zeros((8, hidden), f32)
-    vectors = vectors.at[0].set(b_up).at[1, :192].set(b_qv[0]).at[1, 384:576].set(b_qv[1])
-    rows = [v[None, :] for v in (b_out, ln1_gain, ln1_bias, b_down, ln2_gain, ln2_bias)]
-    (x, qkv, lse, ctx, n1, f1, hl, act, gp, n2, f2, res, wq, wo, wu, wd) = forward(
+    vectors = (b_qv, b_up, b_out, ln1_gain, ln1_bias, b_down, ln2_gain, ln2_bias)
+    quarter = model_width // 4
+    weights_in = (
+        w_qkv.transpose(0, 2, 1).reshape(4, 3 * quarter // 4, model_width),
+        w_out.reshape(4, quarter // 4, model_width),
+        w_up.reshape(4, quarter, hidden),
+        w_down.reshape(4, hidden // 4, model_width),
+    )
+    (x, qkv, lse, ctx, n1, f1, hl, act, gp, n2, f2, res, wq, wo, wu, wd, pk) = forward(
         n_seq,
         seq_length,
         model_width,
         queries,
-        lengths,
+        (lengths, positions),
         tokens,
-        packed_qkv,
-        w_out.reshape(4, 48, model_width),
-        w_up.reshape(4, 192, hidden),
-        w_down.reshape(4, 192, model_width),
+        weights_in,
         vectors,
-        rows,
     )
     docs = lax.axis_size("doc")
     if docs == 8 and n_seq == 2:
         share = model_width // docs
-        states_rows = max(16, -(-queries // 16) * 16)
-        states = jnp.zeros((states_rows, 128), bf16).at[:queries, :share].set(query_states)
         tables = (
             lengths,
             positions,
             targets,
-            states,
+            query_weight,
+            query_states,
             doc_ids,
-            query_weight[:, None],
             doc_table,
             w_query.reshape(docs, share, w_query.shape[1]),
-            rows[1],
-            rows[4],
+            ln1_gain,
+            ln2_gain,
+            pk,
         )
         kept = (res, x, qkv, lse, ctx, n1, f1, hl, act, gp, n2, f2, wq, wo, wu, wd)
-        (output, nll, gt, gs, gwq, g_down, g_up, g_qk, g_vo, sums) = backward(
+        (output, nll, gt, gs, gwq, g_down, g_up, g_qkv, g_out, sums) = backward(
             n_seq, seq_length, model_width, docs, tables, vocab_table, out_grad, kept
         )
-        d = lax.axis_index("doc")
-        six = lax.dynamic_slice_in_dim(sums[4, :6], d * share, share, 1)
-        mine = lax.dynamic_index_in_dim(sums[:4], t, 0, keepdims=False)
-        return (
-            output,
-            nll[:, 0],
-            gt.reshape(sequences, seq_length, part_width).astype(f32),
-            gs,
-            jnp.stack([g_qk[:, :192], g_qk[:, 192:], g_vo[:, :192]]),
-            jnp.stack([mine[1, :192], mine[1, 384:576]]),
-            g_vo[:, 192:].T,
-            six[0],
-            six[1],
-            six[2],
-            g_up,
-            mine[0],
-            g_down.T,
-            six[3],
-            six[4],
-            six[5],
-            gwq,
+        return tuple(
+            finish(n_seq, docs, (output, res, gt, nll, gs, gwq, g_down, g_up, g_qkv, g_out, sums))
         )
     output = lax.all_gather(res, "tensor", axis=0, tiled=True)
     row_index = lax.axis_index("doc") * sequences + jnp.arange(sequences, dtype=jnp.int32)
@@ -1364,7 +1532,7 @@
     d_low = dy2.astype(bf16)
     act, gp = act.reshape(4, row_count, hidden), gp.reshape(4, row_count, hidden)
     wu, wd = wu.reshape(4, model_width, hidden), wd.reshape(4, hidden, model_width)
-    wq, wo = wq.reshape(4, model_width, 576), wo.reshape(4, 192, model_width)
+    wq, wo = wq.reshape(4, 576, model_width).transpose(0, 2, 1), wo.reshape(4, 192, model_width)
     qkv, ctx = qkv.reshape(4, n_seq, seq_length, 576), ctx.reshape(4, row_count, 192)
     g_down = jnp.einsum("tmf,md->tfd", act, d_low, preferred_element_type=f32)
     d_act = jnp.einsum("md,tfd->tmf", d_low, wd, preferred_element_type=f32)

time: 268 us -> 192 us (0.72)
  Pallas kernels: 240 us -> 191 us
  local copies, waits for them, and re-layouts: 21.7 us -> 0 us
  other arithmetic: 4.24 us -> 0 us
    pallas_call x1, Pallas kernels: 153 us -> 112 us  [backward(): pl.pallas_call(functools.partial(backward_kernel, (n_seq, seq, model, que...]
    pallas_call x1, Pallas kernels: 86.7 us -> 74 us  [forward(): pl.pallas_call(functools.partial(forward_kernel, (n_seq, seq, model, quer...]
    unnamed x44 -> x0, local copies, waits for them, and re-layouts: 6.45 us -> none
    slice x10 -> x0, local copies, waits for them, and re-layouts: 5.93 us -> none  [the longest x2 1.37 us: shards(): w_qkv[0]]
    pallas_call x0 -> x1, Pallas kernels: none -> 5.23 us  [finish(): pl.pallas_call(functools.partial(finish_kernel, (n_seq, docs)), out_shape...]
    broadcast_in_dim x7 -> x0, local copies, waits for them, and re-layouts: 4.16 us -> none  [the longest x6 3.49 us: shards(): v[None, :]]
where the time goes in v3:
time: 192 us
  Pallas kernels  191 us (99%)
    pallas_call x1, Pallas kernels, backward(): pl.pallas_call(functools.partial(backward_kernel, (n_seq, seq, model, que...  112 us
    pallas_call x1, Pallas kernels, forward(): pl.pallas_call(functools.partial(forward_kernel, (n_seq, seq, model, quer...  74 us
    pallas_call x1, Pallas kernels, finish(): pl.pallas_call(functools.partial(finish_kernel, (n_seq, docs)), out_shape...  5.23 us

profile of v3, /device:TPU:0, one launch (start us, length us, event | category | flops | bytes accessed | tf_op | source)
XLA Modules:
  0.0 191.6 jit_solution(12389693634856852842)
XLA Ops:
  0.7 74.0 %layer_forward.1 = (bf16[2,288,768]{2,1,0:T(8,128)(2,1)}, bf16[4,2,288,576]{3,2,1,0:T(8,128)(2,1)}, f32[4,2,3,1,288]{4,3,2,1,0:T(1,128)}, bf16[4,2,288,192]{3,2,...) custom-call(s32[8,8]{1,0:T(8,128)} %lengths.3, ...), custom_call_target="tpu_custom_call" | custom-call | tf_op jit(solution)/shard_map/layer_forward/pallas_call | solution.py:444
  74.6 111.6 %layer_backward.1 = (bf16[8,288,768]{2,1,0:T(8,128)(2,1)}, f32[8,128]{1,0:T(8,128)}, bf16[4,288,384]{2,1,0:T(8,128)(2,1)}, f32[8,96]{1,0:T(8,128)}, f32[96,128]{...) custom-call(s32[8,8]{1,0:T(8,128)} %lengths.3, ...), custom_call_target="tpu_custom_call" | custom-call | tf_op jit(solution)/shard_map/layer_backward/pallas_call | solution.py:1227
  186.2 5.2 %layer_results.1 = (bf16[8,288,768]{2,1,0:T(8,128)(2,1)}, f32[8]{0:T(128)}, f32[8,288,192]{2,1,0:T(8,128)}, f32[8,96]{1,0:T(8,128)}, f32[3,96,192]{2,1,0:T(8,128...) custom-call(bf16[8,288,768]{2,1,0:T(8,128)(2,1)} %get-tuple-element., ...), custom_call_target="tpu_custom_call" | custom-call | tf_op jit(solution)/shard_map/layer_results/pallas_call | solution.py:1330

commit v4 on v3

--- a/solution.py
+++ b/solution.py
@@ -84,6 +84,8 @@
     wu_all,
     wd_all,
     pk,
+    raw,
+    packed,
     tok,
     x_s,
     qkv_s,
@@ -123,6 +125,7 @@
         copy.start()
         return copy
 
+    own_tok = local(1, tokens, raw)
     own_q = local(0, w_qkv, wq.at[t])
     barrier = pltpu.get_barrier_semaphore()
     peers = ({"tensor": t1}, {"tensor": t2}, {"tensor": t3}, {"doc": d1}, {"doc": d2})
@@ -142,7 +145,6 @@
 
     gathered = (wq, wo, wu, wd)
     inputs = (w_qkv, w_out, w_up, w_down)
-    outputs = (wq_all, wo_all, wu_all, wd_all)
     started = []
 
     def send(number, src, dst, peer):
@@ -150,65 +152,78 @@
         copy.start()
         started.append(copy)
 
-    hops = [(({"doc": d1}, q1), ({"doc": d2}, q2))] * 4
-    hops[1] = hops[3] = hops[0][::-1]
-
-    def send_x(a, pieces=1):
-        count = inputs[a].shape[1] // pieces
-        for k in range(pieces):
-            rows = pl.ds(k * count, count)
-            src, dst = inputs[a].at[q, rows], gathered[a].at[t, q, rows]
-            remote(9 * a, src, dst, {"tensor": t2}).start()
-        started.append(remote(9 * a, inputs[a].at[q], gathered[a].at[t, q], {"tensor": t2}))
-
-    def send_core(a):
-        send(9 * a + 4, inputs[a], gathered[a].at[t], {"tensor": t1})
+    half = model // 8
+    sources = ((0, None), (1, None), (2, 0), (2, 1), (3, 0), (3, 1))
+    hops = (({"doc": d1}, q1), ({"doc": d2}, q2))
+
+    def rows_view(ref, k, begin=0, count=None):
+        if k is None and count is None:
+            return ref
+        begin = begin + (0 if k is None else k * half)
+        return ref.at[pl.ds(begin, half if count is None else count)]
+
+    def piece(a, part, shard=None):
+        which, k = sources[a]
+        return rows_view(gathered[which].at[t2 if shard is None else shard, part], k)
+
+    def send_x(a, pieces):
+        which, k = sources[a]
+        src, dst = inputs[which].at[q], gathered[which].at[t, q]
+        count = (src.shape[0] if k is None else half) // pieces
+        for n in range(pieces):
+            part = rows_view(src, k, n * count, count)
+            remote(8 * a, part, rows_view(dst, k, n * count, count), {"tensor": t2}).start()
+        started.append(remote(8 * a, rows_view(src, k), rows_view(dst, k), {"tensor": t2}))
+
+    def send_core(which):
+        send(core_base + which, inputs[which], gathered[which].at[t], {"tensor": t1})
 
     def arrived(number, ref):
         remote(number, ref, ref, {"tensor": t1}).wait_recv()
 
-    def piece(a, part):
-        return gathered[a].at[t2, part]
+    def own_core(which):
+        arrived(core_base + which, gathered[which].at[t1])
 
     def after_x(a):
-        (first, _), (second, _) = hops[a]
-        arrived(9 * a, piece(a, q))
-        send(9 * a + 1, piece(a, q), piece(a, q), first)
-        send(9 * a + 2, piece(a, q), piece(a, q), second)
-        send(9 * a + 5, piece(a, q), piece(a, q), {"tensor": t1})
+        (first, _), (second, _) = hops[:: -1 if a % 2 else 1]
+        arrived(8 * a, piece(a, q))
+        send(8 * a + 1, piece(a, q), piece(a, q), first)
+        send(8 * a + 2, piece(a, q), piece(a, q), second)
+        send(8 * a + 4, piece(a, q), piece(a, q), {"tensor": t1})
 
     def after_first(a):
-        (_, part), (second, _) = hops[a]
-        arrived(9 * a + 1, piece(a, part))
-        send(9 * a + 3, piece(a, part), piece(a, part), second)
-        send(9 * a + 6, piece(a, part), piece(a, part), {"tensor": t1})
+        (_, part), (second, _) = hops[:: -1 if a % 2 else 1]
+        arrived(8 * a + 1, piece(a, part))
+        send(8 * a + 3, piece(a, part), piece(a, part), second)
+        send(8 * a + 5, piece(a, part), piece(a, part), {"tensor": t1})
 
     def after_second(a):
-        (_, _), (_, part) = hops[a]
-        arrived(9 * a + 2, piece(a, part))
-        send(9 * a + 7, piece(a, part), piece(a, part), {"tensor": t1})
-        arrived(9 * a + 3, piece(a, q3))
-        send(9 * a + 8, piece(a, q3), piece(a, q3), {"tensor": t1})
+        (_, _), (_, part) = hops[:: -1 if a % 2 else 1]
+        arrived(8 * a + 2, piece(a, part))
+        send(8 * a + 6, piece(a, part), piece(a, part), {"tensor": t1})
+        arrived(8 * a + 3, piece(a, q3))
+        send(8 * a + 7, piece(a, q3), piece(a, q3), {"tensor": t1})
 
     def after_core(a):
-        (_, one), (_, two) = hops[a]
+        (_, one), (_, two) = hops[:: -1 if a % 2 else 1]
         for k, part in enumerate((q, one, two, q3)):
-            arrived(9 * a + 5 + k, gathered[a].at[t3, part])
-
-    tok_base, vec_base, pick_base = 36, 39, 42
+            arrived(8 * a + 4 + k, piece(a, part, t3))
+
+    core_base, tok_base, vec_base, pick_base = 48, 52, 55, 58
     own = pl.multiple_of(t * n_seq, n_seq)
-    own_tok = local(1, tokens.at[pl.ds(own, n_seq)], tok.at[t])
-
     def send_tokens(k, peer):
-        theirs = pl.multiple_of(peer * n_seq, n_seq)
-        send(tok_base + k, tokens.at[pl.ds(theirs, n_seq)], tok.at[t], {"tensor": peer})
+        send(tok_base + k, packed.at[peer], tok.at[t], {"tensor": peer})
 
     send_x(0, 3)
+    own_tok.wait()
+    part_width = model // 4
+    for j in range(4):
+        packed[j] = jnp.concatenate([raw[j * n_seq + s] for s in range(n_seq)], 1)
+    tok[t] = packed[t]
     send_tokens(2, t1)
     send_tokens(0, t2)
     send_tokens(1, t3)
     own_o = local(3, w_out, wo.at[t])
-    part_width = model // 4
     gap = jnp.zeros((1, part_width), f32)
     vec[t, 1:2] = jnp.concatenate([b_qv[0:1], gap, b_qv[1:2], gap], 1)
     singles = (b_up, None, b_out, gain_one, bias_one, b_down, gain_two, bias_two)
@@ -222,10 +237,9 @@
     own_u = local(4, w_up, wu.at[t])
     own_d = local(5, w_down, wd.at[t])
     after_x(0)
-    send_x(2)
     send_x(1, 3)
-    after_first(0)
-    own_tok.wait()
+    after_x(1)
+    send_x(3, 2)
     for k, peer in enumerate((t2, t3, t1)):
         arrived(tok_base + k, tok.at[peer])
 
@@ -239,9 +253,9 @@
         copy.start()
         stores.append(copy)
 
-    @pl.loop(0, n_seq)
-    def _(s):
-        x_s[s] = jnp.concatenate([tok[j, s] for j in range(4)], axis=1)
+    for s in range(n_seq):
+        lanes = slice(s * part_width, (s + 1) * part_width)
+        x_s[s] = jnp.concatenate([tok[j, :, lanes] for j in range(4)], axis=1)
 
     store(x_s, x_out)
 
@@ -281,27 +295,30 @@
                     att_s[s, :, cols] += term
 
     own_q.wait()
+    after_first(0)
+    send_x(2, 2)
     attention(t, True)
-    send_x(3)
-    after_x(1)
+    send_x(4, 3)
+    after_first(1)
     own_o.wait()
     project(t, True)
-    after_x(2)
     for k, peer in enumerate((t2, t3, t1)):
         arrived(vec_base + k, vec.at[peer])
-    arrived(4, wq.at[t1])
-    arrived(9 + 4, wo.at[t1])
+    own_core(0)
+    own_core(1)
+    after_x(3)
     attention(t1, False)
-    after_first(1)
+    send_x(5, 3)
     project(t1, False)
+    after_x(2)
     after_second(0)
-    after_x(3)
     attention(t2, False)
     after_second(1)
     project(t2, False)
+    after_x(4)
     after_core(0)
     attention(t3, False)
-    after_first(2)
+    after_x(5)
     after_core(1)
     project(t3, False)
     store(qkv_s, qkv_out)
@@ -310,6 +327,7 @@
     store(wq, wq_all)
     store(wo, wo_all)
 
+    after_first(3)
     chunk = 96
     chunks = seq // chunk
 
@@ -326,7 +344,7 @@
     store(n1_s, n1_out)
     store(f1_s, f1_out)
     store(hl_s, hl_out)
-    after_first(3)
+    after_first(2)
     own_u.wait()
     own_d.wait()
 
@@ -366,20 +384,26 @@
 
     ffn_up(t)
     store_ffn(t)
+    after_first(4)
     ffn_down(t, True)
-    arrived(2 * 9 + 4, wu.at[t1])
+    after_first(5)
+    own_core(2)
     ffn_up(t1)
-    arrived(3 * 9 + 4, wd.at[t1])
+    own_core(3)
     store_ffn(t1)
     ffn_down(t1, False)
+    after_second(3)
     after_second(2)
     ffn_up(t2)
-    after_second(3)
+    after_second(4)
+    after_second(5)
     store_ffn(t2)
     ffn_down(t2, False)
+    after_core(3)
     after_core(2)
     ffn_up(t3)
-    after_core(3)
+    after_core(4)
+    after_core(5)
     store_ffn(t3)
     ffn_down(t3, False)
 
@@ -429,15 +453,16 @@
     weights = [(4,) + w.shape for w in weights_in]
     any_spec = pl.BlockSpec(memory_space=pl.ANY)
     vmem_spec = pl.BlockSpec(memory_space=pltpu.VMEM)
-    scratch = [pltpu.VMEM((4, n_seq, seq, model // 4), bf16)]
+    packed = (4, seq, n_seq * model // 4)
+    scratch = [pltpu.VMEM(tokens.shape, bf16), pltpu.VMEM(packed, bf16), pltpu.VMEM(packed, bf16)]
     scratch += [pltpu.VMEM(*a) for a in acts[:4]]
     scratch += [pltpu.VMEM((n_seq, seq, model), f32)]
     scratch += [pltpu.VMEM(*a) for a in acts[4:]]
     scratch += [pltpu.VMEM(w, bf16) for w in weights]
     scratch += [pltpu.VMEM((4, 8, model), f32)]
     scratch += [
-        pltpu.SemaphoreType.DMA((45,)),
-        pltpu.SemaphoreType.DMA((45,)),
+        pltpu.SemaphoreType.DMA((61,)),
+        pltpu.SemaphoreType.DMA((61,)),
         pltpu.SemaphoreType.DMA((6,)),
         pltpu.SemaphoreType.DMA((32,)),
     ]
@@ -680,7 +705,8 @@
         loads[name] = copy
 
     own = pl.multiple_of(t * n_seq, n_seq)
-    load("vocab", vocab, big)
+    for j in range(vocab.shape[0]):
+        load("vocab%d" % j, vocab.at[j], big.at[j])
     base = 0
     share_width = model // docs
     wide = states[...].astype(f32)
@@ -694,26 +720,7 @@
         send(base + k, own_states, st_all.at[d], {"doc": p})
     states_base = base
     base += docs - 1
-    load("og", out_grad.at[pl.ds(own, n_seq)], og)
-    load("n2", n2_in, n2)
-    load("f2", f2_in, f2)
     order = (t3, t2, t1, t)
-    load("act0", act_in.at[order[0]], act.at[0])
-    load("act1", act_in.at[order[1]], act.at[1])
-    for i in range(2):
-        load("wd%d" % i, wd_in.at[order[i]], wd.at[i])
-        load("wu%d" % i, wu_in.at[order[i]], wu.at[i])
-    load("gp0", gp_in.at[order[0]], gp.at[0])
-    load("gp1", gp_in.at[order[1]], gp.at[1])
-    load("hl", hl_in, tmp)
-    load("n1", n1_in, n1)
-    load("f1", f1_in, f1)
-    load("wo", wo_in, wo)
-    for i in range(2):
-        load("wq%d" % i, wq_in.at[order[i]], wq.at[i])
-        load("qkv%d" % i, qkv_in.at[order[i]], qkv.at[i])
-    load("ctx", ctx_in, ctx)
-    load("lse", lse_in, lse)
     first_row = d * (4 * n_seq)
     hot = picks(positions, first_row + t * n_seq, n_seq, queries)
     out_base = base
@@ -727,12 +734,14 @@
         query = lax.rem(first_row + b // 8, queries)
         goal = jnp.where(tall == b, targets[query, b % 8], goal)
     goal = goal - t * vocab_local
-    loads["vocab"].wait()
-
-    @pl.loop(0, vocab_local // chunk)
-    def _(j):
-        start = pl.multiple_of(j * chunk, chunk)
-        lg[:, pl.ds(start, chunk)] = dot_nt(rows_of(pk[...]), square(big[j]))
+    picked = rows_of(pk[...])
+    for j in range(vocab_local // chunk):
+        loads["vocab%d" % j].wait()
+        lg[:, j * chunk : (j + 1) * chunk] = dot_nt(picked, square(big[j]))
+    load("og", out_grad.at[pl.ds(own, n_seq)], og)
+    load("n2", n2_in, n2)
+    load("f2", f2_in, f2)
+    load("hl", hl_in, tmp)
 
     high = jnp.max(lg[...], 1, keepdims=True)
     ut[...] = jnp.zeros_like(ut)
@@ -768,6 +777,8 @@
     for k, p in enumerate((t2, t3, t1)):
         send(part_base + 3 + k, us.at[p], ur.at[t], {"tensor": p})
     ur[t] = us[t]
+    for i in range(2):
+        load("act%d" % i, act_in.at[order[i]], act.at[i])
     sums[0] = jnp.zeros(sums.shape[1:], f32)
     for name in ("og", "n2", "f2"):
         loads[name].wait()
@@ -818,6 +829,10 @@
     loads["hl"].wait()
     x_t[...] = tmp[...].T
     load("x", x_in, tmp)
+    for i in range(2):
+        load("wd%d" % i, wd_in.at[order[i]], wd.at[i])
+        load("gp%d" % i, gp_in.at[order[i]], gp.at[i])
+        load("wu%d" % i, wu_in.at[order[i]], wu.at[i])
     for k, p in enumerate((t2, t3, t1)):
         arrived(part_base + 3 + k, ur.at[p])
     gap = jnp.zeros((own_rows, model), f32)
@@ -925,6 +940,14 @@
         if i == 1:
             down.other.start()
     down.mine.start()
+    load("n1", n1_in, n1)
+    load("f1", f1_in, f1)
+    load("wo", wo_in, wo)
+    load("ctx", ctx_in, ctx)
+    load("lse", lse_in, lse)
+    for i in range(2):
+        load("qkv%d" % i, qkv_in.at[order[i]], qkv.at[i])
+        load("wq%d" % i, wq_in.at[order[i]], wq.at[i])
     for i, shard in enumerate(order):
         for name in ("gp", "wd", "wu"):
             loads["%s%d" % (name, i)].wait()
@@ -1222,7 +1245,7 @@
     scratch += [
         pltpu.SemaphoreType.DMA((copies,)),
         pltpu.SemaphoreType.DMA((copies,)),
-        pltpu.SemaphoreType.DMA((40,)),
+        pltpu.SemaphoreType.DMA((48,)),
     ]
     return pl.pallas_call(
         functools.partial(backward_kernel, (n_seq, seq, model, queries, slots, table, docs)),

time: 192 us -> 183 us (0.953)
  Pallas kernels: 191 us -> 182 us
    pallas_call x1, Pallas kernels: 74 us -> 65.6 us  [forward(): pl.pallas_call(functools.partial(forward_kernel, (n_seq, seq, model, quer...]
where the time goes in v4:
time: 183 us
  Pallas kernels  182 us (99%)
    pallas_call x1, Pallas kernels, backward(): pl.pallas_call(functools.partial(backward_kernel, (n_seq, seq, model, que...  111 us
    pallas_call x1, Pallas kernels, forward(): pl.pallas_call(functools.partial(forward_kernel, (n_seq, seq, model, quer...  65.6 us
    pallas_call x1, Pallas kernels, finish(): pl.pallas_call(functools.partial(finish_kernel, (n_seq, docs)), out_shape...  5.23 us

profile of v4, /device:TPU:0, one launch (start us, length us, event | category | flops | bytes accessed | tf_op | source)
XLA Modules:
  0.0 182.9 jit_solution(10570208737544028204)
XLA Ops:
  0.7 65.6 %layer_forward.1 = (bf16[2,288,768]{2,1,0:T(8,128)(2,1)}, bf16[4,2,288,576]{3,2,1,0:T(8,128)(2,1)}, f32[4,2,3,1,288]{4,3,2,1,0:T(1,128)}, bf16[4,2,288,192]{3,2,...) custom-call(s32[8,8]{1,0:T(8,128)} %lengths.3, ...), custom_call_target="tpu_custom_call" | custom-call | tf_op jit(solution)/shard_map/layer_forward/pallas_call | solution.py:469
  66.3 111.2 %layer_backward.1 = (bf16[8,288,768]{2,1,0:T(8,128)(2,1)}, f32[8,128]{1,0:T(8,128)}, bf16[4,288,384]{2,1,0:T(8,128)(2,1)}, f32[8,96]{1,0:T(8,128)}, f32[96,128]{...) custom-call(s32[8,8]{1,0:T(8,128)} %lengths.3, ...), custom_call_target="tpu_custom_call" | custom-call | tf_op jit(solution)/shard_map/layer_backward/pallas_call | solution.py:1250
  177.5 5.2 %layer_results.1 = (bf16[8,288,768]{2,1,0:T(8,128)(2,1)}, f32[8]{0:T(128)}, f32[8,288,192]{2,1,0:T(8,128)}, f32[8,96]{1,0:T(8,128)}, f32[3,96,192]{2,1,0:T(8,128...) custom-call(bf16[8,288,768]{2,1,0:T(8,128)(2,1)} %get-tuple-element., ...), custom_call_target="tpu_custom_call" | custom-call | tf_op jit(solution)/shard_map/layer_results/pallas_call | solution.py:1353

commit v5 on v4

--- a/solution.py
+++ b/solution.py
@@ -670,6 +670,15 @@
         "z1": (lax.div(d, 4), {"doc": flip(d, 4)}),
     }
 
+    loads = {}
+
+    def load(name, src, dst):
+        copy = pltpu.make_async_copy(src, dst, local_sem.at[len(loads)])
+        copy.start()
+        loads[name] = copy
+
+    for j in range(vocab.shape[0]):
+        load("vocab%d" % j, vocab.at[j], big.at[j])
     barrier = pltpu.get_barrier_semaphore()
     doc_peers = [lax.rem(d + k, docs) for k in range(1, docs)]
     peers = [{"tensor": p} for p in (t1, t2, t3)] + [{"doc": p} for p in doc_peers]
@@ -697,16 +706,7 @@
     def arrived(number, ref):
         remote(number, ref, ref, {"tensor": t1}).wait_recv()
 
-    loads = {}
-
-    def load(name, src, dst):
-        copy = pltpu.make_async_copy(src, dst, local_sem.at[len(loads)])
-        copy.start()
-        loads[name] = copy
-
     own = pl.multiple_of(t * n_seq, n_seq)
-    for j in range(vocab.shape[0]):
-        load("vocab%d" % j, vocab.at[j], big.at[j])
     base = 0
     share_width = model // docs
     wide = states[...].astype(f32)
@@ -721,6 +721,7 @@
     states_base = base
     base += docs - 1
     order = (t3, t2, t1, t)
+    down_order = (t3, t1, t2, t)
     first_row = d * (4 * n_seq)
     hot = picks(positions, first_row + t * n_seq, n_seq, queries)
     out_base = base
@@ -778,7 +779,7 @@
         send(part_base + 3 + k, us.at[p], ur.at[t], {"tensor": p})
     ur[t] = us[t]
     for i in range(2):
-        load("act%d" % i, act_in.at[order[i]], act.at[i])
+        load("act%d" % i, act_in.at[down_order[i]], act.at[i])
     sums[0] = jnp.zeros(sums.shape[1:], f32)
     for name in ("og", "n2", "f2"):
         loads[name].wait()
@@ -904,42 +905,41 @@
     down, up, attn = reds
     block_shape = (2, 2, 2, model // docs)
 
-    def emit(red, i, sending, shard, lanes, value):
+    def emit(red, shard, sending, lanes, value):
         value = value.reshape(block_shape + (value.shape[-1],))
         which = lax.div(shard, 2)
-        if i % 2 == 0:
+        if sending is not None:
             sending[which, :, :, :, :, lanes] = value.astype(bf16)
         else:
             total = value + red.held[which, :, :, :, :, lanes].astype(f32)
             red.held[which, :, :, :, :, lanes] = total.astype(bf16)
 
-    def before_block(red, i, shard):
-        if i % 2 == 1:
-            which = lax.div(shard, 2)
-            arrived(red.base + i // 2, red.held.at[which])
-
-    def after_block(red, i, sending, shard):
-        if i % 2 == 0:
-            which = lax.div(shard, 2)
-            send(red.base + i // 2, sending.at[which], red.held.at[which], {"tensor": t1})
+    def before_block(red, number, shard):
+        arrived(red.base + number, red.held.at[lax.div(shard, 2)])
+
+    def after_block(red, number, sending, shard):
+        which = lax.div(shard, 2)
+        send(red.base + number, sending.at[which], red.held.at[which], {"tensor": t1})
 
     down_send, up_send = big.at[0:2], big.at[2:4]
     tiles = model // 256
-    for i, shard in enumerate(order):
+    for i, shard in enumerate(down_order):
         loads["act%d" % i].wait()
-        before_block(down, i, shard)
+        if i >= 2:
+            before_block(down, i - 2, shard)
 
         @pl.loop(0, tiles)
         def _(n):
             lanes = pl.ds(pl.multiple_of(n * 256, 256), 256)
-            emit(down, i, down_send, shard, lanes, dot(d_t[...], act[i % 2, :, lanes]))
+            value = dot(d_t[...], act[i % 2, :, lanes])
+            emit(down, shard, down_send if i < 2 else None, lanes, value)
 
         if i + 2 < 4:
-            load("act%d" % (i + 2), act_in.at[order[i + 2]], act.at[i % 2])
-        after_block(down, i, down_send, shard)
-        if i == 1:
+            load("act%d" % (i + 2), act_in.at[down_order[i + 2]], act.at[i % 2])
+        if i < 2:
+            after_block(down, i, down_send, shard)
+        if i == 2:
             down.other.start()
-    down.mine.start()
     load("n1", n1_in, n1)
     load("f1", f1_in, f1)
     load("wo", wo_in, wo)
@@ -951,7 +951,6 @@
     for i, shard in enumerate(order):
         for name in ("gp", "wd", "wu"):
             loads["%s%d" % (name, i)].wait()
-        before_block(up, i, shard)
 
         @pl.loop(0, tiles)
         def _(n):
@@ -959,11 +958,13 @@
             value = dot_nt(rows_of(og[...]), wd[i % 2, lanes]) * gp[i % 2, :, lanes].astype(f32)
             low = value.astype(bf16)
             d_up[:, lanes] = low
-            sums[0, shard, :, lanes] = jnp.sum(low.astype(f32), 0, keepdims=True)
+            sums[0, 4 + shard, :, lanes] = jnp.sum(low.astype(f32), 0, keepdims=True)
 
         if i + 2 < 4:
             load("gp%d" % (i + 2), gp_in.at[order[i + 2]], gp.at[i % 2])
             load("wd%d" % (i + 2), wd_in.at[order[i + 2]], wd.at[i % 2])
+        if i % 2:
+            before_block(up, i // 2, shard)
 
         @pl.loop(0, tiles)
         def _(n):
@@ -973,18 +974,17 @@
                 n2[:, lanes] = value
             else:
                 n2[:, lanes] += value
-            emit(up, i, up_send, shard, lanes, dot(x_t[...], d_up[:, lanes]))
+            value = dot(x_t[...], d_up[:, lanes])
+            emit(up, shard, None if i % 2 else up_send, lanes, value)
 
         if i + 2 < 4:
             load("wu%d" % (i + 2), wu_in.at[order[i + 2]], wu.at[i % 2])
-        after_block(up, i, up_send, shard)
-        if i == 1:
-            down.other.middle()
+        if i % 2 == 0:
+            after_block(up, i // 2, up_send, shard)
+        if i == 0:
+            down.mine.start()
+        if i == 2:
             up.other.start()
-        if i == 2:
-            down.mine.middle()
-    up.mine.start()
-    down.pass_other()
     arrived(out_base, output.at[pl.ds(t2 * n_seq, n_seq)])
     passed = output.at[pl.ds(t2 * n_seq, n_seq)]
     send(out_base + 2, passed, passed, {"tensor": t1})
@@ -1005,21 +1005,40 @@
         og[s, pl.ds(pl.multiple_of(start, step_rows), step_rows)] = back.astype(bf16)
 
     d_t[...] = rows_of(og[...]).T
-    up.other.middle()
+    up.mine.start()
     loads["x"].wait()
     x_t[...] = tmp[...].T
     for name in ("wo", "ctx", "lse"):
         loads[name].wait()
     vec_base = base
     vec_peers = [{"tensor": t1}, bits["y"][1], bits["z0"][1], bits["x"][1], bits["z1"][1]]
-    base += len(vec_peers)
-
-    def vec_start(k):
-        send(vec_base + k, sums.at[k], sums_in.at[k], vec_peers[k])
-
-    def vec_finish(k):
-        arrived(vec_base + k, sums_in.at[k])
-        sums[k + 1] = sums[k] + sums_in[k]
+    base += 2 * len(vec_peers)
+    early, late = pl.ds(4, 10), pl.ds(0, 4)
+
+    def vec_start(k, rows):
+        number = vec_base + k + (5 if rows is late else 0)
+        send(number, sums.at[k, rows], sums_in.at[k, rows], vec_peers[k])
+
+    def vec_finish(k, rows):
+        number = vec_base + k + (5 if rows is late else 0)
+        arrived(number, sums_in.at[k, rows])
+        sums[k + 1, rows] = sums[k, rows] + sums_in[k, rows]
+
+    def vec_next(k, rows):
+        vec_finish(k, rows)
+        vec_start(k + 1, rows)
+
+    vec_start(0, early)
+
+    def add_dx(i, first):
+        @pl.loop(0, tiles)
+        def _(n):
+            lanes = pl.ds(pl.multiple_of(n * 256, 256), 256)
+            value = dot(dqkv[i % 2], wq[i % 2, :, lanes])
+            if first:
+                n1[:, lanes] = value
+            else:
+                n1[:, lanes] += value
 
     key_index = lax.broadcasted_iota(jnp.int32, (seq, seq), 0)
     for i, shard in enumerate(order):
@@ -1050,47 +1069,47 @@
                 d_q.append(dot_tn(kh, d_score) * 0.125)
             first = jnp.concatenate(d_q, 0).T
             both = jnp.concatenate([first] + d_k + d_v, 1).astype(bf16)
-            dqkv[rows] = both
+            dqkv[i % 2, rows] = both
             lse_sum = jnp.sum(both.astype(f32), 0, keepdims=True)
             parts[s] = lse_sum
 
         total = parts[0]
         for s in range(1, n_seq):
             total = total + parts[s]
-        sums[0, 4 + shard, :, : 3 * 192] = total
-        before_block(attn, i, shard)
-        value = jnp.concatenate([dot(x_t[...], dqkv[...]), dot(d_t[...], ctx[shard])], 1)
-        emit(attn, i, attn_send, shard, slice(None), value)
-        after_block(attn, i, attn_send, shard)
+        sums[0, shard, :, : 3 * 192] = total
+        if i % 2:
+            before_block(attn, i // 2, shard)
+        value = jnp.concatenate([dot(x_t[...], dqkv[i % 2]), dot(d_t[...], ctx[shard])], 1)
+        emit(attn, shard, None if i % 2 else attn_send, slice(None), value)
+        if i % 2 == 0:
+            after_block(attn, i // 2, attn_send, shard)
         if i == 0:
-            down.pass_mine()
-            up.mine.middle()
+            down.other.middle()
+            down.mine.middle()
+            up.other.middle()
+            down.pass_other()
         if i == 1:
             attn.other.start()
+            up.mine.middle()
             up.pass_other()
         if i == 2:
-            down_out[...] = down.result()
-            up.pass_mine()
+            down.pass_mine()
             attn.other.middle()
         if i == 3:
             attn.mine.start()
-            vec_start(0)
-            up_out[...] = up.result()
-            attn.pass_other()
-
-        @pl.loop(0, tiles)
-        def _(n):
-            lanes = pl.ds(pl.multiple_of(n * 256, 256), 256)
-            value = dot(dqkv[...], wq[i % 2, :, lanes])
-            if i == 0:
-                n1[:, lanes] = value
-            else:
-                n1[:, lanes] += value
-
-        if i + 2 < 4:
-            load("qkv%d" % (i + 2), qkv_in.at[order[i + 2]], qkv.at[i % 2])
-            load("wq%d" % (i + 2), wq_in.at[order[i + 2]], wq.at[i % 2])
-
+            vec_start(0, late)
+            up.pass_mine()
+        if i < 4:
+            vec_next(i, early)
+        if i < 2:
+            add_dx(i, i == 0)
+            load("qkv%d" % (i + 2), qkv_in.at[order[i + 2]], qkv.at[i])
+            load("wq%d" % (i + 2), wq_in.at[order[i + 2]], wq.at[i])
+
+    add_dx(2, False)
+    add_dx(3, False)
+    vec_next(0, late)
+    attn.pass_other()
     for j in range(4):
         lanes = slice(j * 192, j * 192 + 192)
         block = (n1[:, lanes] + dy[:, lanes]).astype(bf16)
@@ -1100,21 +1119,19 @@
     for k, p in enumerate((t2, t3, t1)):
         send(tok_base + k, dxb.at[p], gt.at[t], {"tensor": p})
     gt[t] = dxb[t]
-    vec_finish(0)
-    vec_start(1)
+    vec_next(1, late)
+    down_out[...] = down.result()
     attn.mine.middle()
-    vec_finish(1)
-    vec_start(2)
-    vec_finish(2)
-    vec_start(3)
+    vec_next(2, late)
+    vec_finish(4, early)
     attn.pass_mine()
-    vec_finish(3)
-    vec_start(4)
+    vec_next(3, late)
+    up_out[...] = up.result()
+    vec_finish(4, late)
+    vec_out[...] = sums[5]
     for k, p in enumerate((t2, t3, t1)):
         arrived(tok_base + k, gt.at[p])
     load("gt", gt, gt_out)
-    vec_finish(4)
-    vec_out[...] = sums[5]
     total = attn.result()
     for k in range(3):
         qkv_out[k] = total[:, k * 192 : k * 192 + 192]
@@ -1224,7 +1241,7 @@
         vm((model, m_rows), bf16),
         vm((m_rows, model), bf16),
         vm((m_rows, 192), bf16),
-        vm((m_rows, 576), bf16),
+        vm((2, m_rows, 576), bf16),
         vm((4, seq, n_seq * 192), bf16),
         vm((4, seq, n_seq * 192), bf16),
         vm((6, 14, 1, model), f32),
@@ -1241,7 +1258,7 @@
             scratch.append(vm((2, share, model), bf16))
         scratch.append(vm((2, share, model), bf16))
         scratch.append(vm((share, model), bf16))
-    copies = 2 * (docs - 1) + 3 + 6 + 12 * 3 + 3 + 5
+    copies = 2 * (docs - 1) + 3 + 6 + 12 * 3 + 3 + 10
     scratch += [
         pltpu.SemaphoreType.DMA((copies,)),
         pltpu.SemaphoreType.DMA((copies,)),
@@ -1301,10 +1318,10 @@
     copies[1].wait()
     copies[2].wait()
     nll_out[...] = nll[:, 0]
-    heads = sums[4 + t]
+    heads = sums[t]
     b_qv_out[0:1] = heads[:, :part_width]
     b_qv_out[1:2] = heads[:, 2 * part_width : 3 * part_width]
-    b_up_out[...] = sums[t].reshape(b_up_out.shape)
+    b_up_out[...] = sums[4 + t].reshape(b_up_out.shape)
     width = b_out_out.shape[0]
     singles = (b_out_out, gain_one_out, bias_one_out, b_down_out, gain_two_out, bias_two_out)
     for k, ref in enumerate(singles):

time: 183 us -> 181 us (0.989)
  Pallas kernels: 182 us -> 180 us
    pallas_call x1, Pallas kernels: 111 us -> 109 us  [backward(): pl.pallas_call(functools.partial(backward_kernel, (n_seq, seq, model, que...]
where the time goes in v5:
time: 181 us; the launch traced here: 180 us
  Pallas kernels  180 us (99%)
    pallas_call x1, Pallas kernels, backward(): pl.pallas_call(functools.partial(backward_kernel, (n_seq, seq, model, que...  109 us
    pallas_call x1, Pallas kernels, forward(): pl.pallas_call(functools.partial(forward_kernel, (n_seq, seq, model, quer...  65.6 us
    pallas_call x1, Pallas kernels, finish(): pl.pallas_call(functools.partial(finish_kernel, (n_seq, docs)), out_shape...  5.23 us

profile of v5, /device:TPU:0, one launch (start us, length us, event | category | flops | bytes accessed | tf_op | source)
XLA Modules:
  0.0 180.4 jit_solution(3264622213568684012)
XLA Ops:
  0.7 65.6 %layer_forward.1 = (bf16[2,288,768]{2,1,0:T(8,128)(2,1)}, bf16[4,2,288,576]{3,2,1,0:T(8,128)(2,1)}, f32[4,2,3,1,288]{4,3,2,1,0:T(1,128)}, bf16[4,2,288,192]{3,2,...) custom-call(s32[8,8]{1,0:T(8,128)} %lengths.3, ...), custom_call_target="tpu_custom_call" | custom-call | tf_op jit(solution)/shard_map/layer_forward/pallas_call | solution.py:469
  66.3 108.7 %layer_backward.1 = (bf16[8,288,768]{2,1,0:T(8,128)(2,1)}, f32[8,128]{1,0:T(8,128)}, bf16[4,288,384]{2,1,0:T(8,128)(2,1)}, f32[8,96]{1,0:T(8,128)}, f32[96,128]{...) custom-call(s32[8,8]{1,0:T(8,128)} %lengths.3, ...), custom_call_target="tpu_custom_call" | custom-call | tf_op jit(solution)/shard_map/layer_backward/pallas_call | solution.py:1267
  175.0 5.2 %layer_results.1 = (bf16[8,288,768]{2,1,0:T(8,128)(2,1)}, f32[8]{0:T(128)}, f32[8,288,192]{2,1,0:T(8,128)}, f32[8,96]{1,0:T(8,128)}, f32[3,96,192]{2,1,0:T(8,128...) custom-call(bf16[8,288,768]{2,1,0:T(8,128)(2,1)} %get-tuple-element., ...), custom_call_target="tpu_custom_call" | custom-call | tf_op jit(solution)/shard_map/layer_results/pallas_call | solution.py:1370

commit v6 on v5

--- a/solution.py
+++ b/solution.py
@@ -1098,7 +1098,6 @@
         if i == 3:
             attn.mine.start()
             vec_start(0, late)
-            up.pass_mine()
         if i < 4:
             vec_next(i, early)
         if i < 2:
@@ -1107,6 +1106,7 @@
             load("wq%d" % (i + 2), wq_in.at[order[i + 2]], wq.at[i])
 
     add_dx(2, False)
+    up.pass_mine()
     add_dx(3, False)
     vec_next(0, late)
     attn.pass_other()
@@ -1283,7 +1283,7 @@
     output_out, nll_out, tokens_out, gs_out, qkv_out, b_qv_out, out_out = refs[11:18]
     b_out_out, gain_one_out, bias_one_out, up_out, b_up_out, down_out = refs[18:24]
     b_down_out, gain_two_out, bias_two_out, gwq_out, gt, nll, sums, whole = refs[24:32]
-    held, sem, sem_out = refs[32:-2], refs[-2], refs[-1]
+    wide, held, sem, sem_out = refs[32], refs[33:-2], refs[-2], refs[-1]
     d = lax.axis_index("doc")
     t = lax.axis_index("tensor")
     pairs = [(gt_in, gt), (sums_in, sums), (nll_in, nll), (res, whole.at[pl.ds(t * n_seq, n_seq)])]
@@ -1304,17 +1304,21 @@
         copy.start()
         ends.append(copy)
 
+    part_width = gt.shape[-1] // n_seq
+    copies[0].wait()
+    for j in range(4):
+        for s in range(n_seq):
+            lanes = slice(s * part_width, (s + 1) * part_width)
+            wide[j * n_seq + s] = gt[j, :, lanes].astype(f32)
+        part = pl.ds(j * n_seq, n_seq)
+        copy = pltpu.make_async_copy(wide.at[part], tokens_out.at[part], sem_out.at[len(ends)])
+        copy.start()
+        ends.append(copy)
     for k in range(4):
         part = pl.ds(lax.rem(t + k, 4) * n_seq, n_seq)
         forward_to(3 + k, whole.at[part], output_out.at[part])
     for k, (pair, buf) in enumerate(zip(passed, held)):
         forward_to(7 + k, buf, pair[1])
-    part_width = gt.shape[-1] // n_seq
-    copies[0].wait()
-    for j in range(4):
-        for s in range(n_seq):
-            lanes = slice(s * part_width, (s + 1) * part_width)
-            tokens_out[j * n_seq + s] = gt[j, :, lanes].astype(f32)
     copies[1].wait()
     copies[2].wait()
     nll_out[...] = nll[:, 0]
@@ -1365,7 +1369,7 @@
     any_spec = pl.BlockSpec(memory_space=pltpu.HBM)
     vmem_spec = pl.BlockSpec(memory_space=pltpu.VMEM)
     out_specs = [vmem_spec] * 17
-    for k in (0, 3, 4, 6, 10, 12, 16):
+    for k in (0, 2, 3, 4, 6, 10, 12, 16):
         out_specs[k] = any_spec
     results = pl.pallas_call(
         functools.partial(finish_kernel, (n_seq, docs)),
@@ -1377,9 +1381,10 @@
             pltpu.VMEM(nll.shape, nll.dtype),
             pltpu.VMEM(sums.shape, sums.dtype),
             pltpu.VMEM(output.shape, output.dtype),
+            pltpu.VMEM((4 * n_seq, gt.shape[1], part_width), f32),
             *(pltpu.VMEM(a.shape, a.dtype) for a in (down, up, qkv, out, gs, gwq)),
             pltpu.SemaphoreType.DMA((13,)),
-            pltpu.SemaphoreType.DMA((10,)),
+            pltpu.SemaphoreType.DMA((14,)),
         ],
         compiler_params=pltpu.CompilerParams(vmem_limit_bytes=62 * MIB),
         name="layer_results",

time: 181 us -> 180 us (level)
  no operation moved by 1% of the time
where the time goes in v6:
time: 180 us
  Pallas kernels  179 us (99%)
    pallas_call x1, Pallas kernels, backward(): pl.pallas_call(functools.partial(backward_kernel, (n_seq, seq, model, que...  109 us
    pallas_call x1, Pallas kernels, forward(): pl.pallas_call(functools.partial(forward_kernel, (n_seq, seq, model, quer...  65.6 us
    pallas_call x1, Pallas kernels, finish(): pl.pallas_call(functools.partial(finish_kernel, (n_seq, docs)), out_shape...  4.96 us

profile of v6, /device:TPU:0, one launch (start us, length us, event | category | flops | bytes accessed | tf_op | source)
XLA Modules:
  0.0 180.1 jit_solution(8508818903221250694)
XLA Ops:
  0.7 65.6 %layer_forward.1 = (bf16[2,288,768]{2,1,0:T(8,128)(2,1)}, bf16[4,2,288,576]{3,2,1,0:T(8,128)(2,1)}, f32[4,2,3,1,288]{4,3,2,1,0:T(1,128)}, bf16[4,2,288,192]{3,2,...) custom-call(s32[8,8]{1,0:T(8,128)} %lengths.3, ...), custom_call_target="tpu_custom_call" | custom-call | tf_op jit(solution)/shard_map/layer_forward/pallas_call | solution.py:469
  66.3 108.7 %layer_backward.1 = (bf16[8,288,768]{2,1,0:T(8,128)(2,1)}, f32[8,128]{1,0:T(8,128)}, bf16[4,288,384]{2,1,0:T(8,128)(2,1)}, f32[8,96]{1,0:T(8,128)}, f32[96,128]{...) custom-call(s32[8,8]{1,0:T(8,128)} %lengths.3, ...), custom_call_target="tpu_custom_call" | custom-call | tf_op jit(solution)/shard_map/layer_backward/pallas_call | solution.py:1267
  175.0 5.0 %layer_results.1 = (bf16[8,288,768]{2,1,0:T(8,128)(2,1)}, f32[8]{0:T(128)}, f32[8,288,192]{2,1,0:T(8,128)}, f32[8,96]{1,0:T(8,128)}, f32[3,96,192]{2,1,0:T(8,128...) custom-call(bf16[8,288,768]{2,1,0:T(8,128)(2,1)} %get-tuple-element., ...), custom_call_target="tpu_custom_call" | custom-call | tf_op jit(solution)/shard_map/layer_results/pallas_call | solution.py:1374
